TPU v7x, 32 devices: a whole 2x2x4 slice. The times are simulated.
32 devices in a mesh: grp: 2 (over y), orb: 4 (over z), cmp: 4 (over x, core).
Axes of the slice: x: 2, y: 2, z: 4, core: 2. Of those that a mesh axis runs over, the one named last changes fastest.
Arguments:
- psi: float32 [64, 64, 1024], P(('grp', 'orb'), 'cmp'), parts along dimension 0, may hold values from -6 to 6
- potential: float32 [128, 1024], P(('grp', 'cmp')), parts along dimension 0, may hold values from -2 to 2
- extent: int32 [64], P('grp'), parts along dimension 0, may hold values from 256 to 1024, as said below
Outputs:
- psi_new: float32 [64, 64, 1024], P(('grp', 'orb'), 'cmp'), parts along dimension 0
- density: float32 [128, 1024], P(('grp', 'cmp'), 'orb'), parts along dimension 0
There are 2 independent parts, one for each index of `grp`. A program takes and returns all parts, laid end to end along the dimension named above; each array names one. Nothing has to cross between parts.
Inputs may be any that keep to these rules, and one draw needn't show every extreme that they name: `extent`: some orbital's region covers the whole plane in every draw.
All inputs are finite; a program needn't handle non-finite values.
Results may differ from a plain program's by a relative error of at most 0.00007.
Values sent between devices are 32-bit elements; how exact they have to be, the bound alone decides.
No kernel may reach another device: no remote copies, remote signals or barrier semaphores. Data moves between devices by JAX's collectives and lax.ppermute only.
A program may use at most 64 MiB of HBM per device.

v0:
```python
import math

import jax
import jax.numpy as jnp
from jax import lax
from jax.sharding import PartitionSpec as P

step_length = 0.2
reach = 14


def padded_2(cells, sides, width):
    for axis, dim in sides:
        count = lax.axis_size(axis)
        head = lax.slice_in_dim(cells, 0, width, axis=dim)
        tail = lax.slice_in_dim(cells, cells.shape[dim] - width, cells.shape[dim], axis=dim)
        cells = jnp.concatenate(
            [
                lax.ppermute(tail, axis, [(i, (i + 1) % count) for i in range(count)]),
                cells,
                lax.ppermute(head, axis, [((i + 1) % count, i) for i in range(count)]),
            ],
            axis=dim,
        )
    return cells


def band_matrix(length):
    rows = lax.broadcasted_iota(jnp.int32, (length + 2 * reach, length), 0)
    cols = lax.broadcasted_iota(jnp.int32, (length + 2 * reach, length), 1)
    spread = jnp.abs(rows - reach - cols)
    safe = jnp.maximum(spread, 1).astype(jnp.float32)
    signed = jnp.where(spread % 2 == 1, 2.0, -2.0) / (safe * safe)
    value = jnp.where(spread == 0, -math.pi**2 / 3.0, signed)
    return jnp.where(spread <= reach, value, 0.0)


def across_planes(padded, planes):
    return jnp.einsum("awp,wy->ayp", padded, band_matrix(planes), precision=lax.Precision.HIGHEST)


def along_grid(field):
    orbs, planes, grid_p = field.shape
    width = 128
    blocks = field.reshape(orbs, planes, grid_p // width, width)
    before = jnp.roll(blocks[..., width - reach :], 1, axis=2)
    after = jnp.roll(blocks[..., :reach], -1, axis=2)
    window = jnp.concatenate([before, blocks, after], axis=3)
    result = jnp.einsum(
        "axnw,wq->axnq", window, band_matrix(width), precision=lax.Precision.HIGHEST
    )
    return result.reshape(orbs, planes, grid_p)


def per_device(psi, potential, extent):
    orb_dev, planes, grid_p = psi.shape
    n_orb = lax.axis_size("orb")
    norbitals = orb_dev * n_orb
    cells = planes * lax.axis_size("cmp") * grid_p
    column = lax.broadcasted_iota(jnp.int32, (norbitals, grid_p), 1)
    live_all = (column < extent[:, None]).astype(jnp.float32)
    own_live = lax.dynamic_slice_in_dim(live_all, lax.axis_index("orb") * orb_dev, orb_dev, 0)
    phi = psi * own_live[:, None, :]
    padded = padded_2(phi, (("cmp", 1),), reach)
    kinetic = -0.5 * (across_planes(padded, planes) + along_grid(phi))
    hphi = own_live[:, None, :] * (kinetic + potential[None] * phi)
    phi_c, hphi_c = (
        lax.all_to_all(phi, "orb", split_axis=2, concat_axis=0, tiled=True),
        lax.all_to_all(hphi, "orb", split_axis=2, concat_axis=0, tiled=True),
    )
    flat_phi = phi_c.reshape(norbitals, -1)
    flat_h = hphi_c.reshape(norbitals, -1)
    partial_correlation = lax.dot_general(
        flat_phi,
        flat_h,
        (((1,), (1,)), ((), ())),
        precision=lax.Precision.HIGHEST,
        preferred_element_type=jnp.float32,
    )
    correlation = lax.psum(partial_correlation, ("orb", "cmp")) / cells
    grad_c = (flat_h - jnp.dot(correlation.T, flat_phi, precision=lax.Precision.HIGHEST)).reshape(
        phi_c.shape
    )
    grad = lax.all_to_all(grad_c, "orb", split_axis=0, concat_axis=2, tiled=True)
    psi_new = phi - step_length * grad
    density = (
        lax.psum_scatter(jnp.sum(psi_new * psi_new, axis=0), "orb", scatter_dimension=1, tiled=True)
        / norbitals
    )
    return (psi_new, density)


def solution(mesh):
    return jax.shard_map(
        per_device,
        mesh=mesh,
        in_specs=(P(("grp", "orb"), "cmp", None), P(("grp", "cmp"), None), P("grp")),
        out_specs=(P(("grp", "orb"), "cmp", None), P(("grp", "cmp"), "orb")),
        check_vma=False,
    )
```

profile of v0, /device:TPU:0, one launch (start us, length us, event | category | flops | bytes accessed | tf_op | source)
XLA Modules:
  0.0 166.2 jit_solution(2926780683935509482)
XLA Ops:
  7.2 0.7 dynamic-slice
  7.9 0.1 fusion.58
  8.0 1.1 broadcast_multiply_fusion.1
  9.1 0.9 fusion.107
  9.9 0.5 collective-permute-start
  10.4 1.9 %collective-permute-start.1 = (f32[8,14,1024]{2,1,0:T(8,128)S(1)}, f32[8,14,1024]{2,1,0:T(8,128)}, u32[]{:S(2)}, u32[]{:S(2)}) collective-permute-start(f32[8,14,1024]{2,1,0:T(8,128)S(1)} %get-tuple-element.5), channel_id=1, source_target_pairs={{1,0},{2,1},{3,2},{0,3},{5,4},{6,5},{7,6},{4,7},{9,8},{10,9},{11,1... | collective-permute-start | bytes 1376264 | tf_op jit(solution)/shard_map/ppermute | solution.py:21
  12.3 2.6 %copy.11 = f32[8,16,1024]{1,0,2:T(8,128)} copy(f32[8,16,1024]{2,1,0:T(8,128)S(1)} %broadcast_multiply_fusion.1) | data formatting | bytes 1048576 | tf_op jit(solution)/shard_map/mul | solution.py:63
  14.9 4.6 %reshape.37 = f32[4,1,32768]{2,1,0:T(1,128)} reshape(f32[1024,8,16]{2,1,0:T(8,128)} %bitcast.53) | data formatting | bytes 1048576
  19.6 5.7 %all-to-all-start.1 = ((f32[4,1,32768]{2,1,0:T(1,128)}), f32[4,1,32768]{2,1,0:T(1,128)S(1)}, u32[]{:S(2)}, u32[]{:S(2)}) async-start(f32[4,1,32768]{2,1,0:T(1,128)} %reshape.37), calls=%async_computation.1 | async-start | bytes 1048576 | tf_op jit(solution)/shard_map/all_to_all | solution.py:68
  25.2 0.1 copy.16
  25.3 0.2 fusion.109
  25.5 0.2 fusion.108
  25.8 0.0 copy-start.1
  25.8 1.5 fusion.21
  27.2 0.1 reshape.29
  27.3 0.0 collective-permute-done
  27.4 0.0 collective-permute-done.1
  27.4 0.0 copy-done.1
  27.4 2.1 %fusion.18 = f32[8,16,1024]{2,1,0:T(8,128)S(1)} fusion(f32[8,16,1024]{2,1,0:T(8,128)S(1)} %reshape.29, f32[8,14,1024]{2,1,0:T(8,128)} %collective-permute-done.1, f32[8,16,1024]{2,1,0:T(8,128)S(1)} %broadcast_multiply_fusion.1, f32[8,14,1024]{2,1,0:T(8,128)S(1)} %collective-permute-done, f32[16,1024]{1,0:T(8,128)S(1)} %copy-done.1, ...), kind=kOutput, calls=%fused_computation.11 | convolution fusion | flops 70598464 | bytes 2588848 | tf_op jit(solution)/shard_map/awp,wy->ayp/dot_general | solution.py:39
  29.4 2.6 %copy.9 = f32[8,16,1024]{1,0,2:T(8,128)} copy(f32[8,16,1024]{2,1,0:T(8,128)S(1)} %fusion.18) | data formatting | bytes 1048576 | tf_op jit(solution)/shard_map/mul | solution.py:66
  32.1 4.6 %reshape.35 = f32[4,1,32768]{2,1,0:T(1,128)} reshape(f32[1024,8,16]{2,1,0:T(8,128)} %bitcast.50) | data formatting | bytes 1048576
  36.7 3.1 %all-to-all-done.1 = f32[4,1,32768]{2,1,0:T(1,128)S(1)} async-done(((f32[4,1,32768]{2,1,0:T(1,128)}), f32[4,1,32768]{2,1,0:T(1,128)S(1)}, u32[]{:S(2)}, u32[]{:S(2)}) %all-to-all-start.1) | async-done | bytes 524320 | tf_op jit(solution)/shard_map/all_to_all | solution.py:68
  39.8 3.5 %all-to-all-start = ((f32[4,1,32768]{2,1,0:T(1,128)}), f32[4,1,32768]{2,1,0:T(1,128)S(1)}, u32[]{:S(2)}, u32[]{:S(2)}) async-start(f32[4,1,32768]{2,1,0:T(1,128)} %reshape.35), calls=%async_computation | async-start | bytes 1048576 | tf_op jit(solution)/shard_map/all_to_all | solution.py:69
  43.2 0.2 reduce-scatter.2.cloned.1.call-start
  43.5 0.5 broadcast.53
  44.0 2.1 %reduce.1 = f32[4,32768]{1,0:T(4,128)S(1)} reduce(f32[4,1,32768]{2,1,0:T(1,128)S(1)} %all-to-all-done.1, f32[]{:T(128)} %broadcast.53), dimensions={1}, to_apply=%all_to_all.32.reduce_sub_computation | reduce | bytes 1048580 | tf_op jit(solution)/shard_map/all_to_all | solution.py:68
  46.1 3.4 %reshape.38 = f32[1024,8,16]{2,1,0:T(8,128)} reshape(f32[4,32768]{1,0:T(4,128)S(1)} %reduce.1) | data formatting | bytes 1048576
  49.5 2.8 %copy.17 = f32[4,8,16,256]{3,1,2,0:T(8,128)S(1)} copy(f32[4,8,16,256]{2,1,3,0:T(8,128)} %bitcast.51) | data formatting | bytes 1048576
  52.4 4.8 %all-to-all-done = f32[4,1,32768]{2,1,0:T(1,128)S(1)} async-done(((f32[4,1,32768]{2,1,0:T(1,128)}), f32[4,1,32768]{2,1,0:T(1,128)S(1)}, u32[]{:S(2)}, u32[]{:S(2)}) %all-to-all-start) | async-done | bytes 524320 | tf_op jit(solution)/shard_map/all_to_all | solution.py:69
  57.2 2.1 %reduce = f32[4,32768]{1,0:T(4,128)S(1)} reduce(f32[4,1,32768]{2,1,0:T(1,128)S(1)} %all-to-all-done, f32[]{:T(128)} %broadcast.53), dimensions={1}, to_apply=%all_to_all.14.reduce_sub_computation | reduce | bytes 1048580 | tf_op jit(solution)/shard_map/all_to_all | solution.py:69
  59.3 3.4 %reshape.36 = f32[1024,8,16]{2,1,0:T(8,128)} reshape(f32[4,32768]{1,0:T(4,128)S(1)} %reduce) | data formatting | bytes 1048576
  62.7 2.8 %copy.10 = f32[8,16,4,256]{3,0,1,2:T(8,128)S(1)} copy(f32[8,16,4,256]{1,0,3,2:T(8,128)} %bitcast.52) | data formatting | bytes 1048576 | tf_op jit(solution)/shard_map/all_to_all | solution.py:69
  65.6 0.6 fusion.110
  66.1 57.6 %psum.7 = f32[32,32]{1,0:T(8,128)S(1)} all-reduce(f32[32,32]{1,0:T(8,128)S(1)} %fusion.110), channel_id=1, replica_groups=mesh['grp'=2,'orb'=4,'cmp'=4] {'orb','cmp'}, use_global_device_ids=true, to_apply=%region_0.1 | all-reduce | flops 1024 | bytes 8192 | tf_op jit(solution)/shard_map/psum | solution.py:80
  123.8 0.6 convolution_subtract_fusion
  124.4 0.2 copy.18
  124.6 0.0 copy-start
  124.6 12.9 %all_to_all.39 = f32[32,16,256]{2,1,0:T(8,128)S(1)} all-to-all(f32[32,16,256]{2,1,0:T(8,128)S(1)} %bitcast.63), channel_id=1, replica_groups=mesh['grp'=2,'orb'=4,'cmp'=4] {'orb'}, dimensions={0} | all-to-all | bytes 1048576 | tf_op jit(solution)/shard_map/all_to_all | solution.py:84
  137.5 0.1 broadcast_multiply_fusion
  137.6 0.0 copy-done
  137.6 1.5 multiply_reduce_fusion
  139.2 0.0 reduce-scatter.2.cloned.1.call-update
  139.2 18.8 %reduce-scatter.2.cloned.1.call-done = f32[16,256]{1,0:T(8,128)} async-done(((f32[16,1024]{1,0:T(8,128)}), f32[16,256]{1,0:T(8,128)}) %reduce-scatter.2.cloned.1.call-update) | async-done | bytes 16400 | tf_op jit(solution)/shard_map/reduce_scatter | solution.py:87
  158.0 1.3 broadcast_multiply_fusion.2
  (3 shorter events, 0.1 us)
Async XLA Ops:
  9.9 17.4 %collective-permute-start = (f32[8,14,1024]{2,1,0:T(8,128)}, f32[8,14,1024]{2,1,0:T(8,128)S(1)}, u32[]{:S(2)}, u32[]{:S(2)}) collective-permute-start(f32[8,14,1024]{2,1,0:T(8,128)} %get-tuple-element.4), channel_id=1, source_target_pairs={{0,1},{1,2},{2,3},{3,0},{4,5},{5,6},{6,7},{7,4},{8,9},{9,10},{10,1... | collective-permute-start | bytes 1376264 | tf_op jit(solution)/shard_map/ppermute | solution.py:19
  10.4 17.0 %collective-permute-start.1 = (f32[8,14,1024]{2,1,0:T(8,128)S(1)}, f32[8,14,1024]{2,1,0:T(8,128)}, u32[]{:S(2)}, u32[]{:S(2)}) collective-permute-start(f32[8,14,1024]{2,1,0:T(8,128)S(1)} %get-tuple-element.5), channel_id=1, source_target_pairs={{1,0},{2,1},{3,2},{0,3},{5,4},{6,5},{7,6},{4,7},{9,8},{10,9},{11,1... | collective-permute-start | bytes 1376264 | tf_op jit(solution)/shard_map/ppermute | solution.py:21
  19.6 20.2 %all-to-all-start.1 = ((f32[4,1,32768]{2,1,0:T(1,128)}), f32[4,1,32768]{2,1,0:T(1,128)S(1)}, u32[]{:S(2)}, u32[]{:S(2)}) async-start(f32[4,1,32768]{2,1,0:T(1,128)} %reshape.37), calls=%async_computation.1 | async-start | bytes 1048576 | tf_op jit(solution)/shard_map/all_to_all | solution.py:68
  25.8 1.6 copy-start.1
  39.8 17.4 %all-to-all-start = ((f32[4,1,32768]{2,1,0:T(1,128)}), f32[4,1,32768]{2,1,0:T(1,128)S(1)}, u32[]{:S(2)}, u32[]{:S(2)}) async-start(f32[4,1,32768]{2,1,0:T(1,128)} %reshape.35), calls=%async_computation | async-start | bytes 1048576 | tf_op jit(solution)/shard_map/all_to_all | solution.py:69
  43.2 114.8 %reduce-scatter.2.cloned.1.call-start = ((), (), s32[]{:S(2)}) async-start(), calls=%async_computation.4 | async-start | bytes 81920 | tf_op jit(solution)/shard_map/reduce_scatter | solution.py:87
  124.6 13.1 %copy-start = (f32[8,16,1024]{2,1,0:T(8,128)S(1)}, f32[8,16,1024]{2,1,0:T(8,128)}, u32[]{:S(2)}) copy-start(f32[8,16,1024]{2,1,0:T(8,128)} %param.3) | copy-start | bytes 1572868
Sparse Core Ops, SparseCore 0:
  139.3 18.6 reduce-scatter.1
where the time goes:
time: 167 us; the launch traced here: 166 us
  blocking collectives  70.6 us (42%)
  local copies, waits for them, and re-layouts  29.9 us (18%)
  waiting for transfers between devices  26.8 us (16%)
  between operations  14.2 us (9%)
  starting transfers between devices  11.8 us (7%)
  other arithmetic  8.34 us (5%)
  matrix products  4.69 us (3%)
    psum x1, blocking collectives, per_device(): correlation = lax.psum(partial_correlation, ('orb', 'cmp')) / cells  57.6 us
    unnamed x11, local copies, waits for them, and re-layouts  19.2 us
    reduce_scatter x1, waiting for transfers between devices, per_device(): lax.psum_scatter(jnp.sum(psi_new * psi_new, axis=0), 'orb', scatter_dimen...  18.8 us
    all_to_all x1, blocking collectives, per_device(): lax.all_to_all(grad_c, 'orb', split_axis=0, concat_axis=2, tiled=True)  12.9 us
    all_to_all x1, starting transfers between devices, per_device(): lax.all_to_all(phi, 'orb', split_axis=2, concat_axis=0, tiled=True)  5.68 us
    all_to_all x1, waiting for transfers between devices, per_device(): lax.all_to_all(hphi, 'orb', split_axis=2, concat_axis=0, tiled=True)  4.81 us
    all_to_all x1, starting transfers between devices, per_device(): lax.all_to_all(hphi, 'orb', split_axis=2, concat_axis=0, tiled=True)  3.47 us
    all_to_all x2, local copies, waits for them, and re-layouts, per_device(): lax.all_to_all(hphi, 'orb', split_axis=2, concat_axis=0, tiled=True)  3.36 us
  transfers between devices with their start and end apart: 5, of which 3 were waited for; matrix products, arithmetic and copies ran while one was open for 17% of the time, Pallas kernels for 0%

commit v1 on v0

--- a/solution.py
+++ b/solution.py
@@ -1,12 +1,17 @@
+import functools
 import math
 
 import jax
 import jax.numpy as jnp
+import numpy as np
 from jax import lax
+from jax.experimental import pallas as pl
+from jax.experimental.pallas import tpu as pltpu
 from jax.sharding import PartitionSpec as P
 
 step_length = 0.2
 reach = 14
+lanes = 128
 
 
 def padded_2(cells, sides, width):
@@ -52,7 +57,7 @@
     return result.reshape(orbs, planes, grid_p)
 
 
-def per_device(psi, potential, extent):
+def general_device(psi, potential, extent):
     orb_dev, planes, grid_p = psi.shape
     n_orb = lax.axis_size("orb")
     norbitals = orb_dev * n_orb
@@ -90,6 +95,311 @@
     return (psi_new, density)
 
 
+def weight(spread):
+    spread = np.abs(spread)
+    safe = np.maximum(spread, 1).astype(np.float64)
+    value = np.where(spread % 2 == 1, 2.0, -2.0) / (safe * safe)
+    value = np.where(spread == 0, -math.pi**2 / 3.0, value)
+    return np.where(spread <= reach, value, 0.0).astype(np.float32)
+
+
+def two_parts(value):
+    high = value.astype(jnp.bfloat16)
+    return high, (value - high.astype(np.float32)).astype(jnp.bfloat16)
+
+
+def column_band():
+    rows = np.arange(2 * lanes)[:, None]
+    cols = np.arange(lanes)[None, :]
+    high, low = two_parts(weight(rows - cols - reach))
+    return np.concatenate([high, low], axis=1)
+
+
+def plane_band(planes):
+    rows = np.arange(planes)[:, None]
+    cols = np.arange(3 * planes)[None, :]
+    high, low = two_parts(weight(cols - planes - rows))
+    return np.concatenate([high, high, low], axis=1)
+
+
+def in_vmem():
+    return pl.BlockSpec(memory_space=pltpu.VMEM)
+
+
+def in_smem():
+    return pl.BlockSpec(memory_space=pltpu.SMEM)
+
+
+def columns_of(shape):
+    return lax.broadcasted_iota(jnp.int32, shape, len(shape) - 1)
+
+
+def local_kernel(psi_ref, potential_ref, extent_ref, band_ref, out_ref, phi_ref):
+    orbs, planes, grid_p = psi_ref.shape
+    tiles = grid_p // lanes
+    column = columns_of((planes, grid_p))
+    for o in range(orbs):
+        phi_ref[o * planes : (o + 1) * planes, :] = jnp.where(
+            column < extent_ref[o], psi_ref[o], 0.0
+        )
+    moved = pltpu.roll(phi_ref[...], reach, 1)
+    high, low = two_parts(moved)
+    for t in range(tiles):
+        here, after = t * lanes, (t + 1) % tiles * lanes
+        high_t = jnp.concatenate([high[:, here : here + lanes], high[:, after : after + lanes]], 1)
+        low_t = jnp.concatenate([low[:, here : here + lanes], low[:, after : after + lanes]], 1)
+        both = jnp.dot(high_t, band_ref[...], preferred_element_type=jnp.float32)
+        rest = jnp.dot(low_t, band_ref[:, :lanes], preferred_element_type=jnp.float32)
+        second = both[:, :lanes] + both[:, lanes:] + rest
+        field = phi_ref[:, here : here + lanes].reshape(orbs, planes, lanes)
+        out_ref[:, :, here : here + lanes] = (
+            potential_ref[:, here : here + lanes][None] * field
+            - 0.5 * second.reshape(orbs, planes, lanes)
+        )
+
+
+def plane_kernel(before_ref, psi_ref, after_ref, local_ref, extent_ref, band_ref, out_ref):
+    orbs, planes, grid_p = psi_ref.shape
+    column = columns_of((planes, grid_p))
+    for o in range(orbs):
+        slab = jnp.concatenate([before_ref[o], psi_ref[o], after_ref[o]], axis=0)
+        high, low = two_parts(slab)
+        second = jnp.dot(
+            band_ref[...],
+            jnp.concatenate([high, low, high], axis=0),
+            preferred_element_type=jnp.float32,
+        )
+        out_ref[o] = jnp.where(column < extent_ref[o], local_ref[o] - 0.5 * second, 0.0)
+
+
+def overlap_kernel(scale, n_fields, own_fields, *refs):
+    fields = refs[:n_fields]
+    images = refs[n_fields : n_fields + 2]
+    extent_ref, out_ref, rows_ref = refs[n_fields + 2 :]
+    orbs, planes, grid_p = fields[0].shape
+    column = columns_of((planes, grid_p))
+    pieces = [(p, t) for p in range(0, planes, 8) for t in range(0, grid_p, lanes)]
+    for f, field_ref in enumerate(fields):
+
+        def one(a, carry):
+            phi = jnp.where(column < extent_ref[f * orbs + a], field_ref[a], 0.0)
+            for b in range(2 * orbs):
+                image = images[b // orbs]
+                total = None
+                for p, t in pieces:
+                    term = phi[p : p + 8, t : t + lanes] * image[b % orbs, p : p + 8, t : t + lanes]
+                    total = term if total is None else total + term
+                rows_ref[b, pl.ds(f * orbs + a, 1), :] = jnp.sum(total, axis=0, keepdims=True)
+            return carry
+
+        lax.fori_loop(0, orbs, one, 0)
+    for b in range(2 * orbs):
+        out_ref[:, b : b + 1] = jnp.sum(rows_ref[b], axis=1, keepdims=True) * scale
+
+
+def combined(phi_ref, base, coefficient, chunk):
+    total = list(base)
+    for a in range(phi_ref.shape[0]):
+        phi = phi_ref[a, :, chunk]
+        for b in range(len(total)):
+            total[b] = total[b] + coefficient(a, b) * phi
+    return total
+
+
+def density_kernel(
+    own_ref, pair_ref, third_ref, fourth_ref, image_ref, ward_ref, corr_ref, extent_ref, mid_ref,
+    out_ref, phi_ref,
+):
+    orbs, planes, grid_p = own_ref.shape
+    width = 2 * lanes
+
+    @pl.when(mid_ref[0] == 1)
+    def _():
+        column = columns_of((planes, grid_p))
+        for f, field_ref in enumerate((own_ref, pair_ref, third_ref, fourth_ref)):
+            for a in range(orbs):
+                phi_ref[f * orbs + a] = jnp.where(
+                    column < extent_ref[f * orbs + a], field_ref[a], 0.0
+                )
+
+        def one(c, carry):
+            chunk = pl.ds(pl.multiple_of(c * width, width), width)
+            density = jnp.zeros((planes, width), jnp.float32)
+            for part, half_ref in enumerate((image_ref, ward_ref)):
+                base = [
+                    phi_ref[part * orbs + b, :, chunk] - step_length * half_ref[b, :, chunk]
+                    for b in range(orbs)
+                ]
+                total = combined(
+                    phi_ref, base, lambda a, b: step_length * corr_ref[a, part * orbs + b], chunk
+                )
+                for value in total:
+                    density = density + value * value
+            out_ref[:, chunk] = density * (1.0 / phi_ref.shape[0])
+            return carry
+
+        lax.fori_loop(0, grid_p // width, one, 0)
+
+    @pl.when(mid_ref[0] != 1)
+    def _():
+        out_ref[...] = jnp.zeros_like(out_ref)
+
+
+def update_kernel(
+    own_ref, pair_ref, third_in, third_out, fourth_in, fourth_out, image_ref, corr_ref, extent_ref,
+    mid_ref, out_ref, phi_ref,
+):
+    orbs, planes, grid_p = own_ref.shape
+    width = 2 * lanes
+    column = columns_of((planes, grid_p))
+
+    def put(first, field_ref):
+        for a in range(orbs):
+            phi_ref[first + a] = jnp.where(column < extent_ref[first + a], field_ref[a], 0.0)
+
+    put(0, own_ref)
+    put(orbs, pair_ref)
+
+    @pl.when(mid_ref[0] == 1)
+    def _():
+        put(2 * orbs, third_in)
+        put(3 * orbs, fourth_in)
+
+    @pl.when(mid_ref[0] != 1)
+    def _():
+        put(2 * orbs, third_out)
+        put(3 * orbs, fourth_out)
+
+    def one(c, carry):
+        chunk = pl.ds(pl.multiple_of(c * width, width), width)
+        base = [phi_ref[b, :, chunk] - step_length * image_ref[b, :, chunk] for b in range(orbs)]
+        total = combined(phi_ref, base, lambda a, b: step_length * corr_ref[a, b], chunk)
+        for b in range(orbs):
+            out_ref[b, :, chunk] = total[b]
+        return carry
+
+    lax.fori_loop(0, grid_p // width, one, 0)
+
+
+params = pltpu.CompilerParams(vmem_limit_bytes=24 * 2**20)
+small = pl.CostEstimate(flops=1, bytes_accessed=1, transcendentals=0)
+
+
+def line_device(psi, potential, extent):
+    orbs, planes, grid_p = psi.shape
+    n_cmp = lax.axis_size("cmp")
+    norbitals = 4 * orbs
+    cells = planes * n_cmp * grid_p
+    z = lax.axis_index("orb")
+    inner = (z == 1) | (z == 2)
+    swap = [(0, 1), (1, 0), (2, 3), (3, 2)]
+    across = [(1, 2), (2, 1)]
+    outward = [(1, 0), (2, 3)]
+    inward = [(0, 1), (3, 2)]
+
+    third_of = jnp.where(z < 2, 2, 1)
+    fourth_of = jnp.where(z < 2, 3, 0)
+    by_owner = extent.reshape(4, orbs)
+    order = jnp.stack([z, z ^ 1, third_of, fourth_of])
+    extents = jnp.take(by_owner, order, axis=0).reshape(-1)
+    own_extent = extents[:orbs]
+    is_inner = inner.astype(jnp.int32).reshape(1)
+
+    block = jax.ShapeDtypeStruct(psi.shape, jnp.float32)
+
+    pair = lax.ppermute(psi, "orb", swap)
+    third_in = lax.ppermute(psi, "orb", across)
+    before = lax.ppermute(psi, "cmp", [(i, (i + 1) % n_cmp) for i in range(n_cmp)])
+    after = lax.ppermute(psi, "cmp", [((i + 1) % n_cmp, i) for i in range(n_cmp)])
+
+    local = pl.pallas_call(
+        local_kernel,
+        out_shape=block,
+        in_specs=[in_vmem(), in_vmem(), in_smem(), in_vmem()],
+        out_specs=in_vmem(),
+        scratch_shapes=[pltpu.VMEM((orbs * planes, grid_p), jnp.float32)],
+        compiler_params=params,
+        cost_estimate=small,
+    )(psi, potential, own_extent, jnp.asarray(column_band()))
+    image = pl.pallas_call(
+        plane_kernel,
+        out_shape=block,
+        in_specs=[in_vmem()] * 4 + [in_smem(), in_vmem()],
+        out_specs=in_vmem(),
+        compiler_params=params,
+        cost_estimate=small,
+    )(before, psi, after, local, own_extent, jnp.asarray(plane_band(planes)))
+
+    ward = lax.ppermute(image, "orb", inward)
+    fourth_in = lax.ppermute(pair, "orb", across)
+    third_out = lax.ppermute(third_in, "orb", outward)
+    fourth_out = lax.ppermute(fourth_in, "orb", outward)
+
+    ward, fourth_in, third_out = lax.optimization_barrier((ward, fourth_in, third_out))
+
+    part = pl.pallas_call(
+        functools.partial(overlap_kernel, 1.0 / cells, 4, 3),
+        out_shape=jax.ShapeDtypeStruct((norbitals, 2 * orbs), jnp.float32),
+        in_specs=[in_vmem()] * 6 + [in_smem()],
+        out_specs=in_vmem(),
+        scratch_shapes=[pltpu.VMEM((2 * orbs, norbitals, lanes), jnp.float32)],
+        compiler_params=params,
+        cost_estimate=small,
+    )(psi, pair, third_in, fourth_in, image, ward, extents)
+    near = lax.ppermute(part, "cmp", [(i, i ^ 1) for i in range(n_cmp)])
+    far = lax.ppermute(part, "cmp", [(i, i ^ 2) for i in range(n_cmp)])
+    farther = lax.ppermute(part, "cmp", [(i, i ^ 3) for i in range(n_cmp)])
+    correlation = (part + near) + (far + farther)
+
+    given = lax.ppermute(correlation, "orb", outward)
+    given = given.reshape(4, orbs, 2 * orbs)[:, :, orbs:]
+    given = jnp.concatenate([given[1], given[0], given[2], given[3]], axis=0)
+    own_correlation = jnp.where(inner, correlation[:, :orbs], given)
+
+    density = pl.pallas_call(
+        density_kernel,
+        out_shape=jax.ShapeDtypeStruct((planes, grid_p), jnp.float32),
+        in_specs=[in_vmem()] * 6 + [in_smem()] * 3,
+        out_specs=in_vmem(),
+        scratch_shapes=[pltpu.VMEM((norbitals, planes, grid_p), jnp.float32)],
+        compiler_params=params,
+        cost_estimate=small,
+    )(psi, pair, third_in, fourth_in, image, ward, correlation, extents, is_inner)
+
+    share = grid_p // 4
+    owned = lambda who: lax.dynamic_slice_in_dim(density, who * share, share, 1)
+    total = owned(z)
+    total = total + lax.ppermute(owned(z ^ 1), "orb", [(1, 0), (2, 3)])
+    total = total + lax.ppermute(owned(z ^ 2), "orb", [(1, 3), (2, 0)])
+    total = total + lax.ppermute(owned(z ^ 3), "orb", [(1, 2), (2, 1)])
+
+    psi_new = pl.pallas_call(
+        update_kernel,
+        out_shape=block,
+        in_specs=[in_vmem()] * 7 + [in_smem()] * 3,
+        out_specs=in_vmem(),
+        scratch_shapes=[pltpu.VMEM((norbitals, planes, grid_p), jnp.float32)],
+        compiler_params=params,
+        cost_estimate=small,
+    )(
+        psi, pair, third_in, third_out, fourth_in, fourth_out, image, own_correlation, extents,
+        is_inner,
+    )
+    return (psi_new, total)
+
+
+def per_device(psi, potential, extent):
+    orbs, planes, grid_p = psi.shape
+    fits = (
+        lax.axis_size("orb") == 4
+        and lax.axis_size("cmp") == 4
+        and orbs == 8
+        and planes == 16
+        and grid_p % (4 * lanes) == 0
+    )
+    return (line_device if fits else general_device)(psi, potential, extent)
+
+
 def solution(mesh):
     return jax.shard_map(
         per_device,

time: 167 us -> 65.9 us (0.39)
  blocking collectives: 70.6 us -> 0 us
  local copies, waits for them, and re-layouts: 29.9 us -> 3.43 us
  between operations: 14.2 us -> 0.79 us
  Pallas kernels: 0 us -> 10 us
  starting transfers between devices: 11.8 us -> 21.3 us
  other arithmetic: 8.34 us -> 0.87 us
  matrix products: 4.69 us -> 0 us
  waiting for transfers between devices: 26.8 us -> 29.1 us
    psum x1 -> x0, blocking collectives: 57.6 us -> none  [per_device(): correlation = lax.psum(partial_correlation, ('orb', 'cmp')) / cells]
    ppermute x2 -> x15, waiting for transfers between devices: 0.01 us -> 29.1 us  [the longest x1 11.1 us: line_device(): given = lax.ppermute(correlation, 'orb', outward)]
    ppermute x2 -> x15, starting transfers between devices: 2.38 us -> 21.3 us  [the longest x1 4.44 us: line_device(): pair = lax.ppermute(psi, 'orb', swap)]
    reduce_scatter x1 -> x0, waiting for transfers between devices: 18.8 us -> none  [per_device(): lax.psum_scatter(jnp.sum(psi_new * psi_new, axis=0), 'orb', scatter_dimen...]
    unnamed x11 -> x10, local copies, waits for them, and re-layouts: 19.2 us -> 1.96 us
    all_to_all x1 -> x0, blocking collectives: 12.9 us -> none  [per_device(): lax.all_to_all(grad_c, 'orb', split_axis=0, concat_axis=2, tiled=True)]
    pallas_call x0 -> x5, Pallas kernels: none -> 10 us  [the longest x1 3.77 us: line_device(): pl.pallas_call(functools.partial(overlap_kernel, 1.0 / cells, 4, 3), out_...]
    all_to_all x2 -> x0, starting transfers between devices: 9.16 us -> none  [the longest x1 5.68 us: per_device(): lax.all_to_all(phi, 'orb', split_axis=2, concat_axis=0, tiled=True)]
  transfers between devices with their start and end apart: 5 -> 15, of which waited for: 3 -> 8; matrix products, arithmetic and copies ran while one was open for 17% -> 4% of each run, Pallas kernels for 0% -> 4%
where the time goes in v1:
time: 65.9 us; the launch traced here: 65.5 us
  waiting for transfers between devices  29.1 us (44%)
  starting transfers between devices  21.3 us (32%)
  Pallas kernels  10 us (15%)
  local copies, waits for them, and re-layouts  3.43 us (5%)
  other arithmetic  0.87 us (1%)
  between operations  0.79 us (1%)
    ppermute x1, waiting for transfers between devices, line_device(): given = lax.ppermute(correlation, 'orb', outward)  11.1 us
    ppermute x1, waiting for transfers between devices, line_device(): ward = lax.ppermute(image, 'orb', inward)  8.44 us
    ppermute x1, starting transfers between devices, line_device(): pair = lax.ppermute(psi, 'orb', swap)  4.44 us
    ppermute x1, waiting for transfers between devices, line_device(): third_out = lax.ppermute(third_in, 'orb', outward)  4.26 us
    pallas_call x1, Pallas kernels, line_device(): pl.pallas_call(functools.partial(overlap_kernel, 1.0 / cells, 4, 3), out_...  3.77 us
    ppermute x1, starting transfers between devices, line_device(): ward = lax.ppermute(image, 'orb', inward)  3.51 us
    pallas_call x1, Pallas kernels, line_device(): pl.pallas_call(update_kernel, out_shape=block, in_specs=[in_vmem()] * 7 +...  3.42 us
    ppermute x1, waiting for transfers between devices, line_device(): lax.ppermute(psi, 'cmp', [((i + 1) % n_cmp, i) for i in range(n_cmp)])  2.88 us
  transfers between devices with their start and end apart: 15, of which 8 were waited for; matrix products, arithmetic and copies ran while one was open for 4% of the time, Pallas kernels for 4%

profile of v1, /device:TPU:0, one launch (start us, length us, event | category | flops | bytes accessed | tf_op | source)
XLA Modules:
  0.0 65.5 jit_solution(1339815400925461866)
XLA Ops:
  0.6 0.0 copy-start.3
  0.6 2.4 %collective-permute-start.3 = (f32[8,16,1024]{2,1,0:T(8,128)}, f32[8,16,1024]{2,1,0:T(8,128)S(1)}, u32[]{:S(2)}, u32[]{:S(2)}) collective-permute-start(f32[8,16,1024]{2,1,0:T(8,128)} %own_ref.3), channel_id=1, source_target_pairs={{1,0},{2,1},{3,2},{0,3},{5,4},{6,5},{7,6},{4,7},{9,8},{10,9},{11,1... | collective-permute-start | bytes 1572872 | tf_op jit(solution)/shard_map/ppermute | solution.py:313
  3.1 0.0 collective-permute-start.2
  3.1 0.7 %collective-permute-start.1 = (f32[8,16,1024]{2,1,0:T(8,128)}, f32[8,16,1024]{2,1,0:T(8,128)S(1)}, u32[]{:S(2)}, u32[]{:S(2)}) collective-permute-start(f32[8,16,1024]{2,1,0:T(8,128)} %own_ref.3), channel_id=1, source_target_pairs={{4,8},{8,4},{5,9},{9,5},{6,10},{10,6},{7,11},{11,7},{20,24},{24,20... | collective-permute-start | bytes 1572872 | tf_op jit(solution)/shard_map/ppermute | solution.py:311
  3.8 4.4 %collective-permute-start = (f32[8,16,1024]{2,1,0:T(8,128)}, f32[8,16,1024]{2,1,0:T(8,128)S(1)}, u32[]{:S(2)}, u32[]{:S(2)}) collective-permute-start(f32[8,16,1024]{2,1,0:T(8,128)} %own_ref.3), channel_id=1, source_target_pairs={{0,4},{4,0},{8,12},{12,8},{1,5},{5,1},{9,13},{13,9},{2,6},{6,2},{1... | collective-permute-start | bytes 1572872 | tf_op jit(solution)/shard_map/ppermute | solution.py:310
  8.2 0.7 %reshape.202 = s32[4,8]{1,0:T(4,128)S(1)} reshape(s32[32]{0:T(128)} %param.7) | data formatting | bytes 256 | tf_op jit(solution)/shard_map/reshape | solution.py:302
  8.9 0.1 fusion
  9.0 0.6 gather_fusion
  9.6 0.1 compare_and_fusion
  9.7 0.1 broadcast_select_fusion
  9.7 0.0 copy-done.3
  9.7 0.0 copy-start
  9.8 1.0 %copy-done = f32[8,16,1024]{2,1,0:T(8,128)S(1)} copy-done((f32[8,16,1024]{2,1,0:T(8,128)S(1)}, f32[8,16,1024]{2,1,0:T(8,128)}, u32[]{:S(2)}) %copy-start) | copy-done | bytes 524312
  10.8 0.0 copy-start.2
  10.8 0.9 %copy-done.2 = bf16[256,256]{1,0:T(8,128)(2,1)S(1)} copy-done((bf16[256,256]{1,0:T(8,128)(2,1)S(1)}, bf16[256,256]{1,0:T(8,128)(2,1)}, u32[]{:S(2)}) %copy-start.2) | copy-done | bytes 131096
  11.7 0.0 copy-start.4
  11.7 1.1 %shard_map.68.local_ref = f32[8,16,1024]{2,1,0:T(8,128)S(1)} custom-call(f32[8,16,1024]{2,1,0:T(8,128)S(1)} %copy-done, f32[16,1024]{1,0:T(8,128)S(1)} %copy-done.3, s32[8]{0:T(128)S(1)} %slice_bitcast_fusion.4.extent_ref, bf16[256,256]{1,0:T(8,128)(2,1)S(1)} %copy-done.2), custom_call_target="tpu_custom_call" | custom-call | flops 1 | bytes 1 | tf_op jit(solution)/shard_map/pallas_call | solution.py:315
  12.8 0.0 copy-start.1
  12.8 2.9 %collective-permute-done.3.after_ref = f32[8,16,1024]{2,1,0:T(8,128)S(1)} collective-permute-done((f32[8,16,1024]{2,1,0:T(8,128)}, f32[8,16,1024]{2,1,0:T(8,128)S(1)}, u32[]{:S(2)}, u32[]{:S(2)}) %collective-permute-start.3) | collective-permute-done | bytes 524320 | tf_op jit(solution)/shard_map/ppermute | solution.py:313
  15.6 1.0 %collective-permute-done.2.before_ref = f32[8,16,1024]{2,1,0:T(8,128)S(1)} collective-permute-done((f32[8,16,1024]{2,1,0:T(8,128)}, f32[8,16,1024]{2,1,0:T(8,128)S(1)}, u32[]{:S(2)}, u32[]{:S(2)}) %collective-permute-start.2) | collective-permute-done | bytes 524320 | tf_op jit(solution)/shard_map/ppermute | solution.py:312
  16.6 0.0 copy-done.4
  16.6 1.0 %shard_map.69.refs_4_.image_ref = f32[8,16,1024]{2,1,0:T(8,128)S(1)} custom-call(f32[8,16,1024]{2,1,0:T(8,128)S(1)} %collective-permute-done.2.before_ref, f32[8,16,1024]{2,1,0:T(8,128)S(1)} %copy-done, f32[8,16,1024]{2,1,0:T(8,128)S(1)} %collective-permute-done.3.after_ref, f32[8,16,1024]{2,1,0:T(8,128)S(1)} %shard_map.68.local_ref, ...), custom_call_target="tpu_custom_call" | custom-call | flops 1 | bytes 1 | tf_op jit(solution)/shard_map/pallas_call | solution.py:324
  17.6 3.5 %collective-permute-start.4 = (f32[8,16,1024]{2,1,0:T(8,128)S(1)}, f32[8,16,1024]{2,1,0:T(8,128)S(1)}, u32[]{:S(2)}, u32[]{:S(2)}) collective-permute-start(f32[8,16,1024]{2,1,0:T(8,128)S(1)} %shard_map.69.refs_4_.image_ref), channel_id=1, source_target_pairs={{0,4},{12,8},{1,5},{13,9},{2,6},{14,10},{3,7},{15,11},{16,20},{28,... | collective-permute-start | bytes 1572872 | tf_op jit(solution)/shard_map/ppermute | solution.py:333
  21.1 0.0 collective-permute-done.1.refs_2_.third_in.third_ref
  21.1 1.3 %collective-permute-start.6 = (f32[8,16,1024]{2,1,0:T(8,128)S(1)}, f32[8,16,1024]{2,1,0:T(8,128)}, u32[]{:S(2)}, u32[]{:S(2)}) collective-permute-start(f32[8,16,1024]{2,1,0:T(8,128)S(1)} %collective-permute-done.1.refs_2_.third_in.third_ref), channel_id=1, source_target_pairs={{4,0},{8,12},{5,1},{9,13},{6,2},{10,14},{7,3},{11,15},{20,16},{24,... | collective-permute-start | bytes 1572872 | tf_op jit(solution)/shard_map/ppermute | solution.py:335
  22.4 0.0 collective-permute-done.refs_1_.pair_ref
  22.4 0.7 %collective-permute-start.5 = (f32[8,16,1024]{2,1,0:T(8,128)S(1)}, f32[8,16,1024]{2,1,0:T(8,128)S(1)}, u32[]{:S(2)}, u32[]{:S(2)}) collective-permute-start(f32[8,16,1024]{2,1,0:T(8,128)S(1)} %collective-permute-done.refs_1_.pair_ref), channel_id=1, source_target_pairs={{4,8},{8,4},{5,9},{9,5},{6,10},{10,6},{7,11},{11,7},{20,24},{24,20... | collective-permute-start | bytes 1572872 | tf_op jit(solution)/shard_map/ppermute | solution.py:334
  23.1 0.1 select_n.57.refs_6_.extent_ref
  23.2 8.4 %collective-permute-done.4.refs_5_.ward_ref = f32[8,16,1024]{2,1,0:T(8,128)S(1)} collective-permute-done((f32[8,16,1024]{2,1,0:T(8,128)S(1)}, f32[8,16,1024]{2,1,0:T(8,128)S(1)}, u32[]{:S(2)}, u32[]{:S(2)}) %collective-permute-start.4) | collective-permute-done | bytes 524320 | tf_op jit(solution)/shard_map/ppermute | solution.py:333
  31.7 4.3 %collective-permute-done.6.third_out = f32[8,16,1024]{2,1,0:T(8,128)} collective-permute-done((f32[8,16,1024]{2,1,0:T(8,128)S(1)}, f32[8,16,1024]{2,1,0:T(8,128)}, u32[]{:S(2)}, u32[]{:S(2)}) %collective-permute-start.6) | collective-permute-done | bytes 524320 | tf_op jit(solution)/shard_map/ppermute | solution.py:335
  35.9 0.0 collective-permute-done.5.refs_3_.fourth_in.fourth_ref
  35.9 0.0 copy-done.1
  35.9 3.8 %shard_map.70 = f32[32,16]{1,0:T(8,128)S(1)} custom-call(f32[8,16,1024]{2,1,0:T(8,128)S(1)} %copy-done.1, f32[8,16,1024]{2,1,0:T(8,128)S(1)} %collective-permute-done.refs_1_.pair_ref, f32[8,16,1024]{2,1,0:T(8,128)S(1)} %collective-permute-done.1.refs_2_.third_in.third_ref, f32[8,16,1024]{2,1,0:T(8,128)S(1)} %collective-permute-done.5.refs_3_.fourth_in.fourth_ref, ...), custom_call_target="tpu_custom_call" | custom-call | flops 1 | bytes 1 | tf_op jit(solution)/shard_map/pallas_call | solution.py:340
  39.7 0.8 %collective-permute-start.10 = (f32[32,16]{1,0:T(8,128)S(1)}, f32[32,16]{1,0:T(8,128)S(1)}, u32[]{:S(2)}, u32[]{:S(2)}) collective-permute-start(f32[32,16]{1,0:T(8,128)S(1)} %shard_map.70), channel_id=1, source_target_pairs={{0,3},{1,2},{2,1},{3,0},{4,7},{5,6},{6,5},{7,4},{8,11},{9,10},{10,... | collective-permute-start | bytes 6152 | tf_op jit(solution)/shard_map/ppermute | solution.py:351
  40.5 1.6 %collective-permute-start.9 = (f32[32,16]{1,0:T(8,128)S(1)}, f32[32,16]{1,0:T(8,128)S(1)}, u32[]{:S(2)}, u32[]{:S(2)}) collective-permute-start(f32[32,16]{1,0:T(8,128)S(1)} %shard_map.70), channel_id=1, source_target_pairs={{0,2},{1,3},{2,0},{3,1},{4,6},{5,7},{6,4},{7,5},{8,10},{9,11},{10,... | collective-permute-start | bytes 6152 | tf_op jit(solution)/shard_map/ppermute | solution.py:350
  42.1 0.0 collective-permute-start.8
  42.2 1.3 %collective-permute-start.7 = (f32[8,16,1024]{2,1,0:T(8,128)S(1)}, f32[8,16,1024]{2,1,0:T(8,128)S(1)}, u32[]{:S(2)}, u32[]{:S(2)}) collective-permute-start(f32[8,16,1024]{2,1,0:T(8,128)S(1)} %collective-permute-done.5.refs_3_.fourth_in.fourth_ref), channel_id=1, source_target_pairs={{4,0},{8,12},{5,1},{9,13},{6,2},{10,14},{7,3},{11,15},{20,16},{24,... | collective-permute-start | bytes 1572872 | tf_op jit(solution)/shard_map/ppermute | solution.py:336
  43.4 0.0 collective-permute-done.10
  43.5 0.8 %collective-permute-done.9 = f32[32,16]{1,0:T(8,128)S(1)} collective-permute-done((f32[32,16]{1,0:T(8,128)S(1)}, f32[32,16]{1,0:T(8,128)S(1)}, u32[]{:S(2)}, u32[]{:S(2)}) %collective-permute-start.9) | collective-permute-done | bytes 2080 | tf_op jit(solution)/shard_map/ppermute | solution.py:350
  44.3 0.0 collective-permute-done.8
  44.3 1.3 %collective-permute-start.11 = (f32[32,16]{1,0:T(8,128)S(1)}, f32[32,16]{1,0:T(8,128)S(1)}, u32[]{:S(2)}, u32[]{:S(2)}) collective-permute-start(f32[32,16]{1,0:T(8,128)S(1)} %add_add_fusion.1.corr_ref), channel_id=1, source_target_pairs={{4,0},{8,12},{5,1},{9,13},{6,2},{10,14},{7,3},{11,15},{20,16},{24,... | collective-permute-start | bytes 6152 | tf_op jit(solution)/shard_map/ppermute | solution.py:354
  45.6 0.8 %shard_map.72 = f32[16,1024]{1,0:T(8,128)S(1)} custom-call(f32[8,16,1024]{2,1,0:T(8,128)S(1)} %copy-done.1, f32[8,16,1024]{2,1,0:T(8,128)S(1)} %collective-permute-done.refs_1_.pair_ref, f32[8,16,1024]{2,1,0:T(8,128)S(1)} %collective-permute-done.1.refs_2_.third_in.third_ref, f32[8,16,1024]{2,1,0:T(8,128)S(1)} %collective-permute-done.5.refs_3_.fourth_in.fourth_ref, ...), custom_call_target="tpu_custom_call" | custom-call | flops 1 | bytes 1 | tf_op jit(solution)/shard_map/pallas_call | solution.py:359
  46.5 1.3 %collective-permute-start.12 = (f32[16,256]{1,0:T(8,128)S(1)}, f32[16,256]{1,0:T(8,128)S(1)}, u32[]{:S(2)}, u32[]{:S(2)}) collective-permute-start(f32[16,256]{1,0:T(8,128)S(1)} %get-tuple-element.8), channel_id=1, source_target_pairs={{4,0},{8,12},{5,1},{9,13},{6,2},{10,14},{7,3},{11,15},{20,16},{24,... | collective-permute-start | bytes 49160 | tf_op jit(solution)/shard_map/ppermute | solution.py:372
  47.8 0.7 %collective-permute-start.14 = (f32[16,256]{1,0:T(8,128)S(1)}, f32[16,256]{1,0:T(8,128)S(1)}, u32[]{:S(2)}, u32[]{:S(2)}) collective-permute-start(f32[16,256]{1,0:T(8,128)S(1)} %get-tuple-element.9), channel_id=1, source_target_pairs={{4,8},{8,4},{5,9},{9,5},{6,10},{10,6},{7,11},{11,7},{20,24},{24,20... | collective-permute-start | bytes 49160 | tf_op jit(solution)/shard_map/ppermute | solution.py:374
  48.4 1.3 %collective-permute-start.13 = (f32[16,256]{1,0:T(8,128)S(1)}, f32[16,256]{1,0:T(8,128)S(1)}, u32[]{:S(2)}, u32[]{:S(2)}) collective-permute-start(f32[16,256]{1,0:T(8,128)S(1)} %get-tuple-element.10), channel_id=1, source_target_pairs={{4,12},{8,0},{5,13},{9,1},{6,14},{10,2},{7,15},{11,3},{20,28},{24,... | collective-permute-start | bytes 49160 | tf_op jit(solution)/shard_map/ppermute | solution.py:373
  49.7 11.1 %collective-permute-done.11 = f32[32,16]{1,0:T(8,128)S(1)} collective-permute-done((f32[32,16]{1,0:T(8,128)S(1)}, f32[32,16]{1,0:T(8,128)S(1)}, u32[]{:S(2)}, u32[]{:S(2)}) %collective-permute-start.11) | collective-permute-done | bytes 2080 | tf_op jit(solution)/shard_map/ppermute | solution.py:354
  60.9 0.1 slice_bitcast_fusion.3
  60.9 0.1 collective-permute-done.12
  61.0 0.0 collective-permute-done.14
  61.0 0.4 collective-permute-done.13
  61.5 0.6 add_add_fusion
  62.1 0.0 collective-permute-done.7.fourth_out
  62.1 3.4 %shard_map.71 = f32[8,16,1024]{2,1,0:T(8,128)} custom-call(f32[8,16,1024]{2,1,0:T(8,128)S(1)} %copy-done.1, f32[8,16,1024]{2,1,0:T(8,128)S(1)} %collective-permute-done.refs_1_.pair_ref, f32[8,16,1024]{2,1,0:T(8,128)S(1)} %collective-permute-done.1.refs_2_.third_in.third_ref, f32[8,16,1024]{2,1,0:T(8,128)} %collective-permute-done.6.third_out, ...), custom_call_target="tpu_custom_call" | custom-call | flops 1 | bytes 1 | tf_op jit(solution)/shard_map/pallas_call | solution.py:376
  (5 shorter events, 0.0 us)
Async XLA Ops:
  0.6 9.1 %copy-start.3 = (f32[16,1024]{1,0:T(8,128)S(1)}, f32[16,1024]{1,0:T(8,128)}, u32[]{:S(2)}) copy-start(f32[16,1024]{1,0:T(8,128)} %potential_ref.1) | copy-start | bytes 196612
  0.6 15.0 %collective-permute-start.3 = (f32[8,16,1024]{2,1,0:T(8,128)}, f32[8,16,1024]{2,1,0:T(8,128)S(1)}, u32[]{:S(2)}, u32[]{:S(2)}) collective-permute-start(f32[8,16,1024]{2,1,0:T(8,128)} %own_ref.3), channel_id=1, source_target_pairs={{1,0},{2,1},{3,2},{0,3},{5,4},{6,5},{7,6},{4,7},{9,8},{10,9},{11,1... | collective-permute-start | bytes 1572872 | tf_op jit(solution)/shard_map/ppermute | solution.py:313
  3.1 13.6 %collective-permute-start.2 = (f32[8,16,1024]{2,1,0:T(8,128)}, f32[8,16,1024]{2,1,0:T(8,128)S(1)}, u32[]{:S(2)}, u32[]{:S(2)}) collective-permute-start(f32[8,16,1024]{2,1,0:T(8,128)} %own_ref.3), channel_id=1, source_target_pairs={{0,1},{1,2},{2,3},{3,0},{4,5},{5,6},{6,7},{7,4},{8,9},{9,10},{10,1... | collective-permute-start | bytes 1572872 | tf_op jit(solution)/shard_map/ppermute | solution.py:312
  3.1 18.0 %collective-permute-start.1 = (f32[8,16,1024]{2,1,0:T(8,128)}, f32[8,16,1024]{2,1,0:T(8,128)S(1)}, u32[]{:S(2)}, u32[]{:S(2)}) collective-permute-start(f32[8,16,1024]{2,1,0:T(8,128)} %own_ref.3), channel_id=1, source_target_pairs={{4,8},{8,4},{5,9},{9,5},{6,10},{10,6},{7,11},{11,7},{20,24},{24,20... | collective-permute-start | bytes 1572872 | tf_op jit(solution)/shard_map/ppermute | solution.py:311
  3.8 18.7 %collective-permute-start = (f32[8,16,1024]{2,1,0:T(8,128)}, f32[8,16,1024]{2,1,0:T(8,128)S(1)}, u32[]{:S(2)}, u32[]{:S(2)}) collective-permute-start(f32[8,16,1024]{2,1,0:T(8,128)} %own_ref.3), channel_id=1, source_target_pairs={{0,4},{4,0},{8,12},{12,8},{1,5},{5,1},{9,13},{13,9},{2,6},{6,2},{1... | collective-permute-start | bytes 1572872 | tf_op jit(solution)/shard_map/ppermute | solution.py:310
  9.7 1.0 %copy-start = (f32[8,16,1024]{2,1,0:T(8,128)S(1)}, f32[8,16,1024]{2,1,0:T(8,128)}, u32[]{:S(2)}) copy-start(f32[8,16,1024]{2,1,0:T(8,128)} %own_ref.3) | copy-start | bytes 1572868
  10.8 0.9 %copy-start.2 = (bf16[256,256]{1,0:T(8,128)(2,1)S(1)}, bf16[256,256]{1,0:T(8,128)(2,1)}, u32[]{:S(2)}) copy-start(bf16[256,256]{1,0:T(8,128)(2,1)} %constant.35.clone.band_ref) | copy-start | bytes 393220
  11.7 4.9 %copy-start.4 = (bf16[16,144]{1,0:T(8,128)(2,1)S(1)}, bf16[16,144]{1,0:T(8,128)(2,1)}, u32[]{:S(2)}) copy-start(bf16[16,144]{1,0:T(8,128)(2,1)} %constant.36.clone.band_ref) | copy-start | bytes 13828
  12.8 23.2 %copy-start.1 = (f32[8,16,1024]{2,1,0:T(8,128)S(1)}, f32[8,16,1024]{2,1,0:T(8,128)}, u32[]{:S(2)}) copy-start(f32[8,16,1024]{2,1,0:T(8,128)} %own_ref.3) | copy-start | bytes 1572868
  17.6 14.1 %collective-permute-start.4 = (f32[8,16,1024]{2,1,0:T(8,128)S(1)}, f32[8,16,1024]{2,1,0:T(8,128)S(1)}, u32[]{:S(2)}, u32[]{:S(2)}) collective-permute-start(f32[8,16,1024]{2,1,0:T(8,128)S(1)} %shard_map.69.refs_4_.image_ref), channel_id=1, source_target_pairs={{0,4},{12,8},{1,5},{13,9},{2,6},{14,10},{3,7},{15,11},{16,20},{28,... | collective-permute-start | bytes 1572872 | tf_op jit(solution)/shard_map/ppermute | solution.py:333
  21.1 14.8 %collective-permute-start.6 = (f32[8,16,1024]{2,1,0:T(8,128)S(1)}, f32[8,16,1024]{2,1,0:T(8,128)}, u32[]{:S(2)}, u32[]{:S(2)}) collective-permute-start(f32[8,16,1024]{2,1,0:T(8,128)S(1)} %collective-permute-done.1.refs_2_.third_in.third_ref), channel_id=1, source_target_pairs={{4,0},{8,12},{5,1},{9,13},{6,2},{10,14},{7,3},{11,15},{20,16},{24,... | collective-permute-start | bytes 1572872 | tf_op jit(solution)/shard_map/ppermute | solution.py:335
  22.4 13.5 %collective-permute-start.5 = (f32[8,16,1024]{2,1,0:T(8,128)S(1)}, f32[8,16,1024]{2,1,0:T(8,128)S(1)}, u32[]{:S(2)}, u32[]{:S(2)}) collective-permute-start(f32[8,16,1024]{2,1,0:T(8,128)S(1)} %collective-permute-done.refs_1_.pair_ref), channel_id=1, source_target_pairs={{4,8},{8,4},{5,9},{9,5},{6,10},{10,6},{7,11},{11,7},{20,24},{24,20... | collective-permute-start | bytes 1572872 | tf_op jit(solution)/shard_map/ppermute | solution.py:334
  39.7 3.7 %collective-permute-start.10 = (f32[32,16]{1,0:T(8,128)S(1)}, f32[32,16]{1,0:T(8,128)S(1)}, u32[]{:S(2)}, u32[]{:S(2)}) collective-permute-start(f32[32,16]{1,0:T(8,128)S(1)} %shard_map.70), channel_id=1, source_target_pairs={{0,3},{1,2},{2,1},{3,0},{4,7},{5,6},{6,5},{7,4},{8,11},{9,10},{10,... | collective-permute-start | bytes 6152 | tf_op jit(solution)/shard_map/ppermute | solution.py:351
  40.5 3.7 %collective-permute-start.9 = (f32[32,16]{1,0:T(8,128)S(1)}, f32[32,16]{1,0:T(8,128)S(1)}, u32[]{:S(2)}, u32[]{:S(2)}) collective-permute-start(f32[32,16]{1,0:T(8,128)S(1)} %shard_map.70), channel_id=1, source_target_pairs={{0,2},{1,3},{2,0},{3,1},{4,6},{5,7},{6,4},{7,5},{8,10},{9,11},{10,... | collective-permute-start | bytes 6152 | tf_op jit(solution)/shard_map/ppermute | solution.py:350
  42.1 2.2 %collective-permute-start.8 = (f32[32,16]{1,0:T(8,128)S(1)}, f32[32,16]{1,0:T(8,128)S(1)}, u32[]{:S(2)}, u32[]{:S(2)}) collective-permute-start(f32[32,16]{1,0:T(8,128)S(1)} %shard_map.70), channel_id=1, source_target_pairs={{0,1},{1,0},{2,3},{3,2},{4,5},{5,4},{6,7},{7,6},{8,9},{9,8},{10,11... | collective-permute-start | bytes 6152 | tf_op jit(solution)/shard_map/ppermute | solution.py:349
  42.2 19.9 %collective-permute-start.7 = (f32[8,16,1024]{2,1,0:T(8,128)S(1)}, f32[8,16,1024]{2,1,0:T(8,128)S(1)}, u32[]{:S(2)}, u32[]{:S(2)}) collective-permute-start(f32[8,16,1024]{2,1,0:T(8,128)S(1)} %collective-permute-done.5.refs_3_.fourth_in.fourth_ref), channel_id=1, source_target_pairs={{4,0},{8,12},{5,1},{9,13},{6,2},{10,14},{7,3},{11,15},{20,16},{24,... | collective-permute-start | bytes 1572872 | tf_op jit(solution)/shard_map/ppermute | solution.py:336
  44.3 16.6 %collective-permute-start.11 = (f32[32,16]{1,0:T(8,128)S(1)}, f32[32,16]{1,0:T(8,128)S(1)}, u32[]{:S(2)}, u32[]{:S(2)}) collective-permute-start(f32[32,16]{1,0:T(8,128)S(1)} %add_add_fusion.1.corr_ref), channel_id=1, source_target_pairs={{4,0},{8,12},{5,1},{9,13},{6,2},{10,14},{7,3},{11,15},{20,16},{24,... | collective-permute-start | bytes 6152 | tf_op jit(solution)/shard_map/ppermute | solution.py:354
  46.5 14.6 %collective-permute-start.12 = (f32[16,256]{1,0:T(8,128)S(1)}, f32[16,256]{1,0:T(8,128)S(1)}, u32[]{:S(2)}, u32[]{:S(2)}) collective-permute-start(f32[16,256]{1,0:T(8,128)S(1)} %get-tuple-element.8), channel_id=1, source_target_pairs={{4,0},{8,12},{5,1},{9,13},{6,2},{10,14},{7,3},{11,15},{20,16},{24,... | collective-permute-start | bytes 49160 | tf_op jit(solution)/shard_map/ppermute | solution.py:372
  47.8 13.3 %collective-permute-start.14 = (f32[16,256]{1,0:T(8,128)S(1)}, f32[16,256]{1,0:T(8,128)S(1)}, u32[]{:S(2)}, u32[]{:S(2)}) collective-permute-start(f32[16,256]{1,0:T(8,128)S(1)} %get-tuple-element.9), channel_id=1, source_target_pairs={{4,8},{8,4},{5,9},{9,5},{6,10},{10,6},{7,11},{11,7},{20,24},{24,20... | collective-permute-start | bytes 49160 | tf_op jit(solution)/shard_map/ppermute | solution.py:374
  48.4 13.0 %collective-permute-start.13 = (f32[16,256]{1,0:T(8,128)S(1)}, f32[16,256]{1,0:T(8,128)S(1)}, u32[]{:S(2)}, u32[]{:S(2)}) collective-permute-start(f32[16,256]{1,0:T(8,128)S(1)} %get-tuple-element.10), channel_id=1, source_target_pairs={{4,12},{8,0},{5,13},{9,1},{6,14},{10,2},{7,15},{11,3},{20,28},{24,... | collective-permute-start | bytes 49160 | tf_op jit(solution)/shard_map/ppermute | solution.py:373

commit v2 on v0

--- a/solution.py
+++ b/solution.py
@@ -1,12 +1,17 @@
+import functools
 import math
 
 import jax
 import jax.numpy as jnp
+import numpy as np
 from jax import lax
+from jax.experimental import pallas as pl
+from jax.experimental.pallas import tpu as pltpu
 from jax.sharding import PartitionSpec as P
 
 step_length = 0.2
 reach = 14
+lanes = 128
 
 
 def padded_2(cells, sides, width):
@@ -52,7 +57,7 @@
     return result.reshape(orbs, planes, grid_p)
 
 
-def per_device(psi, potential, extent):
+def general_device(psi, potential, extent):
     orb_dev, planes, grid_p = psi.shape
     n_orb = lax.axis_size("orb")
     norbitals = orb_dev * n_orb
@@ -90,6 +95,407 @@
     return (psi_new, density)
 
 
+def weight(spread):
+    spread = np.abs(spread)
+    safe = np.maximum(spread, 1).astype(np.float64)
+    value = np.where(spread % 2 == 1, 2.0, -2.0) / (safe * safe)
+    value = np.where(spread == 0, -math.pi**2 / 3.0, value)
+    return np.where(spread <= reach, value, 0.0).astype(np.float32)
+
+
+def two_parts(value):
+    high = value.astype(jnp.bfloat16)
+    return high, (value - high.astype(np.float32)).astype(jnp.bfloat16)
+
+
+def column_band():
+    rows = np.arange(2 * lanes)[:, None]
+    cols = np.arange(lanes)[None, :]
+    high, low = two_parts(weight(rows - cols - reach))
+    return np.concatenate([high, low], axis=1)
+
+
+def plane_bands(planes):
+    rows = np.arange(planes)[:, None]
+    cols = np.arange(planes)[None, :]
+    both = []
+    for side in (-planes, planes):
+        band = np.concatenate(
+            [weight(cols + side - rows), weight(cols - rows), weight(cols - side - rows)], axis=1
+        )
+        high, low = two_parts(band)
+        both.append(np.concatenate([high, high, low], axis=1))
+    return np.stack(both)
+
+
+def in_vmem():
+    return pl.BlockSpec(memory_space=pltpu.VMEM)
+
+
+def in_smem():
+    return pl.BlockSpec(memory_space=pltpu.SMEM)
+
+
+def columns_of(shape):
+    return lax.broadcasted_iota(jnp.int32, shape, len(shape) - 1)
+
+
+def owner_of(place_ref, f):
+    z = place_ref[0]
+    if f < 2:
+        return z if f == 0 else jnp.where(z % 2 == 0, z + 1, z - 1)
+    left, right = (2, 1) if f == 2 else (3, 0)
+    return jnp.where(z < 2, left, right)
+
+
+def masked(field_ref, a, extent_ref, owner):
+    orbs, planes, grid_p = field_ref.shape
+    column = columns_of((planes, grid_p))
+    return jnp.where(column < extent_ref[owner * orbs + a], field_ref[a], 0.0)
+
+
+def split_into(parts_ref, field_ref, extent_ref, owner):
+    orbs, planes, _ = field_ref.shape
+    for a in range(orbs):
+        high, low = two_parts(masked(field_ref, a, extent_ref, owner))
+        parts_ref[a * planes : (a + 1) * planes, :] = high
+        parts_ref[(orbs + a) * planes : (orbs + a + 1) * planes, :] = low
+
+
+def split_kernel(f, field_ref, extent_ref, place_ref, parts_ref):
+    split_into(parts_ref, field_ref, extent_ref, owner_of(place_ref, f))
+
+
+def local_kernel(f, psi_ref, potential_ref, extent_ref, place_ref, band_ref, out_ref, parts_ref, phi_ref):
+    orbs, planes, grid_p = psi_ref.shape
+    tiles = grid_p // lanes
+    owner = owner_of(place_ref, f)
+    for a in range(orbs):
+        phi = masked(psi_ref, a, extent_ref, owner)
+        phi_ref[a * planes : (a + 1) * planes, :] = phi
+        high, low = two_parts(phi)
+        parts_ref[a * planes : (a + 1) * planes, :] = high
+        parts_ref[(orbs + a) * planes : (orbs + a + 1) * planes, :] = low
+    high, low = two_parts(pltpu.roll(phi_ref[...], reach, 1))
+    for t in range(tiles):
+        here, after = t * lanes, (t + 1) % tiles * lanes
+        high_t = jnp.concatenate([high[:, here : here + lanes], high[:, after : after + lanes]], 1)
+        low_t = jnp.concatenate([low[:, here : here + lanes], low[:, after : after + lanes]], 1)
+        both = jnp.dot(high_t, band_ref[...], preferred_element_type=jnp.float32)
+        rest = jnp.dot(low_t, band_ref[:, :lanes], preferred_element_type=jnp.float32)
+        second = both[:, :lanes] + both[:, lanes:] + rest
+        field = phi_ref[:, here : here + lanes].reshape(orbs, planes, lanes)
+        out_ref[:, :, here : here + lanes] = (
+            potential_ref[:, here : here + lanes][None] * field
+            - 0.5 * second.reshape(orbs, planes, lanes)
+        )
+
+
+def plane_kernel(
+    f, far_ref, psi_ref, near_ref, local_ref, extent_ref, place_ref, band_ref, out_ref, parts_ref
+):
+    orbs, planes, grid_p = psi_ref.shape
+    column = columns_of((planes, grid_p))
+    owner = owner_of(place_ref, f)
+    band = band_ref[place_ref[1]]
+    for a in range(orbs):
+        slab = jnp.concatenate([far_ref[a], psi_ref[a], near_ref[a]], axis=0)
+        high, low = two_parts(slab)
+        second = jnp.dot(
+            band, jnp.concatenate([high, low, high], axis=0), preferred_element_type=jnp.float32
+        )
+        image = jnp.where(
+            column < extent_ref[owner * orbs + a], local_ref[a] - 0.5 * second, 0.0
+        )
+        out_ref[a] = image
+        high, low = two_parts(image)
+        parts_ref[a * planes : (a + 1) * planes, :] = high
+        parts_ref[(orbs + a) * planes : (orbs + a + 1) * planes, :] = low
+
+
+def overlaps(field_ref, image_ref, planes):
+    half = field_ref.shape[0] // 2
+    product = lax.dot_general(
+        field_ref[...],
+        image_ref[...],
+        (((1,), (1,)), ((), ())),
+        preferred_element_type=jnp.float32,
+    )
+    product = product[:half] + product[half:]
+    product = product[:, :half] + product[:, half:]
+    row = lax.broadcasted_iota(jnp.int32, (half, half), 0)
+    col = lax.broadcasted_iota(jnp.int32, (half, half), 1)
+    product = jnp.where(row % planes == col % planes, product, 0.0)
+    return jnp.sum(product.reshape(half // planes, planes, half), axis=1)
+
+
+def overlap_kernel(planes, n_fields, *refs):
+    fields, image_ref, out_ref = refs[:n_fields], refs[n_fields], refs[n_fields + 1]
+    for f, field_ref in enumerate(fields):
+        value = overlaps(field_ref, image_ref, planes)
+        out_ref[f * value.shape[0] : (f + 1) * value.shape[0], :] = value
+
+
+def correlation_kernel(
+    planes, scale, own_ref, pair_ref, third_ref, fourth_ref, image_ref, ward_ref, early_ref, out_ref
+):
+    half = own_ref.shape[0] // 2
+    orbs = half // planes
+    ward = [overlaps(ref, ward_ref, planes) for ref in (own_ref, pair_ref, third_ref, fourth_ref)]
+    last = overlaps(fourth_ref, image_ref, planes)
+    wide = jnp.concatenate(
+        [jnp.concatenate([early_ref[...], last], axis=0), jnp.concatenate(ward, axis=0)], axis=1
+    )
+    row = lax.broadcasted_iota(jnp.int32, (2 * half, 2 * orbs), 0)
+    col = lax.broadcasted_iota(jnp.int32, (2 * half, 2 * orbs), 1)
+    gather = jnp.where(row // planes == col, scale, 0.0)
+    out_ref[...] = jnp.dot(
+        wide, gather, precision=lax.Precision.HIGHEST, preferred_element_type=jnp.float32
+    )
+
+
+def sum_kernel(*refs):
+    total = refs[0][...]
+    for ref in refs[1:-1]:
+        total = total + ref[...]
+    refs[-1][...] = total
+
+
+def spread_out(corr, planes):
+    n_a, n_b = corr.shape
+
+    def iota(shape, dim):
+        return lax.broadcasted_iota(jnp.int32, shape, dim)
+
+    take_b = (iota((n_b * planes, n_b), 0) // planes == iota((n_b * planes, n_b), 1)).astype(
+        jnp.float32
+    )
+    take_a = (iota((n_a, n_a * planes), 1) // planes == iota((n_a, n_a * planes), 0)).astype(
+        jnp.float32
+    )
+    rows = lax.dot_general(
+        take_b,
+        corr * step_length,
+        (((1,), (1,)), ((), ())),
+        precision=lax.Precision.HIGHEST,
+        preferred_element_type=jnp.float32,
+    )
+    full = jnp.dot(
+        rows, take_a, precision=lax.Precision.HIGHEST, preferred_element_type=jnp.float32
+    )
+    shape = (n_b * planes, n_a * planes)
+    full = jnp.where(iota(shape, 0) % planes == iota(shape, 1) % planes, full, 0.0)
+    return two_parts(full)
+
+
+def projections(high, low, fields, chunk):
+    half = fields[0].shape[0] // 2
+    total = None
+    for f, field_ref in enumerate(fields):
+        here = slice(f * half, (f + 1) * half)
+        left = jnp.concatenate(
+            [
+                jnp.concatenate([high[:, here], high[:, here]], axis=1),
+                jnp.concatenate([low[:, here], low[:, here]], axis=1),
+            ],
+            axis=0,
+        )
+        term = jnp.dot(left, field_ref[:, chunk], preferred_element_type=jnp.float32)
+        total = term if total is None else total + term
+    n = total.shape[0] // 2
+    return total[:n] + total[n:]
+
+
+def density_kernel(
+    own_ref, pair_ref, own_parts, pair_parts, third_parts, fourth_parts, image_ref, ward_ref,
+    corr_ref, extent_ref, place_ref, *refs,
+):
+    orbs, planes, grid_p = own_ref.shape
+    width = 2 * lanes
+    share = grid_p // 4
+    out_ref, all_ref = refs[:4], refs[4]
+    z = place_ref[0]
+    inner = (z == 1) | (z == 2)
+
+    @pl.when(inner)
+    def _():
+        high, low = spread_out(corr_ref[...], planes)
+        fields = (own_parts, pair_parts, third_parts, fourth_parts)
+        limits = [
+            [extent_ref[owner_of(place_ref, f) * orbs + a] for a in range(orbs)] for f in range(2)
+        ]
+        for c in range(grid_p // width):
+            chunk = slice(c * width, (c + 1) * width)
+            column = columns_of((planes, width)) + c * width
+            change = projections(high, low, fields, chunk)
+            density = jnp.zeros((planes, width), jnp.float32)
+            for f, (field_ref, half_ref) in enumerate(((own_ref, image_ref), (pair_ref, ward_ref))):
+                for a in range(orbs):
+                    at = (f * orbs + a) * planes
+                    phi = jnp.where(column < limits[f][a], field_ref[a, :, chunk], 0.0)
+                    value = phi - step_length * half_ref[a, :, chunk] + change[at : at + planes]
+                    density = density + value * value
+            all_ref[:, chunk] = density * (1.0 / (4 * orbs))
+        for k, part_ref in enumerate(out_ref):
+            first = pl.multiple_of(jnp.bitwise_xor(z, k) * share, share)
+            part_ref[...] = all_ref[:, pl.ds(first, share)]
+
+    @pl.when(jnp.logical_not(inner))
+    def _():
+        for part_ref in out_ref:
+            part_ref[...] = jnp.zeros_like(part_ref)
+
+
+def update_kernel(
+    own_ref, own_parts, pair_parts, third_in, third_out, fourth_in, fourth_out, image_ref,
+    corr_ref, given_ref, extent_ref, place_ref, out_ref, third_parts, fourth_parts,
+):
+    orbs, planes, grid_p = own_ref.shape
+    width = 2 * lanes
+    z = place_ref[0]
+    inner = (z == 1) | (z == 2)
+
+    @pl.when(jnp.logical_not(inner))
+    def _():
+        split_into(third_parts, third_out, extent_ref, owner_of(place_ref, 2))
+        split_into(fourth_parts, fourth_out, extent_ref, owner_of(place_ref, 3))
+
+    def write(corr, fields):
+        high, low = spread_out(corr, planes)
+        for c in range(grid_p // width):
+            chunk = slice(c * width, (c + 1) * width)
+            column = columns_of((planes, width)) + c * width
+            change = projections(high, low, fields, chunk)
+            for a in range(orbs):
+                phi = jnp.where(column < extent_ref[z * orbs + a], own_ref[a, :, chunk], 0.0)
+                out_ref[a, :, chunk] = (
+                    phi
+                    - step_length * image_ref[a, :, chunk]
+                    + change[a * planes : (a + 1) * planes]
+                )
+
+    @pl.when(inner)
+    def _():
+        write(corr_ref[:, :orbs], (own_parts, pair_parts, third_in, fourth_in))
+
+    @pl.when(jnp.logical_not(inner))
+    def _():
+        corr = given_ref[:, orbs:]
+        corr = jnp.concatenate([corr[orbs : 2 * orbs], corr[:orbs], corr[2 * orbs :]], axis=0)
+        write(corr, (own_parts, pair_parts, third_parts, fourth_parts))
+
+
+def call(kernel, out_shape, specs, scratch=()):
+    return pl.pallas_call(
+        kernel,
+        out_shape=out_shape,
+        in_specs=[in_smem() if spec == "s" else in_vmem() for spec in specs],
+        out_specs=jax.tree.map(lambda _: in_vmem(), out_shape),
+        scratch_shapes=list(scratch),
+        compiler_params=pltpu.CompilerParams(vmem_limit_bytes=10 * 2**20),
+        cost_estimate=pl.CostEstimate(flops=1, bytes_accessed=1, transcendentals=0),
+    )
+
+
+def line_device(psi, potential, extent):
+    orbs, planes, grid_p = psi.shape
+    n_cmp = lax.axis_size("cmp")
+    rows = orbs * planes
+    cells = planes * n_cmp * grid_p
+    z = lax.axis_index("orb")
+    place = jnp.stack([z, lax.axis_index("cmp") % 2])
+    swap = [(0, 1), (1, 0), (2, 3), (3, 2)]
+    across = [(1, 2), (2, 1)]
+    outward = [(1, 0), (2, 3)]
+    to_near = [(i, i ^ 1) for i in range(n_cmp)]
+    to_far = [(i, i ^ 3) for i in range(n_cmp)]
+
+    block = jax.ShapeDtypeStruct(psi.shape, jnp.float32)
+    parts = jax.ShapeDtypeStruct((2 * rows, grid_p), jnp.bfloat16)
+    field = pltpu.VMEM((rows, grid_p), jnp.float32)
+    columns = jnp.asarray(column_band())
+    bands = jnp.asarray(plane_bands(planes))
+
+    pair = lax.ppermute(psi, "orb", swap)
+    third = lax.ppermute(psi, "orb", across)
+    far = lax.ppermute(psi, "cmp", to_far)
+    near = lax.ppermute(psi, "cmp", to_near)
+
+    local, own_parts = call(functools.partial(local_kernel, 0), (block, parts), "vvssv", [field])(
+        psi, potential, extent, place, columns
+    )
+    pair, local, own_parts = lax.optimization_barrier((pair, local, own_parts))
+    pair_far = lax.ppermute(pair, "cmp", to_far)
+    pair_near = lax.ppermute(pair, "cmp", to_near)
+    fourth = lax.ppermute(pair, "orb", across)
+    third_out = lax.ppermute(third, "orb", outward)
+
+    image, image_parts = call(functools.partial(plane_kernel, 0), (block, parts), "vvvvssv")(
+        far, psi, near, local, extent, place, bands
+    )
+    ward_local, pair_parts = call(
+        functools.partial(local_kernel, 1), (block, parts), "vvssv", [field]
+    )(pair, potential, extent, place, columns)
+    third_parts = call(functools.partial(split_kernel, 2), parts, "vss")(third, extent, place)
+    early = call(
+        functools.partial(overlap_kernel, planes, 3),
+        jax.ShapeDtypeStruct((3 * orbs, rows), jnp.float32),
+        "vvvv",
+    )(own_parts, pair_parts, third_parts, image_parts)
+
+    fourth, ward_local, early = lax.optimization_barrier((fourth, ward_local, early))
+    ward, ward_parts = call(functools.partial(plane_kernel, 1), (block, parts), "vvvvssv")(
+        pair_far, pair, pair_near, ward_local, extent, place, bands
+    )
+    fourth_out = lax.ppermute(fourth, "orb", outward)
+    fourth_parts = call(functools.partial(split_kernel, 3), parts, "vss")(fourth, extent, place)
+    part = call(
+        functools.partial(correlation_kernel, planes, 1.0 / cells),
+        jax.ShapeDtypeStruct((4 * orbs, 2 * orbs), jnp.float32),
+        "vvvvvvv",
+    )(own_parts, pair_parts, third_parts, fourth_parts, image_parts, ward_parts, early)
+    shares = [lax.ppermute(part, "cmp", [(i, i ^ k) for i in range(n_cmp)]) for k in (1, 2, 3)]
+    correlation = call(sum_kernel, jax.ShapeDtypeStruct(part.shape, jnp.float32), "vvvv")(
+        part, *shares
+    )
+    correlation, third_out = lax.optimization_barrier((correlation, third_out))
+    given = lax.ppermute(correlation, "orb", outward)
+
+    share = jax.ShapeDtypeStruct((planes, grid_p // 4), jnp.float32)
+    pieces = call(
+        density_kernel, [share] * 4, "vvvvvvvvvss", [pltpu.VMEM((planes, grid_p), jnp.float32)]
+    )(
+        psi, pair, own_parts, pair_parts, third_parts, fourth_parts, image, ward, correlation,
+        extent, place,
+    )
+    sent = [
+        lax.ppermute(pieces[1], "orb", outward),
+        lax.ppermute(pieces[2], "orb", [(1, 3), (2, 0)]),
+        lax.ppermute(pieces[3], "orb", across),
+    ]
+
+    psi_new = call(
+        update_kernel, block, "vvvvvvvvvvss", [pltpu.VMEM(parts.shape, parts.dtype)] * 2
+    )(
+        psi, own_parts, pair_parts, third_parts, third_out, fourth_parts, fourth_out, image,
+        correlation, given, extent, place,
+    )
+    density = call(sum_kernel, share, "vvvv")(pieces[0], *sent)
+    return (psi_new, density)
+
+
+def per_device(psi, potential, extent):
+    orbs, planes, grid_p = psi.shape
+    fits = (
+        lax.axis_size("orb") == 4
+        and lax.axis_size("cmp") == 4
+        and orbs == 8
+        and planes == 16
+        and grid_p % (4 * lanes) == 0
+    )
+    return (line_device if fits else general_device)(psi, potential, extent)
+
+
 def solution(mesh):
     return jax.shard_map(
         per_device,

time: 167 us -> 57.2 us (0.34)
  blocking collectives: 70.6 us -> 0 us
  local copies, waits for them, and re-layouts: 29.9 us -> 3.74 us
  between operations: 14.2 us -> 0.87 us
  Pallas kernels: 0 us -> 11.3 us
  other arithmetic: 8.34 us -> 0.08 us
  starting transfers between devices: 11.8 us -> 17.4 us
  matrix products: 4.69 us -> 0 us
  waiting for transfers between devices: 26.8 us -> 23.5 us
    psum x1 -> x0, blocking collectives: 57.6 us -> none  [per_device(): correlation = lax.psum(partial_correlation, ('orb', 'cmp')) / cells]
    ppermute x2 -> x16, waiting for transfers between devices: 0.01 us -> 23.5 us  [the longest x1 5.28 us: line_device(): pair = lax.ppermute(psi, 'orb', swap)]
    reduce_scatter x1 -> x0, waiting for transfers between devices: 18.8 us -> none  [per_device(): lax.psum_scatter(jnp.sum(psi_new * psi_new, axis=0), 'orb', scatter_dimen...]
    unnamed x11 -> x16, local copies, waits for them, and re-layouts: 19.2 us -> 3.74 us
    ppermute x2 -> x16, starting transfers between devices: 2.38 us -> 17.4 us  [the longest x1 3.09 us: line_device(): pair = lax.ppermute(psi, 'orb', swap)]
    all_to_all x1 -> x0, blocking collectives: 12.9 us -> none  [per_device(): lax.all_to_all(grad_c, 'orb', split_axis=0, concat_axis=2, tiled=True)]
    pallas_call x0 -> x12, Pallas kernels: none -> 11.3 us  [the longest x1 2.88 us: line_device(): call(update_kernel, block, 'vvvvvvvvvvss', [pltpu.VMEM(parts.shape, parts...]
    all_to_all x2 -> x0, starting transfers between devices: 9.16 us -> none  [the longest x1 5.68 us: per_device(): lax.all_to_all(phi, 'orb', split_axis=2, concat_axis=0, tiled=True)]
  transfers between devices with their start and end apart: 5 -> 16, of which waited for: 3 -> 7; matrix products, arithmetic and copies ran while one was open for 17% -> 0% of each run, Pallas kernels for 0% -> 15%
where the time goes in v2:
time: 57.2 us; the launch traced here: 56.8 us
  waiting for transfers between devices  23.5 us (41%)
  starting transfers between devices  17.4 us (30%)
  Pallas kernels  11.3 us (20%)
  local copies, waits for them, and re-layouts  3.74 us (7%)
  between operations  0.87 us (2%)
    ppermute x1, waiting for transfers between devices, line_device(): pair = lax.ppermute(psi, 'orb', swap)  5.28 us
    ppermute x1, waiting for transfers between devices, line_device(): pair_far = lax.ppermute(pair, 'cmp', to_far)  4.92 us
    ppermute x1, waiting for transfers between devices, line_device(): lax.ppermute(pieces[1], 'orb', outward)  4.65 us
    unnamed x16, local copies, waits for them, and re-layouts  3.74 us
    ppermute x3, waiting for transfers between devices, line_device(): lax.ppermute(part, 'cmp', [(i, i ^ k) for i in range(n_cmp)])  3.36 us
    ppermute x1, waiting for transfers between devices, line_device(): given = lax.ppermute(correlation, 'orb', outward)  3.16 us
    ppermute x1, starting transfers between devices, line_device(): pair = lax.ppermute(psi, 'orb', swap)  3.09 us
    pallas_call x1, Pallas kernels, line_device(): call(update_kernel, block, 'vvvvvvvvvvss', [pltpu.VMEM(parts.shape, parts...  2.88 us
  transfers between devices with their start and end apart: 16, of which 7 were waited for; matrix products, arithmetic and copies ran while one was open for 0% of the time, Pallas kernels for 15%

profile of v2, /device:TPU:0, one launch (start us, length us, event | category | flops | bytes accessed | tf_op | source)
XLA Modules:
  0.0 56.8 jit_solution(18334572416669453023)
XLA Ops:
  0.6 3.1 %collective-permute-start = (f32[8,16,1024]{2,1,0:T(8,128)}, f32[8,16,1024]{2,1,0:T(8,128)S(1)}, u32[]{:S(2)}, u32[]{:S(2)}) collective-permute-start(f32[8,16,1024]{2,1,0:T(8,128)} %own_ref.3), channel_id=1, source_target_pairs={{0,4},{4,0},{8,12},{12,8},{1,5},{5,1},{9,13},{13,9},{2,6},{6,2},{1... | collective-permute-start | bytes 1572872 | tf_op jit(solution)/shard_map/ppermute | solution.py:419
  3.7 0.0 collective-permute-start.4
  3.7 1.6 %collective-permute-start.3 = (f32[8,16,1024]{2,1,0:T(8,128)}, f32[8,16,1024]{2,1,0:T(8,128)S(1)}, u32[]{:S(2)}, u32[]{:S(2)}) collective-permute-start(f32[8,16,1024]{2,1,0:T(8,128)} %own_ref.3), channel_id=1, source_target_pairs={{0,3},{1,2},{2,1},{3,0},{4,7},{5,6},{6,5},{7,4},{8,11},{9,10},{10,... | collective-permute-start | bytes 1572872 | tf_op jit(solution)/shard_map/ppermute | solution.py:421
  5.3 0.7 %collective-permute-start.1 = (f32[8,16,1024]{2,1,0:T(8,128)}, f32[8,16,1024]{2,1,0:T(8,128)S(1)}, u32[]{:S(2)}, u32[]{:S(2)}) collective-permute-start(f32[8,16,1024]{2,1,0:T(8,128)} %own_ref.3), channel_id=1, source_target_pairs={{4,8},{8,4},{5,9},{9,5},{6,10},{10,6},{7,11},{11,7},{20,24},{24,20... | collective-permute-start | bytes 1572872 | tf_op jit(solution)/shard_map/ppermute | solution.py:420
  6.0 0.0 copy-start.7
  6.0 0.1 pad_add_fusion.place_ref
  6.1 0.6 %copy-done.7 = s32[32]{0:T(128)S(1)} copy-done((s32[32]{0:T(128)S(1)}, s32[32]{0:T(128)}, u32[]{:S(2)}) %copy-start.7) | copy-done | bytes 152
  6.7 0.0 copy-start
  6.7 1.0 %copy-done = f32[8,16,1024]{2,1,0:T(8,128)S(1)} copy-done((f32[8,16,1024]{2,1,0:T(8,128)S(1)}, f32[8,16,1024]{2,1,0:T(8,128)}, u32[]{:S(2)}) %copy-start) | copy-done | bytes 524312
  7.7 0.0 copy-start.2
  7.7 0.9 %copy-done.2 = bf16[256,256]{1,0:T(8,128)(2,1)S(1)} copy-done((bf16[256,256]{1,0:T(8,128)(2,1)S(1)}, bf16[256,256]{1,0:T(8,128)(2,1)}, u32[]{:S(2)}) %copy-start.2) | copy-done | bytes 131096
  8.6 0.0 copy-start.4
  8.6 0.8 %copy-done.4 = f32[16,1024]{1,0:T(8,128)S(1)} copy-done((f32[16,1024]{1,0:T(8,128)S(1)}, f32[16,1024]{1,0:T(8,128)}, u32[]{:S(2)}) %copy-start.4) | copy-done | bytes 65560
  9.5 0.0 copy-start.3
  9.5 0.0 copy-start.5
  9.5 1.1 %shard_map.68 = (f32[8,16,1024]{2,1,0:T(8,128)S(1)}, bf16[256,1024]{1,0:T(8,128)(2,1)S(1)}) custom-call(f32[8,16,1024]{2,1,0:T(8,128)S(1)} %copy-done, f32[16,1024]{1,0:T(8,128)S(1)} %copy-done.4, s32[32]{0:T(128)S(1)} %copy-done.7, s32[2]{0:T(128)S(1)} %pad_add_fusion.place_ref, bf16[256,256]{1,0:T(8,128)(2,1)S(1)} %copy-done.2), custom_call_target="tpu_custom_call" | custom-call | flops 1 | bytes 1 | tf_op jit(solution)/shard_map/pallas_call | solution.py:424
  10.6 5.3 %collective-permute-done.psi_ref.pair_ref = f32[8,16,1024]{2,1,0:T(8,128)S(1)} collective-permute-done((f32[8,16,1024]{2,1,0:T(8,128)}, f32[8,16,1024]{2,1,0:T(8,128)S(1)}, u32[]{:S(2)}, u32[]{:S(2)}) %collective-permute-start) | collective-permute-done | bytes 524320 | tf_op jit(solution)/shard_map/ppermute | solution.py:419
  15.9 0.7 %collective-permute-start.2 = (f32[8,16,1024]{2,1,0:T(8,128)S(1)}, f32[8,16,1024]{2,1,0:T(8,128)S(1)}, u32[]{:S(2)}, u32[]{:S(2)}) collective-permute-start(f32[8,16,1024]{2,1,0:T(8,128)S(1)} %collective-permute-done.psi_ref.pair_ref), channel_id=1, source_target_pairs={{4,8},{8,4},{5,9},{9,5},{6,10},{10,6},{7,11},{11,7},{20,24},{24,20... | collective-permute-start | bytes 1572872 | tf_op jit(solution)/shard_map/ppermute | solution.py:430
  16.5 0.1 collective-permute-start.6
  16.6 0.0 collective-permute-done.4.near_ref
  16.6 1.8 %collective-permute-start.5 = (f32[8,16,1024]{2,1,0:T(8,128)S(1)}, f32[8,16,1024]{2,1,0:T(8,128)S(1)}, u32[]{:S(2)}, u32[]{:S(2)}) collective-permute-start(f32[8,16,1024]{2,1,0:T(8,128)S(1)} %collective-permute-done.psi_ref.pair_ref), channel_id=1, source_target_pairs={{0,3},{1,2},{2,1},{3,0},{4,7},{5,6},{6,5},{7,4},{8,11},{9,10},{10,... | collective-permute-start | bytes 1572872 | tf_op jit(solution)/shard_map/ppermute | solution.py:428
  18.4 0.0 collective-permute-done.1.field_ref
  18.4 1.3 %collective-permute-start.10 = (f32[8,16,1024]{2,1,0:T(8,128)S(1)}, f32[8,16,1024]{2,1,0:T(8,128)S(1)}, u32[]{:S(2)}, u32[]{:S(2)}) collective-permute-start(f32[8,16,1024]{2,1,0:T(8,128)S(1)} %collective-permute-done.1.field_ref), channel_id=1, source_target_pairs={{4,0},{8,12},{5,1},{9,13},{6,2},{10,14},{7,3},{11,15},{20,16},{24,... | collective-permute-start | bytes 1572872 | tf_op jit(solution)/shard_map/ppermute | solution.py:431
  19.7 0.0 copy-done.3
  19.7 0.0 copy-done.5
  19.7 1.1 %shard_map.69 = (f32[8,16,1024]{2,1,0:T(8,128)S(1)}, bf16[256,1024]{1,0:T(8,128)(2,1)S(1)}) custom-call(f32[8,16,1024]{2,1,0:T(8,128)S(1)} %collective-permute-done.psi_ref.pair_ref, f32[16,1024]{1,0:T(8,128)S(1)} %copy-done.5, s32[32]{0:T(128)S(1)} %copy-done.7, s32[2]{0:T(128)S(1)} %pad_add_fusion.place_ref, bf16[256,256]{1,0:T(8,128)(2,1)S(1)} %copy-done.3), custom_call_target="tpu_custom_call" | custom-call | flops 1 | bytes 1 | tf_op jit(solution)/shard_map/pallas_call | solution.py:436
  20.8 0.0 copy-start.1
  20.8 0.0 copy-start.6
  20.8 0.6 %shard_map.70.refs_2_.third_ref.third_in.third_parts = bf16[256,1024]{1,0:T(8,128)(2,1)S(1)} custom-call(f32[8,16,1024]{2,1,0:T(8,128)S(1)} %collective-permute-done.1.field_ref, s32[32]{0:T(128)S(1)} %copy-done.7, s32[2]{0:T(128)S(1)} %pad_add_fusion.place_ref), custom_call_target="tpu_custom_call" | custom-call | flops 1 | bytes 1 | tf_op jit(solution)/shard_map/pallas_call | solution.py:439
  21.5 0.0 collective-permute-done.3.far_ref
  21.5 0.4 copy-done.1
  21.9 0.0 copy-done.6
  21.9 1.0 %shard_map.71 = (f32[8,16,1024]{2,1,0:T(8,128)S(1)}, bf16[256,1024]{1,0:T(8,128)(2,1)S(1)}) custom-call(f32[8,16,1024]{2,1,0:T(8,128)S(1)} %collective-permute-done.3.far_ref, f32[8,16,1024]{2,1,0:T(8,128)S(1)} %copy-done.1, f32[8,16,1024]{2,1,0:T(8,128)S(1)} %collective-permute-done.4.near_ref, f32[8,16,1024]{2,1,0:T(8,128)S(1)} %get-tuple-element.28.local_ref, ...), custom_call_target="tpu_custom_call" | custom-call | flops 1 | bytes 1 | tf_op jit(solution)/shard_map/pallas_call | solution.py:433
  22.9 0.6 %shard_map.72.early_ref = f32[24,128]{1,0:T(8,128)S(1)} custom-call(bf16[256,1024]{1,0:T(8,128)(2,1)S(1)} %get-tuple-element.24.refs_0_.own_ref.own_parts, bf16[256,1024]{1,0:T(8,128)(2,1)S(1)} %get-tuple-element.26.refs_1_.pair_ref.pair_parts, bf16[256,1024]{1,0:T(8,128)(2,1)S(1)} %shard_map.70.refs_2_.third_ref.third_in.third_parts, ...), custom_call_target="tpu_custom_call" | custom-call | flops 1 | bytes 1 | tf_op jit(solution)/shard_map/pallas_call | solution.py:440
  23.5 0.0 collective-permute-done.2.field_ref
  23.5 1.3 %collective-permute-start.11 = (f32[8,16,1024]{2,1,0:T(8,128)S(1)}, f32[8,16,1024]{2,1,0:T(8,128)S(1)}, u32[]{:S(2)}, u32[]{:S(2)}) collective-permute-start(f32[8,16,1024]{2,1,0:T(8,128)S(1)} %collective-permute-done.2.field_ref), channel_id=1, source_target_pairs={{4,0},{8,12},{5,1},{9,13},{6,2},{10,14},{7,3},{11,15},{20,16},{24,... | collective-permute-start | bytes 1572872 | tf_op jit(solution)/shard_map/ppermute | solution.py:450
  24.8 0.6 %shard_map.73.fourth_ref.fourth_in.fourth_parts = bf16[256,1024]{1,0:T(8,128)(2,1)S(1)} custom-call(f32[8,16,1024]{2,1,0:T(8,128)S(1)} %collective-permute-done.2.field_ref, s32[32]{0:T(128)S(1)} %copy-done.7, s32[2]{0:T(128)S(1)} %pad_add_fusion.place_ref), custom_call_target="tpu_custom_call" | custom-call | flops 1 | bytes 1 | tf_op jit(solution)/shard_map/pallas_call | solution.py:451
  25.4 0.0 collective-permute-done.6.near_ref
  25.4 4.9 %collective-permute-done.5.far_ref = f32[8,16,1024]{2,1,0:T(8,128)S(1)} collective-permute-done((f32[8,16,1024]{2,1,0:T(8,128)S(1)}, f32[8,16,1024]{2,1,0:T(8,128)S(1)}, u32[]{:S(2)}, u32[]{:S(2)}) %collective-permute-start.5) | collective-permute-done | bytes 524320 | tf_op jit(solution)/shard_map/ppermute | solution.py:428
  30.4 1.0 %shard_map.74 = (f32[8,16,1024]{2,1,0:T(8,128)S(1)}, bf16[256,1024]{1,0:T(8,128)(2,1)S(1)}) custom-call(f32[8,16,1024]{2,1,0:T(8,128)S(1)} %collective-permute-done.5.far_ref, f32[8,16,1024]{2,1,0:T(8,128)S(1)} %collective-permute-done.psi_ref.pair_ref, f32[8,16,1024]{2,1,0:T(8,128)S(1)} %collective-permute-done.6.near_ref, ...), custom_call_target="tpu_custom_call" | custom-call | flops 1 | bytes 1 | tf_op jit(solution)/shard_map/pallas_call | solution.py:447
  31.4 1.1 %shard_map.75.refs_0_ = f32[32,16]{1,0:T(8,128)S(1)} custom-call(bf16[256,1024]{1,0:T(8,128)(2,1)S(1)} %get-tuple-element.24.refs_0_.own_ref.own_parts, bf16[256,1024]{1,0:T(8,128)(2,1)S(1)} %get-tuple-element.26.refs_1_.pair_ref.pair_parts, bf16[256,1024]{1,0:T(8,128)(2,1)S(1)} %shard_map.70.refs_2_.third_ref.third_in.third_parts, ...), custom_call_target="tpu_custom_call" | custom-call | flops 1 | bytes 1 | tf_op jit(solution)/shard_map/pallas_call | solution.py:452
  32.5 2.0 %collective-permute-start.9 = (f32[32,16]{1,0:T(8,128)S(1)}, f32[32,16]{1,0:T(8,128)S(1)}, u32[]{:S(2)}, u32[]{:S(2)}) collective-permute-start(f32[32,16]{1,0:T(8,128)S(1)} %shard_map.75.refs_0_), channel_id=1, source_target_pairs={{0,3},{1,2},{2,1},{3,0},{4,7},{5,6},{6,5},{7,4},{8,11},{9,10},{10,... | collective-permute-start | bytes 6152 | tf_op jit(solution)/shard_map/ppermute | solution.py:457
  34.5 0.4 collective-permute-start.8
  34.9 0.0 collective-permute-start.7
  34.9 1.1 %collective-permute-done.9.refs_3_ = f32[32,16]{1,0:T(8,128)S(1)} collective-permute-done((f32[32,16]{1,0:T(8,128)S(1)}, f32[32,16]{1,0:T(8,128)S(1)}, u32[]{:S(2)}, u32[]{:S(2)}) %collective-permute-start.9) | collective-permute-done | bytes 2080 | tf_op jit(solution)/shard_map/ppermute | solution.py:457
  35.9 2.3 %collective-permute-done.8.refs_2_ = f32[32,16]{1,0:T(8,128)S(1)} collective-permute-done((f32[32,16]{1,0:T(8,128)S(1)}, f32[32,16]{1,0:T(8,128)S(1)}, u32[]{:S(2)}, u32[]{:S(2)}) %collective-permute-start.8) | collective-permute-done | bytes 2080 | tf_op jit(solution)/shard_map/ppermute | solution.py:457
  38.2 0.0 collective-permute-done.7.refs_1_
  38.3 0.0 collective-permute-done.10.third_out
  38.3 0.6 shard_map.78
  38.8 1.3 %collective-permute-start.13 = (f32[16,256]{1,0:T(8,128)S(1)}, f32[16,256]{1,0:T(8,128)S(1)}, u32[]{:S(2)}, u32[]{:S(2)}) collective-permute-start(f32[16,256]{1,0:T(8,128)S(1)} %get-tuple-element.39), channel_id=1, source_target_pairs={{4,0},{8,12},{5,1},{9,13},{6,2},{10,14},{7,3},{11,15},{20,16},{24,... | collective-permute-start | bytes 49160 | tf_op jit(solution)/shard_map/ppermute | solution.py:472
  40.1 1.3 %collective-permute-start.14 = (f32[16,256]{1,0:T(8,128)S(1)}, f32[16,256]{1,0:T(8,128)S(1)}, u32[]{:S(2)}, u32[]{:S(2)}) collective-permute-start(f32[16,256]{1,0:T(8,128)S(1)} %get-tuple-element.40), channel_id=1, source_target_pairs={{4,12},{8,0},{5,13},{9,1},{6,14},{10,2},{7,15},{11,3},{20,28},{24,... | collective-permute-start | bytes 49160 | tf_op jit(solution)/shard_map/ppermute | solution.py:473
  41.4 0.7 %collective-permute-start.15 = (f32[16,256]{1,0:T(8,128)S(1)}, f32[16,256]{1,0:T(8,128)S(1)}, u32[]{:S(2)}, u32[]{:S(2)}) collective-permute-start(f32[16,256]{1,0:T(8,128)S(1)} %get-tuple-element.41), channel_id=1, source_target_pairs={{4,8},{8,4},{5,9},{9,5},{6,10},{10,6},{7,11},{11,7},{20,24},{24,20... | collective-permute-start | bytes 49160 | tf_op jit(solution)/shard_map/ppermute | solution.py:474
  42.1 1.3 %collective-permute-start.12 = (f32[32,16]{1,0:T(8,128)S(1)}, f32[32,16]{1,0:T(8,128)S(1)}, u32[]{:S(2)}, u32[]{:S(2)}) collective-permute-start(f32[32,16]{1,0:T(8,128)S(1)} %shard_map.76.corr_ref), channel_id=1, source_target_pairs={{4,0},{8,12},{5,1},{9,13},{6,2},{10,14},{7,3},{11,15},{20,16},{24,... | collective-permute-start | bytes 6152 | tf_op jit(solution)/shard_map/ppermute | solution.py:462
  43.4 4.7 %collective-permute-done.13.refs_1_ = f32[16,256]{1,0:T(8,128)S(1)} collective-permute-done((f32[16,256]{1,0:T(8,128)S(1)}, f32[16,256]{1,0:T(8,128)S(1)}, u32[]{:S(2)}, u32[]{:S(2)}) %collective-permute-start.13) | collective-permute-done | bytes 16416 | tf_op jit(solution)/shard_map/ppermute | solution.py:472
  48.1 2.1 %collective-permute-done.14.refs_2_ = f32[16,256]{1,0:T(8,128)S(1)} collective-permute-done((f32[16,256]{1,0:T(8,128)S(1)}, f32[16,256]{1,0:T(8,128)S(1)}, u32[]{:S(2)}, u32[]{:S(2)}) %collective-permute-start.14) | collective-permute-done | bytes 16416 | tf_op jit(solution)/shard_map/ppermute | solution.py:473
  50.1 0.0 collective-permute-done.15.refs_3_
  50.1 0.6 %shard_map.79 = f32[16,256]{1,0:T(8,128)} custom-call(f32[16,256]{1,0:T(8,128)S(1)} %get-tuple-element.38.refs_0_, f32[16,256]{1,0:T(8,128)S(1)} %collective-permute-done.13.refs_1_, f32[16,256]{1,0:T(8,128)S(1)} %collective-permute-done.14.refs_2_, f32[16,256]{1,0:T(8,128)S(1)} %collective-permute-done.15.refs_3_), custom_call_target="tpu_custom_call" | custom-call | flops 1 | bytes 1 | tf_op jit(solution)/shard_map/pallas_call | solution.py:483
  50.8 3.2 %collective-permute-done.12.given_ref = f32[32,16]{1,0:T(8,128)S(1)} collective-permute-done((f32[32,16]{1,0:T(8,128)S(1)}, f32[32,16]{1,0:T(8,128)S(1)}, u32[]{:S(2)}, u32[]{:S(2)}) %collective-permute-start.12) | collective-permute-done | bytes 2080 | tf_op jit(solution)/shard_map/ppermute | solution.py:462
  53.9 0.0 collective-permute-done.11.fourth_out
  53.9 2.9 %shard_map.77 = f32[8,16,1024]{2,1,0:T(8,128)} custom-call(f32[8,16,1024]{2,1,0:T(8,128)S(1)} %copy-done.1, bf16[256,1024]{1,0:T(8,128)(2,1)S(1)} %get-tuple-element.24.refs_0_.own_ref.own_parts, bf16[256,1024]{1,0:T(8,128)(2,1)S(1)} %get-tuple-element.26.refs_1_.pair_ref.pair_parts, bf16[256,1024]{1,0:T(8,128)(2,1)S(1)} %shard_map.70.refs_2_.third_ref.third_in.third_parts, ...), custom_call_target="tpu_custom_call" | custom-call | flops 1 | bytes 1 | tf_op jit(solution)/shard_map/pallas_call | solution.py:477
  (1 shorter events, 0.0 us)
Async XLA Ops:
  0.6 15.2 %collective-permute-start = (f32[8,16,1024]{2,1,0:T(8,128)}, f32[8,16,1024]{2,1,0:T(8,128)S(1)}, u32[]{:S(2)}, u32[]{:S(2)}) collective-permute-start(f32[8,16,1024]{2,1,0:T(8,128)} %own_ref.3), channel_id=1, source_target_pairs={{0,4},{4,0},{8,12},{12,8},{1,5},{5,1},{9,13},{13,9},{2,6},{6,2},{1... | collective-permute-start | bytes 1572872 | tf_op jit(solution)/shard_map/ppermute | solution.py:419
  3.7 12.9 %collective-permute-start.4 = (f32[8,16,1024]{2,1,0:T(8,128)}, f32[8,16,1024]{2,1,0:T(8,128)S(1)}, u32[]{:S(2)}, u32[]{:S(2)}) collective-permute-start(f32[8,16,1024]{2,1,0:T(8,128)} %own_ref.3), channel_id=1, source_target_pairs={{0,1},{1,0},{2,3},{3,2},{4,5},{5,4},{6,7},{7,6},{8,9},{9,8},{10,11... | collective-permute-start | bytes 1572872 | tf_op jit(solution)/shard_map/ppermute | solution.py:422
  3.7 17.8 %collective-permute-start.3 = (f32[8,16,1024]{2,1,0:T(8,128)}, f32[8,16,1024]{2,1,0:T(8,128)S(1)}, u32[]{:S(2)}, u32[]{:S(2)}) collective-permute-start(f32[8,16,1024]{2,1,0:T(8,128)} %own_ref.3), channel_id=1, source_target_pairs={{0,3},{1,2},{2,1},{3,0},{4,7},{5,6},{6,5},{7,4},{8,11},{9,10},{10,... | collective-permute-start | bytes 1572872 | tf_op jit(solution)/shard_map/ppermute | solution.py:421
  5.3 13.1 %collective-permute-start.1 = (f32[8,16,1024]{2,1,0:T(8,128)}, f32[8,16,1024]{2,1,0:T(8,128)S(1)}, u32[]{:S(2)}, u32[]{:S(2)}) collective-permute-start(f32[8,16,1024]{2,1,0:T(8,128)} %own_ref.3), channel_id=1, source_target_pairs={{4,8},{8,4},{5,9},{9,5},{6,10},{10,6},{7,11},{11,7},{20,24},{24,20... | collective-permute-start | bytes 1572872 | tf_op jit(solution)/shard_map/ppermute | solution.py:420
  6.0 0.7 %copy-start.7 = (s32[32]{0:T(128)S(1)}, s32[32]{0:T(128)}, u32[]{:S(2)}) copy-start(s32[32]{0:T(128)} %extent_ref.15) | copy-start | bytes 388
  6.7 1.0 %copy-start = (f32[8,16,1024]{2,1,0:T(8,128)S(1)}, f32[8,16,1024]{2,1,0:T(8,128)}, u32[]{:S(2)}) copy-start(f32[8,16,1024]{2,1,0:T(8,128)} %own_ref.3) | copy-start | bytes 1572868
  7.7 0.9 %copy-start.2 = (bf16[256,256]{1,0:T(8,128)(2,1)S(1)}, bf16[256,256]{1,0:T(8,128)(2,1)}, u32[]{:S(2)}) copy-start(bf16[256,256]{1,0:T(8,128)(2,1)} %constant.24.clone.band_ref) | copy-start | bytes 393220
  8.6 0.8 %copy-start.4 = (f32[16,1024]{1,0:T(8,128)S(1)}, f32[16,1024]{1,0:T(8,128)}, u32[]{:S(2)}) copy-start(f32[16,1024]{1,0:T(8,128)} %potential_ref.3) | copy-start | bytes 196612
  9.5 10.2 %copy-start.3 = (bf16[256,256]{1,0:T(8,128)(2,1)S(1)}, bf16[256,256]{1,0:T(8,128)(2,1)}, u32[]{:S(2)}) copy-start(bf16[256,256]{1,0:T(8,128)(2,1)} %constant.24.clone.band_ref) | copy-start | bytes 393220
  9.5 10.2 %copy-start.5 = (f32[16,1024]{1,0:T(8,128)S(1)}, f32[16,1024]{1,0:T(8,128)}, u32[]{:S(2)}) copy-start(f32[16,1024]{1,0:T(8,128)} %potential_ref.3) | copy-start | bytes 196612
  15.9 7.6 %collective-permute-start.2 = (f32[8,16,1024]{2,1,0:T(8,128)S(1)}, f32[8,16,1024]{2,1,0:T(8,128)S(1)}, u32[]{:S(2)}, u32[]{:S(2)}) collective-permute-start(f32[8,16,1024]{2,1,0:T(8,128)S(1)} %collective-permute-done.psi_ref.pair_ref), channel_id=1, source_target_pairs={{4,8},{8,4},{5,9},{9,5},{6,10},{10,6},{7,11},{11,7},{20,24},{24,20... | collective-permute-start | bytes 1572872 | tf_op jit(solution)/shard_map/ppermute | solution.py:430
  16.5 8.9 %collective-permute-start.6 = (f32[8,16,1024]{2,1,0:T(8,128)S(1)}, f32[8,16,1024]{2,1,0:T(8,128)S(1)}, u32[]{:S(2)}, u32[]{:S(2)}) collective-permute-start(f32[8,16,1024]{2,1,0:T(8,128)S(1)} %collective-permute-done.psi_ref.pair_ref), channel_id=1, source_target_pairs={{0,1},{1,0},{2,3},{3,2},{4,5},{5,4},{6,7},{7,6},{8,9},{9,8},{10,11... | collective-permute-start | bytes 1572872 | tf_op jit(solution)/shard_map/ppermute | solution.py:429
  16.6 13.7 %collective-permute-start.5 = (f32[8,16,1024]{2,1,0:T(8,128)S(1)}, f32[8,16,1024]{2,1,0:T(8,128)S(1)}, u32[]{:S(2)}, u32[]{:S(2)}) collective-permute-start(f32[8,16,1024]{2,1,0:T(8,128)S(1)} %collective-permute-done.psi_ref.pair_ref), channel_id=1, source_target_pairs={{0,3},{1,2},{2,1},{3,0},{4,7},{5,6},{6,5},{7,4},{8,11},{9,10},{10,... | collective-permute-start | bytes 1572872 | tf_op jit(solution)/shard_map/ppermute | solution.py:428
  18.4 19.9 %collective-permute-start.10 = (f32[8,16,1024]{2,1,0:T(8,128)S(1)}, f32[8,16,1024]{2,1,0:T(8,128)S(1)}, u32[]{:S(2)}, u32[]{:S(2)}) collective-permute-start(f32[8,16,1024]{2,1,0:T(8,128)S(1)} %collective-permute-done.1.field_ref), channel_id=1, source_target_pairs={{4,0},{8,12},{5,1},{9,13},{6,2},{10,14},{7,3},{11,15},{20,16},{24,... | collective-permute-start | bytes 1572872 | tf_op jit(solution)/shard_map/ppermute | solution.py:431
  20.8 1.0 %copy-start.1 = (f32[8,16,1024]{2,1,0:T(8,128)S(1)}, f32[8,16,1024]{2,1,0:T(8,128)}, u32[]{:S(2)}) copy-start(f32[8,16,1024]{2,1,0:T(8,128)} %own_ref.3) | copy-start | bytes 1572868
  20.8 1.0 %copy-start.6 = (bf16[2,16,144]{2,1,0:T(8,128)(2,1)S(1)}, bf16[2,16,144]{2,1,0:T(8,128)(2,1)}, u32[]{:S(2)}) copy-start(bf16[2,16,144]{2,1,0:T(8,128)(2,1)} %constant.25.clone.band_ref) | copy-start | bytes 27652
  23.5 30.4 %collective-permute-start.11 = (f32[8,16,1024]{2,1,0:T(8,128)S(1)}, f32[8,16,1024]{2,1,0:T(8,128)S(1)}, u32[]{:S(2)}, u32[]{:S(2)}) collective-permute-start(f32[8,16,1024]{2,1,0:T(8,128)S(1)} %collective-permute-done.2.field_ref), channel_id=1, source_target_pairs={{4,0},{8,12},{5,1},{9,13},{6,2},{10,14},{7,3},{11,15},{20,16},{24,... | collective-permute-start | bytes 1572872 | tf_op jit(solution)/shard_map/ppermute | solution.py:450
  32.5 3.4 %collective-permute-start.9 = (f32[32,16]{1,0:T(8,128)S(1)}, f32[32,16]{1,0:T(8,128)S(1)}, u32[]{:S(2)}, u32[]{:S(2)}) collective-permute-start(f32[32,16]{1,0:T(8,128)S(1)} %shard_map.75.refs_0_), channel_id=1, source_target_pairs={{0,3},{1,2},{2,1},{3,0},{4,7},{5,6},{6,5},{7,4},{8,11},{9,10},{10,... | collective-permute-start | bytes 6152 | tf_op jit(solution)/shard_map/ppermute | solution.py:457
  34.5 3.7 %collective-permute-start.8 = (f32[32,16]{1,0:T(8,128)S(1)}, f32[32,16]{1,0:T(8,128)S(1)}, u32[]{:S(2)}, u32[]{:S(2)}) collective-permute-start(f32[32,16]{1,0:T(8,128)S(1)} %shard_map.75.refs_0_), channel_id=1, source_target_pairs={{0,2},{1,3},{2,0},{3,1},{4,6},{5,7},{6,4},{7,5},{8,10},{9,11},{10,... | collective-permute-start | bytes 6152 | tf_op jit(solution)/shard_map/ppermute | solution.py:457
  34.9 3.4 %collective-permute-start.7 = (f32[32,16]{1,0:T(8,128)S(1)}, f32[32,16]{1,0:T(8,128)S(1)}, u32[]{:S(2)}, u32[]{:S(2)}) collective-permute-start(f32[32,16]{1,0:T(8,128)S(1)} %shard_map.75.refs_0_), channel_id=1, source_target_pairs={{0,1},{1,0},{2,3},{3,2},{4,5},{5,4},{6,7},{7,6},{8,9},{9,8},{10,11... | collective-permute-start | bytes 6152 | tf_op jit(solution)/shard_map/ppermute | solution.py:457
  38.8 9.2 %collective-permute-start.13 = (f32[16,256]{1,0:T(8,128)S(1)}, f32[16,256]{1,0:T(8,128)S(1)}, u32[]{:S(2)}, u32[]{:S(2)}) collective-permute-start(f32[16,256]{1,0:T(8,128)S(1)} %get-tuple-element.39), channel_id=1, source_target_pairs={{4,0},{8,12},{5,1},{9,13},{6,2},{10,14},{7,3},{11,15},{20,16},{24,... | collective-permute-start | bytes 49160 | tf_op jit(solution)/shard_map/ppermute | solution.py:472
  40.1 10.0 %collective-permute-start.14 = (f32[16,256]{1,0:T(8,128)S(1)}, f32[16,256]{1,0:T(8,128)S(1)}, u32[]{:S(2)}, u32[]{:S(2)}) collective-permute-start(f32[16,256]{1,0:T(8,128)S(1)} %get-tuple-element.40), channel_id=1, source_target_pairs={{4,12},{8,0},{5,13},{9,1},{6,14},{10,2},{7,15},{11,3},{20,28},{24,... | collective-permute-start | bytes 49160 | tf_op jit(solution)/shard_map/ppermute | solution.py:473
  41.4 8.7 %collective-permute-start.15 = (f32[16,256]{1,0:T(8,128)S(1)}, f32[16,256]{1,0:T(8,128)S(1)}, u32[]{:S(2)}, u32[]{:S(2)}) collective-permute-start(f32[16,256]{1,0:T(8,128)S(1)} %get-tuple-element.41), channel_id=1, source_target_pairs={{4,8},{8,4},{5,9},{9,5},{6,10},{10,6},{7,11},{11,7},{20,24},{24,20... | collective-permute-start | bytes 49160 | tf_op jit(solution)/shard_map/ppermute | solution.py:474
  42.1 11.8 %collective-permute-start.12 = (f32[32,16]{1,0:T(8,128)S(1)}, f32[32,16]{1,0:T(8,128)S(1)}, u32[]{:S(2)}, u32[]{:S(2)}) collective-permute-start(f32[32,16]{1,0:T(8,128)S(1)} %shard_map.76.corr_ref), channel_id=1, source_target_pairs={{4,0},{8,12},{5,1},{9,13},{6,2},{10,14},{7,3},{11,15},{20,16},{24,... | collective-permute-start | bytes 6152 | tf_op jit(solution)/shard_map/ppermute | solution.py:462

commit v3 on v2

--- a/solution.py
+++ b/solution.py
@@ -128,20 +128,12 @@
     return np.stack(both)
 
 
-def in_vmem():
-    return pl.BlockSpec(memory_space=pltpu.VMEM)
-
-
-def in_smem():
-    return pl.BlockSpec(memory_space=pltpu.SMEM)
-
-
 def columns_of(shape):
     return lax.broadcasted_iota(jnp.int32, shape, len(shape) - 1)
 
 
 def owner_of(place_ref, f):
-    z = place_ref[0]
+    z = place_ref[0, 0]
     if f < 2:
         return z if f == 0 else jnp.where(z % 2 == 0, z + 1, z - 1)
     left, right = (2, 1) if f == 2 else (3, 0)
@@ -197,7 +189,7 @@
     orbs, planes, grid_p = psi_ref.shape
     column = columns_of((planes, grid_p))
     owner = owner_of(place_ref, f)
-    band = band_ref[place_ref[1]]
+    band = band_ref[place_ref[0, 1]]
     for a in range(orbs):
         slab = jnp.concatenate([far_ref[a], psi_ref[a], near_ref[a]], axis=0)
         high, low = two_parts(slab)
@@ -255,70 +247,74 @@
 
 
 def sum_kernel(*refs):
+    rows = refs[-1].shape[0]
     total = refs[0][...]
     for ref in refs[1:-1]:
-        total = total + ref[...]
+        total = total + ref[:rows, :]
     refs[-1][...] = total
 
 
 def spread_out(corr, planes):
     n_a, n_b = corr.shape
+    shift = planes.bit_length() - 1
+    shape = (n_b * planes, n_a * planes)
 
     def iota(shape, dim):
         return lax.broadcasted_iota(jnp.int32, shape, dim)
 
-    take_b = (iota((n_b * planes, n_b), 0) // planes == iota((n_b * planes, n_b), 1)).astype(
-        jnp.float32
-    )
-    take_a = (iota((n_a, n_a * planes), 1) // planes == iota((n_a, n_a * planes), 0)).astype(
-        jnp.float32
-    )
-    rows = lax.dot_general(
-        take_b,
-        corr * step_length,
-        (((1,), (1,)), ((), ())),
-        precision=lax.Precision.HIGHEST,
-        preferred_element_type=jnp.float32,
-    )
-    full = jnp.dot(
-        rows, take_a, precision=lax.Precision.HIGHEST, preferred_element_type=jnp.float32
-    )
-    shape = (n_b * planes, n_a * planes)
-    full = jnp.where(iota(shape, 0) % planes == iota(shape, 1) % planes, full, 0.0)
-    return two_parts(full)
+    def ones_where(mask):
+        return jnp.where(mask, 1.0, 0.0).astype(jnp.bfloat16)
+
+    take_b = ones_where(
+        jnp.right_shift(iota((shape[0], n_b), 0), shift) == iota((shape[0], n_b), 1)
+    )
+    take_a = ones_where(
+        jnp.right_shift(iota((n_a, shape[1]), 1), shift) == iota((n_a, shape[1]), 0)
+    )
+    same_plane = (jnp.bitwise_xor(iota(shape, 0), iota(shape, 1)) & (planes - 1)) == 0
+
+    def spread(part):
+        rows = lax.dot_general(
+            take_b, part, (((1,), (1,)), ((), ())), preferred_element_type=jnp.float32
+        ).astype(jnp.bfloat16)
+        full = jnp.dot(rows, take_a, preferred_element_type=jnp.float32)
+        return jnp.where(same_plane, full, 0.0).astype(jnp.bfloat16)
+
+    high, low = two_parts(corr * step_length)
+    return spread(high), spread(low)
 
 
 def projections(high, low, fields, chunk):
     half = fields[0].shape[0] // 2
     total = None
-    for f, field_ref in enumerate(fields):
-        here = slice(f * half, (f + 1) * half)
-        left = jnp.concatenate(
-            [
-                jnp.concatenate([high[:, here], high[:, here]], axis=1),
-                jnp.concatenate([low[:, here], low[:, here]], axis=1),
-            ],
-            axis=0,
-        )
-        term = jnp.dot(left, field_ref[:, chunk], preferred_element_type=jnp.float32)
-        total = term if total is None else total + term
-    n = total.shape[0] // 2
-    return total[:n] + total[n:]
-
-
-def density_kernel(
+    for f in range(0, len(fields), 2):
+        pair = fields[f : f + 2]
+        terms = [
+            (low[:, f * half : (f + 2) * half], jnp.concatenate([r[:half, chunk] for r in pair], 0))
+        ]
+        for g, field_ref in enumerate(pair):
+            here = high[:, (f + g) * half : (f + g + 1) * half]
+            terms.append((jnp.concatenate([here, here], axis=1), field_ref[:, chunk]))
+        for left, right in terms:
+            term = jnp.dot(left, right, preferred_element_type=jnp.float32)
+            total = term if total is None else total + term
+    return total
+
+
+def step_kernel(
     own_ref, pair_ref, own_parts, pair_parts, third_parts, fourth_parts, image_ref, ward_ref,
-    corr_ref, extent_ref, place_ref, *refs,
+    corr_ref, extent_ref, place_ref, kept_ref, out1_ref, out2_ref, out3_ref, new_ref, all_ref,
+    own_new, sem,
 ):
     orbs, planes, grid_p = own_ref.shape
     width = 2 * lanes
     share = grid_p // 4
-    out_ref, all_ref = refs[:4], refs[4]
-    z = place_ref[0]
+    z = place_ref[0, 0]
     inner = (z == 1) | (z == 2)
 
     @pl.when(inner)
     def _():
+        out1_ref[planes:, : corr_ref.shape[1]] = corr_ref[...]
         high, low = spread_out(corr_ref[...], planes)
         fields = (own_parts, pair_parts, third_parts, fourth_parts)
         limits = [
@@ -335,63 +331,67 @@
                     phi = jnp.where(column < limits[f][a], field_ref[a, :, chunk], 0.0)
                     value = phi - step_length * half_ref[a, :, chunk] + change[at : at + planes]
                     density = density + value * value
+                    if f == 0:
+                        own_new[a, :, chunk] = value
             all_ref[:, chunk] = density * (1.0 / (4 * orbs))
-        for k, part_ref in enumerate(out_ref):
+        copy = pltpu.make_async_copy(own_new, new_ref, sem)
+        copy.start()
+        for k, part_ref in enumerate((kept_ref, out1_ref, out2_ref, out3_ref)):
             first = pl.multiple_of(jnp.bitwise_xor(z, k) * share, share)
-            part_ref[...] = all_ref[:, pl.ds(first, share)]
+            part_ref[:planes, :] = all_ref[:, pl.ds(first, share)]
+        copy.wait()
 
     @pl.when(jnp.logical_not(inner))
     def _():
-        for part_ref in out_ref:
-            part_ref[...] = jnp.zeros_like(part_ref)
-
-
-def update_kernel(
-    own_ref, own_parts, pair_parts, third_in, third_out, fourth_in, fourth_out, image_ref,
-    corr_ref, given_ref, extent_ref, place_ref, out_ref, third_parts, fourth_parts,
+        kept_ref[...] = jnp.zeros_like(kept_ref)
+
+
+def outer_kernel(
+    own_ref, own_parts, pair_parts, third_ref, fourth_ref, image_ref, given_ref, extent_ref,
+    place_ref, old_ref, new_ref, third_parts, fourth_parts, own_new, sem,
 ):
     orbs, planes, grid_p = own_ref.shape
     width = 2 * lanes
-    z = place_ref[0]
-    inner = (z == 1) | (z == 2)
-
-    @pl.when(jnp.logical_not(inner))
+    z = place_ref[0, 0]
+    outer = (z == 0) | (z == 3)
+    del old_ref
+
+    @pl.when(outer)
     def _():
-        split_into(third_parts, third_out, extent_ref, owner_of(place_ref, 2))
-        split_into(fourth_parts, fourth_out, extent_ref, owner_of(place_ref, 3))
-
-    def write(corr, fields):
+        split_into(third_parts, third_ref, extent_ref, owner_of(place_ref, 2))
+        split_into(fourth_parts, fourth_ref, extent_ref, owner_of(place_ref, 3))
+        corr = given_ref[planes:, orbs : 2 * orbs]
+        corr = jnp.concatenate([corr[orbs : 2 * orbs], corr[:orbs], corr[2 * orbs :]], axis=0)
         high, low = spread_out(corr, planes)
+        fields = (own_parts, pair_parts, third_parts, fourth_parts)
         for c in range(grid_p // width):
             chunk = slice(c * width, (c + 1) * width)
             column = columns_of((planes, width)) + c * width
             change = projections(high, low, fields, chunk)
             for a in range(orbs):
                 phi = jnp.where(column < extent_ref[z * orbs + a], own_ref[a, :, chunk], 0.0)
-                out_ref[a, :, chunk] = (
+                own_new[a, :, chunk] = (
                     phi
                     - step_length * image_ref[a, :, chunk]
                     + change[a * planes : (a + 1) * planes]
                 )
-
-    @pl.when(inner)
-    def _():
-        write(corr_ref[:, :orbs], (own_parts, pair_parts, third_in, fourth_in))
-
-    @pl.when(jnp.logical_not(inner))
-    def _():
-        corr = given_ref[:, orbs:]
-        corr = jnp.concatenate([corr[orbs : 2 * orbs], corr[:orbs], corr[2 * orbs :]], axis=0)
-        write(corr, (own_parts, pair_parts, third_parts, fourth_parts))
-
-
-def call(kernel, out_shape, specs, scratch=()):
+        copy = pltpu.make_async_copy(own_new, new_ref, sem)
+        copy.start()
+        copy.wait()
+
+
+def call(kernel, out_shape, specs, scratch=(), out_specs=None, aliases={}):
+    kinds = {"s": pltpu.SMEM, "v": pltpu.VMEM, "a": pl.ANY}
+    if out_specs is None:
+        out_specs = "v" * len(jax.tree.leaves(out_shape))
+    places = [pl.BlockSpec(memory_space=kinds[kind]) for kind in out_specs]
     return pl.pallas_call(
         kernel,
         out_shape=out_shape,
-        in_specs=[in_smem() if spec == "s" else in_vmem() for spec in specs],
-        out_specs=jax.tree.map(lambda _: in_vmem(), out_shape),
+        in_specs=[pl.BlockSpec(memory_space=kinds[kind]) for kind in specs],
+        out_specs=places if isinstance(out_shape, (tuple, list)) else places[0],
         scratch_shapes=list(scratch),
+        input_output_aliases=aliases,
         compiler_params=pltpu.CompilerParams(vmem_limit_bytes=10 * 2**20),
         cost_estimate=pl.CostEstimate(flops=1, bytes_accessed=1, transcendentals=0),
     )
@@ -403,7 +403,7 @@
     rows = orbs * planes
     cells = planes * n_cmp * grid_p
     z = lax.axis_index("orb")
-    place = jnp.stack([z, lax.axis_index("cmp") % 2])
+    place = jnp.stack([z, lax.axis_index("cmp") % 2]).reshape(1, 2)
     swap = [(0, 1), (1, 0), (2, 3), (3, 2)]
     across = [(1, 2), (2, 1)]
     outward = [(1, 0), (2, 3)]
@@ -418,8 +418,10 @@
 
     pair = lax.ppermute(psi, "orb", swap)
     third = lax.ppermute(psi, "orb", across)
-    far = lax.ppermute(psi, "cmp", to_far)
-    near = lax.ppermute(psi, "cmp", to_near)
+    place = call(sum_kernel, jax.ShapeDtypeStruct(place.shape, place.dtype), "v")(place)
+    slab, place = lax.optimization_barrier((psi, place))
+    near = lax.ppermute(slab, "cmp", to_near)
+    far = lax.ppermute(slab, "cmp", to_far)
 
     local, own_parts = call(functools.partial(local_kernel, 0), (block, parts), "vvssv", [field])(
         psi, potential, extent, place, columns
@@ -459,29 +461,42 @@
         part, *shares
     )
     correlation, third_out = lax.optimization_barrier((correlation, third_out))
-    given = lax.ppermute(correlation, "orb", outward)
 
     share = jax.ShapeDtypeStruct((planes, grid_p // 4), jnp.float32)
-    pieces = call(
-        density_kernel, [share] * 4, "vvvvvvvvvss", [pltpu.VMEM((planes, grid_p), jnp.float32)]
+    wide = jax.ShapeDtypeStruct((planes + 4 * orbs, grid_p // 4), jnp.float32)
+    *pieces, new = call(
+        step_kernel,
+        [share, wide, share, share, block],
+        "vvvvvvvvvss",
+        [
+            pltpu.VMEM((planes, grid_p), jnp.float32),
+            pltpu.VMEM(block.shape, jnp.float32),
+            pltpu.SemaphoreType.DMA,
+        ],
+        "vvvva",
     )(
         psi, pair, own_parts, pair_parts, third_parts, fourth_parts, image, ward, correlation,
         extent, place,
     )
+    given = lax.ppermute(pieces[1], "orb", outward)
     sent = [
-        lax.ppermute(pieces[1], "orb", outward),
         lax.ppermute(pieces[2], "orb", [(1, 3), (2, 0)]),
         lax.ppermute(pieces[3], "orb", across),
     ]
-
-    psi_new = call(
-        update_kernel, block, "vvvvvvvvvvss", [pltpu.VMEM(parts.shape, parts.dtype)] * 2
+    new = call(
+        outer_kernel,
+        block,
+        "vvvvvvvssa",
+        [pltpu.VMEM(parts.shape, parts.dtype)] * 2
+        + [pltpu.VMEM(block.shape, jnp.float32), pltpu.SemaphoreType.DMA],
+        "a",
+        {9: 0},
     )(
-        psi, own_parts, pair_parts, third_parts, third_out, fourth_parts, fourth_out, image,
-        correlation, given, extent, place,
-    )
-    density = call(sum_kernel, share, "vvvv")(pieces[0], *sent)
-    return (psi_new, density)
+        psi, own_parts, pair_parts, third_out, fourth_out, image, given, extent, place, new
+    )
+    sent, kept = lax.optimization_barrier((sent, pieces[0], new))[:2]
+    density = call(sum_kernel, share, "vvvv")(kept, *sent, given)
+    return (new, density)
 
 
 def per_device(psi, potential, extent):

time: 57.2 us -> 52 us (0.909)
  waiting for transfers between devices: 23.5 us -> 20.5 us
  starting transfers between devices: 17.4 us -> 16.2 us
    ppermute x1, waiting for transfers between devices: 2.08 us -> 0.01 us  [line_device(): lax.ppermute(pieces[2], 'orb', [(1, 3), (2, 0)])]
    ppermute x4 -> x3, waiting for transfers between devices: 7.82 us -> 6.38 us  [the longest x1 6.38 us: line_device(): given = lax.ppermute(pieces[1], 'orb', outward)]
    ppermute x4 -> x3, starting transfers between devices: 4.19 us -> 2.95 us  [the longest x1 1.64 us: line_device(): far = lax.ppermute(slab, 'cmp', to_far)]
    pallas_call x3 -> x4, Pallas kernels: 4.05 us -> 3.73 us  [the longest x1 2.54 us: line_device(): call(outer_kernel, block, 'vvvvvvvssa', [pltpu.VMEM(parts.shape, parts.dt...]
  transfers between devices with their start and end apart: 16 -> 15, of which waited for: 7 -> 5; matrix products, arithmetic and copies ran while one was open for 0% -> 0% of each run, Pallas kernels for 15% -> 20%
where the time goes in v3:
time: 52 us; the launch traced here: 51.7 us
  waiting for transfers between devices  20.5 us (39%)
  starting transfers between devices  16.2 us (31%)
  Pallas kernels  10.9 us (21%)
  local copies, waits for them, and re-layouts  3.2 us (6%)
  between operations  0.87 us (2%)
    ppermute x1, waiting for transfers between devices, line_device(): given = lax.ppermute(pieces[1], 'orb', outward)  6.38 us
    ppermute x1, waiting for transfers between devices, line_device(): pair = lax.ppermute(psi, 'orb', swap)  5.76 us
    ppermute x1, waiting for transfers between devices, line_device(): pair_far = lax.ppermute(pair, 'cmp', to_far)  4.93 us
    ppermute x3, waiting for transfers between devices, line_device(): lax.ppermute(part, 'cmp', [(i, i ^ k) for i in range(n_cmp)])  3.36 us
    unnamed x16, local copies, waits for them, and re-layouts  3.2 us
    ppermute x1, starting transfers between devices, line_device(): pair = lax.ppermute(psi, 'orb', swap)  3.09 us
    pallas_call x1, Pallas kernels, line_device(): call(outer_kernel, block, 'vvvvvvvssa', [pltpu.VMEM(parts.shape, parts.dt...  2.54 us
    ppermute x3, starting transfers between devices, line_device(): lax.ppermute(part, 'cmp', [(i, i ^ k) for i in range(n_cmp)])  2.38 us
  transfers between devices with their start and end apart: 15, of which 5 were waited for; matrix products, arithmetic and copies ran while one was open for 0% of the time, Pallas kernels for 20%

profile of v3, /device:TPU:0, one launch (start us, length us, event | category | flops | bytes accessed | tf_op | source)
XLA Modules:
  0.0 51.7 jit_solution(9713213109963980395)
XLA Ops:
  0.6 3.1 %collective-permute-start = (f32[8,16,1024]{2,1,0:T(8,128)}, f32[8,16,1024]{2,1,0:T(8,128)S(1)}, u32[]{:S(2)}, u32[]{:S(2)}) collective-permute-start(f32[8,16,1024]{2,1,0:T(8,128)} %own_ref.3), channel_id=1, source_target_pairs={{0,4},{4,0},{8,12},{12,8},{1,5},{5,1},{9,13},{13,9},{2,6},{6,2},{1... | collective-permute-start | bytes 1572872 | tf_op jit(solution)/shard_map/ppermute | solution.py:419
  3.7 0.1 add_bitcast_fusion.refs_0_
  3.8 0.0 copy-start.7
  3.8 0.0 collective-permute-start.4
  3.8 0.7 %collective-permute-start.1 = (f32[8,16,1024]{2,1,0:T(8,128)}, f32[8,16,1024]{2,1,0:T(8,128)S(1)}, u32[]{:S(2)}, u32[]{:S(2)}) collective-permute-start(f32[8,16,1024]{2,1,0:T(8,128)} %own_ref.3), channel_id=1, source_target_pairs={{4,8},{8,4},{5,9},{9,5},{6,10},{10,6},{7,11},{11,7},{20,24},{24,20... | collective-permute-start | bytes 1572872 | tf_op jit(solution)/shard_map/ppermute | solution.py:420
  4.5 1.6 %collective-permute-start.3 = (f32[8,16,1024]{2,1,0:T(8,128)}, f32[8,16,1024]{2,1,0:T(8,128)S(1)}, u32[]{:S(2)}, u32[]{:S(2)}) collective-permute-start(f32[8,16,1024]{2,1,0:T(8,128)} %own_ref.3), channel_id=1, source_target_pairs={{0,3},{1,2},{2,1},{3,0},{4,7},{5,6},{6,5},{7,4},{8,11},{9,10},{10,... | collective-permute-start | bytes 1572872 | tf_op jit(solution)/shard_map/ppermute | solution.py:424
  6.2 0.0 copy-done.7
  6.2 0.0 copy-start
  6.2 1.1 %copy-done = f32[8,16,1024]{2,1,0:T(8,128)S(1)} copy-done((f32[8,16,1024]{2,1,0:T(8,128)S(1)}, f32[8,16,1024]{2,1,0:T(8,128)}, u32[]{:S(2)}) %copy-start) | copy-done | bytes 524312
  7.2 0.0 copy-start.2
  7.2 0.9 %copy-done.2 = bf16[256,256]{1,0:T(8,128)(2,1)S(1)} copy-done((bf16[256,256]{1,0:T(8,128)(2,1)S(1)}, bf16[256,256]{1,0:T(8,128)(2,1)}, u32[]{:S(2)}) %copy-start.2) | copy-done | bytes 131096
  8.2 0.0 copy-start.4
  8.2 0.8 %copy-done.4 = f32[16,1024]{1,0:T(8,128)S(1)} copy-done((f32[16,1024]{1,0:T(8,128)S(1)}, f32[16,1024]{1,0:T(8,128)}, u32[]{:S(2)}) %copy-start.4) | copy-done | bytes 65560
  9.0 0.0 copy-start.3
  9.0 0.0 copy-start.5
  9.0 1.1 %shard_map.69 = (f32[8,16,1024]{2,1,0:T(8,128)S(1)}, bf16[256,1024]{1,0:T(8,128)(2,1)S(1)}) custom-call(f32[8,16,1024]{2,1,0:T(8,128)S(1)} %copy-done, f32[16,1024]{1,0:T(8,128)S(1)} %copy-done.4, s32[32]{0:T(128)S(1)} %copy-done.7, s32[1,2]{1,0:T(1,128)S(1)} %shard_map.68.place_ref, bf16[256,256]{1,0:T(8,128)(2,1)S(1)} %copy-done.2), custom_call_target="tpu_custom_call" | custom-call | flops 1 | bytes 1 | tf_op jit(solution)/shard_map/pallas_call | solution.py:426
  10.1 5.8 %collective-permute-done.psi_ref.pair_ref = f32[8,16,1024]{2,1,0:T(8,128)S(1)} collective-permute-done((f32[8,16,1024]{2,1,0:T(8,128)}, f32[8,16,1024]{2,1,0:T(8,128)S(1)}, u32[]{:S(2)}, u32[]{:S(2)}) %collective-permute-start) | collective-permute-done | bytes 524320 | tf_op jit(solution)/shard_map/ppermute | solution.py:419
  15.9 0.7 %collective-permute-start.2 = (f32[8,16,1024]{2,1,0:T(8,128)S(1)}, f32[8,16,1024]{2,1,0:T(8,128)S(1)}, u32[]{:S(2)}, u32[]{:S(2)}) collective-permute-start(f32[8,16,1024]{2,1,0:T(8,128)S(1)} %collective-permute-done.psi_ref.pair_ref), channel_id=1, source_target_pairs={{4,8},{8,4},{5,9},{9,5},{6,10},{10,6},{7,11},{11,7},{20,24},{24,20... | collective-permute-start | bytes 1572872 | tf_op jit(solution)/shard_map/ppermute | solution.py:432
  16.5 0.1 collective-permute-start.6
  16.6 0.0 collective-permute-done.4.near_ref
  16.6 1.8 %collective-permute-start.5 = (f32[8,16,1024]{2,1,0:T(8,128)S(1)}, f32[8,16,1024]{2,1,0:T(8,128)S(1)}, u32[]{:S(2)}, u32[]{:S(2)}) collective-permute-start(f32[8,16,1024]{2,1,0:T(8,128)S(1)} %collective-permute-done.psi_ref.pair_ref), channel_id=1, source_target_pairs={{0,3},{1,2},{2,1},{3,0},{4,7},{5,6},{6,5},{7,4},{8,11},{9,10},{10,... | collective-permute-start | bytes 1572872 | tf_op jit(solution)/shard_map/ppermute | solution.py:430
  18.4 0.0 collective-permute-done.1.field_ref
  18.4 1.3 %collective-permute-start.10 = (f32[8,16,1024]{2,1,0:T(8,128)S(1)}, f32[8,16,1024]{2,1,0:T(8,128)S(1)}, u32[]{:S(2)}, u32[]{:S(2)}) collective-permute-start(f32[8,16,1024]{2,1,0:T(8,128)S(1)} %collective-permute-done.1.field_ref), channel_id=1, source_target_pairs={{4,0},{8,12},{5,1},{9,13},{6,2},{10,14},{7,3},{11,15},{20,16},{24,... | collective-permute-start | bytes 1572872 | tf_op jit(solution)/shard_map/ppermute | solution.py:433
  19.7 0.0 copy-done.3
  19.7 0.0 copy-done.5
  19.7 1.1 %shard_map.70 = (f32[8,16,1024]{2,1,0:T(8,128)S(1)}, bf16[256,1024]{1,0:T(8,128)(2,1)S(1)}) custom-call(f32[8,16,1024]{2,1,0:T(8,128)S(1)} %collective-permute-done.psi_ref.pair_ref, f32[16,1024]{1,0:T(8,128)S(1)} %copy-done.5, s32[32]{0:T(128)S(1)} %copy-done.7, s32[1,2]{1,0:T(1,128)S(1)} %shard_map.68.place_ref, bf16[256,256]{1,0:T(8,128)(2,1)S(1)} %copy-done.3), custom_call_target="tpu_custom_call" | custom-call | flops 1 | bytes 1 | tf_op jit(solution)/shard_map/pallas_call | solution.py:438
  20.8 0.0 copy-start.1
  20.8 0.0 copy-start.6
  20.8 0.6 %shard_map.71.refs_2_.third_ref.third_parts = bf16[256,1024]{1,0:T(8,128)(2,1)S(1)} custom-call(f32[8,16,1024]{2,1,0:T(8,128)S(1)} %collective-permute-done.1.field_ref, s32[32]{0:T(128)S(1)} %copy-done.7, s32[1,2]{1,0:T(1,128)S(1)} %shard_map.68.place_ref), custom_call_target="tpu_custom_call" | custom-call | flops 1 | bytes 1 | tf_op jit(solution)/shard_map/pallas_call | solution.py:441
  21.5 0.0 collective-permute-done.3.far_ref
  21.5 0.4 copy-done.1
  21.9 0.0 copy-done.6
  21.9 1.0 %shard_map.72 = (f32[8,16,1024]{2,1,0:T(8,128)S(1)}, bf16[256,1024]{1,0:T(8,128)(2,1)S(1)}) custom-call(f32[8,16,1024]{2,1,0:T(8,128)S(1)} %collective-permute-done.3.far_ref, f32[8,16,1024]{2,1,0:T(8,128)S(1)} %copy-done.1, f32[8,16,1024]{2,1,0:T(8,128)S(1)} %collective-permute-done.4.near_ref, f32[8,16,1024]{2,1,0:T(8,128)S(1)} %get-tuple-element.36.local_ref, ...), custom_call_target="tpu_custom_call" | custom-call | flops 1 | bytes 1 | tf_op jit(solution)/shard_map/pallas_call | solution.py:435
  22.8 0.6 %shard_map.73.early_ref = f32[24,128]{1,0:T(8,128)S(1)} custom-call(bf16[256,1024]{1,0:T(8,128)(2,1)S(1)} %get-tuple-element.31.refs_0_.own_ref.own_parts, bf16[256,1024]{1,0:T(8,128)(2,1)S(1)} %get-tuple-element.33.refs_1_.pair_ref.pair_parts, bf16[256,1024]{1,0:T(8,128)(2,1)S(1)} %shard_map.71.refs_2_.third_ref.third_parts, ...), custom_call_target="tpu_custom_call" | custom-call | flops 1 | bytes 1 | tf_op jit(solution)/shard_map/pallas_call | solution.py:442
  23.5 0.0 collective-permute-done.2.field_ref
  23.5 1.3 %collective-permute-start.11 = (f32[8,16,1024]{2,1,0:T(8,128)S(1)}, f32[8,16,1024]{2,1,0:T(8,128)S(1)}, u32[]{:S(2)}, u32[]{:S(2)}) collective-permute-start(f32[8,16,1024]{2,1,0:T(8,128)S(1)} %collective-permute-done.2.field_ref), channel_id=1, source_target_pairs={{4,0},{8,12},{5,1},{9,13},{6,2},{10,14},{7,3},{11,15},{20,16},{24,... | collective-permute-start | bytes 1572872 | tf_op jit(solution)/shard_map/ppermute | solution.py:452
  24.8 0.6 %shard_map.74.fourth_ref.fourth_parts = bf16[256,1024]{1,0:T(8,128)(2,1)S(1)} custom-call(f32[8,16,1024]{2,1,0:T(8,128)S(1)} %collective-permute-done.2.field_ref, s32[32]{0:T(128)S(1)} %copy-done.7, s32[1,2]{1,0:T(1,128)S(1)} %shard_map.68.place_ref), custom_call_target="tpu_custom_call" | custom-call | flops 1 | bytes 1 | tf_op jit(solution)/shard_map/pallas_call | solution.py:453
  25.4 0.0 collective-permute-done.6.near_ref
  25.4 4.9 %collective-permute-done.5.far_ref = f32[8,16,1024]{2,1,0:T(8,128)S(1)} collective-permute-done((f32[8,16,1024]{2,1,0:T(8,128)S(1)}, f32[8,16,1024]{2,1,0:T(8,128)S(1)}, u32[]{:S(2)}, u32[]{:S(2)}) %collective-permute-start.5) | collective-permute-done | bytes 524320 | tf_op jit(solution)/shard_map/ppermute | solution.py:430
  30.4 1.0 %shard_map.75 = (f32[8,16,1024]{2,1,0:T(8,128)S(1)}, bf16[256,1024]{1,0:T(8,128)(2,1)S(1)}) custom-call(f32[8,16,1024]{2,1,0:T(8,128)S(1)} %collective-permute-done.5.far_ref, f32[8,16,1024]{2,1,0:T(8,128)S(1)} %collective-permute-done.psi_ref.pair_ref, f32[8,16,1024]{2,1,0:T(8,128)S(1)} %collective-permute-done.6.near_ref, ...), custom_call_target="tpu_custom_call" | custom-call | flops 1 | bytes 1 | tf_op jit(solution)/shard_map/pallas_call | solution.py:449
  31.3 1.1 %shard_map.76.refs_0_ = f32[32,16]{1,0:T(8,128)S(1)} custom-call(bf16[256,1024]{1,0:T(8,128)(2,1)S(1)} %get-tuple-element.31.refs_0_.own_ref.own_parts, bf16[256,1024]{1,0:T(8,128)(2,1)S(1)} %get-tuple-element.33.refs_1_.pair_ref.pair_parts, bf16[256,1024]{1,0:T(8,128)(2,1)S(1)} %shard_map.71.refs_2_.third_ref.third_parts, ...), custom_call_target="tpu_custom_call" | custom-call | flops 1 | bytes 1 | tf_op jit(solution)/shard_map/pallas_call | solution.py:454
  32.5 2.0 %collective-permute-start.9 = (f32[32,16]{1,0:T(8,128)S(1)}, f32[32,16]{1,0:T(8,128)S(1)}, u32[]{:S(2)}, u32[]{:S(2)}) collective-permute-start(f32[32,16]{1,0:T(8,128)S(1)} %shard_map.76.refs_0_), channel_id=1, source_target_pairs={{0,3},{1,2},{2,1},{3,0},{4,7},{5,6},{6,5},{7,4},{8,11},{9,10},{10,... | collective-permute-start | bytes 6152 | tf_op jit(solution)/shard_map/ppermute | solution.py:459
  34.5 0.4 collective-permute-start.8
  34.9 0.0 collective-permute-start.7
  34.9 1.1 %collective-permute-done.9.refs_3_ = f32[32,16]{1,0:T(8,128)S(1)} collective-permute-done((f32[32,16]{1,0:T(8,128)S(1)}, f32[32,16]{1,0:T(8,128)S(1)}, u32[]{:S(2)}, u32[]{:S(2)}) %collective-permute-start.9) | collective-permute-done | bytes 2080 | tf_op jit(solution)/shard_map/ppermute | solution.py:459
  35.9 2.3 %collective-permute-done.8.refs_2_ = f32[32,16]{1,0:T(8,128)S(1)} collective-permute-done((f32[32,16]{1,0:T(8,128)S(1)}, f32[32,16]{1,0:T(8,128)S(1)}, u32[]{:S(2)}, u32[]{:S(2)}) %collective-permute-start.8) | collective-permute-done | bytes 2080 | tf_op jit(solution)/shard_map/ppermute | solution.py:459
  38.2 0.0 collective-permute-done.7.refs_1_
  38.2 0.0 collective-permute-done.10.third_ref
  38.3 0.6 %shard_map.78 = (f32[16,256]{1,0:T(8,128)S(1)}, f32[48,256]{1,0:T(8,128)S(1)}, f32[16,256]{1,0:T(8,128)S(1)}, f32[16,256]{1,0:T(8,128)S(1)}, f32[8,16,1024]{2,1,0:T(8,128)}) custom-call(f32[8,16,1024]{2,1,0:T(8,128)S(1)} %copy-done.1, f32[8,16,1024]{2,1,0:T(8,128)S(1)} %collective-permute-done.psi_ref.pair_ref, ...), custom_call_target="tpu_custom_call" | custom-call | flops 1 | bytes 1 | tf_op jit(solution)/shard_map/pallas_call | solution.py:467
  38.8 1.3 %collective-permute-start.12 = (f32[48,256]{1,0:T(8,128)S(1)}, f32[48,256]{1,0:T(8,128)S(1)}, u32[]{:S(2)}, u32[]{:S(2)}) collective-permute-start(f32[48,256]{1,0:T(8,128)S(1)} %get-tuple-element.46), channel_id=1, source_target_pairs={{4,0},{8,12},{5,1},{9,13},{6,2},{10,14},{7,3},{11,15},{20,16},{24,... | collective-permute-start | bytes 147464 | tf_op jit(solution)/shard_map/ppermute | solution.py:481
  40.1 1.3 %collective-permute-start.13 = (f32[16,256]{1,0:T(8,128)S(1)}, f32[16,256]{1,0:T(8,128)S(1)}, u32[]{:S(2)}, u32[]{:S(2)}) collective-permute-start(f32[16,256]{1,0:T(8,128)S(1)} %get-tuple-element.48), channel_id=1, source_target_pairs={{4,12},{8,0},{5,13},{9,1},{6,14},{10,2},{7,15},{11,3},{20,28},{24,... | collective-permute-start | bytes 49160 | tf_op jit(solution)/shard_map/ppermute | solution.py:483
  41.4 0.7 %collective-permute-start.14 = (f32[16,256]{1,0:T(8,128)S(1)}, f32[16,256]{1,0:T(8,128)S(1)}, u32[]{:S(2)}, u32[]{:S(2)}) collective-permute-start(f32[16,256]{1,0:T(8,128)S(1)} %get-tuple-element.49), channel_id=1, source_target_pairs={{4,8},{8,4},{5,9},{9,5},{6,10},{10,6},{7,11},{11,7},{20,24},{24,20... | collective-permute-start | bytes 49160 | tf_op jit(solution)/shard_map/ppermute | solution.py:484
  42.1 6.4 %collective-permute-done.12.given_ref.refs_3_ = f32[48,256]{1,0:T(8,128)S(1)} collective-permute-done((f32[48,256]{1,0:T(8,128)S(1)}, f32[48,256]{1,0:T(8,128)S(1)}, u32[]{:S(2)}, u32[]{:S(2)}) %collective-permute-start.12) | collective-permute-done | bytes 49184 | tf_op jit(solution)/shard_map/ppermute | solution.py:481
  48.5 0.0 collective-permute-done.11.fourth_ref
  48.5 2.5 %shard_map.79 = f32[8,16,1024]{2,1,0:T(8,128)} custom-call(f32[8,16,1024]{2,1,0:T(8,128)S(1)} %copy-done.1, bf16[256,1024]{1,0:T(8,128)(2,1)S(1)} %get-tuple-element.31.refs_0_.own_ref.own_parts, bf16[256,1024]{1,0:T(8,128)(2,1)S(1)} %get-tuple-element.33.refs_1_.pair_ref.pair_parts, ...), custom_call_target="tpu_custom_call", output_to_operand_aliasing={{}: (9, {})} | custom-call | flops 1 | bytes 1 | tf_op jit(solution)/shard_map/pallas_call | solution.py:486
  51.0 0.0 collective-permute-done.13.refs_1_
  51.0 0.0 collective-permute-done.14.refs_2_
  51.1 0.6 %shard_map.80 = f32[16,256]{1,0:T(8,128)} custom-call(f32[16,256]{1,0:T(8,128)S(1)} %get-tuple-element.51.refs_0_, f32[16,256]{1,0:T(8,128)S(1)} %collective-permute-done.13.refs_1_, f32[16,256]{1,0:T(8,128)S(1)} %collective-permute-done.14.refs_2_, f32[48,256]{1,0:T(8,128)S(1)} %collective-permute-done.12.given_ref.refs_3_), custom_call_target="tpu_custom_call" | custom-call | flops 1 | bytes 1 | tf_op jit(solution)/shard_map/pallas_call | solution.py:498
  (2 shorter events, 0.0 us)
Async XLA Ops:
  0.6 15.2 %collective-permute-start = (f32[8,16,1024]{2,1,0:T(8,128)}, f32[8,16,1024]{2,1,0:T(8,128)S(1)}, u32[]{:S(2)}, u32[]{:S(2)}) collective-permute-start(f32[8,16,1024]{2,1,0:T(8,128)} %own_ref.3), channel_id=1, source_target_pairs={{0,4},{4,0},{8,12},{12,8},{1,5},{5,1},{9,13},{13,9},{2,6},{6,2},{1... | collective-permute-start | bytes 1572872 | tf_op jit(solution)/shard_map/ppermute | solution.py:419
  3.8 2.4 %copy-start.7 = (s32[32]{0:T(128)S(1)}, s32[32]{0:T(128)}, u32[]{:S(2)}) copy-start(s32[32]{0:T(128)} %extent_ref.15) | copy-start | bytes 388
  3.8 12.8 %collective-permute-start.4 = (f32[8,16,1024]{2,1,0:T(8,128)}, f32[8,16,1024]{2,1,0:T(8,128)S(1)}, u32[]{:S(2)}, u32[]{:S(2)}) collective-permute-start(f32[8,16,1024]{2,1,0:T(8,128)} %own_ref.3), channel_id=1, source_target_pairs={{0,1},{1,0},{2,3},{3,2},{4,5},{5,4},{6,7},{7,6},{8,9},{9,8},{10,11... | collective-permute-start | bytes 1572872 | tf_op jit(solution)/shard_map/ppermute | solution.py:423
  3.8 14.6 %collective-permute-start.1 = (f32[8,16,1024]{2,1,0:T(8,128)}, f32[8,16,1024]{2,1,0:T(8,128)S(1)}, u32[]{:S(2)}, u32[]{:S(2)}) collective-permute-start(f32[8,16,1024]{2,1,0:T(8,128)} %own_ref.3), channel_id=1, source_target_pairs={{4,8},{8,4},{5,9},{9,5},{6,10},{10,6},{7,11},{11,7},{20,24},{24,20... | collective-permute-start | bytes 1572872 | tf_op jit(solution)/shard_map/ppermute | solution.py:420
  4.5 17.0 %collective-permute-start.3 = (f32[8,16,1024]{2,1,0:T(8,128)}, f32[8,16,1024]{2,1,0:T(8,128)S(1)}, u32[]{:S(2)}, u32[]{:S(2)}) collective-permute-start(f32[8,16,1024]{2,1,0:T(8,128)} %own_ref.3), channel_id=1, source_target_pairs={{0,3},{1,2},{2,1},{3,0},{4,7},{5,6},{6,5},{7,4},{8,11},{9,10},{10,... | collective-permute-start | bytes 1572872 | tf_op jit(solution)/shard_map/ppermute | solution.py:424
  6.2 1.1 %copy-start = (f32[8,16,1024]{2,1,0:T(8,128)S(1)}, f32[8,16,1024]{2,1,0:T(8,128)}, u32[]{:S(2)}) copy-start(f32[8,16,1024]{2,1,0:T(8,128)} %own_ref.3) | copy-start | bytes 1572868
  7.2 0.9 %copy-start.2 = (bf16[256,256]{1,0:T(8,128)(2,1)S(1)}, bf16[256,256]{1,0:T(8,128)(2,1)}, u32[]{:S(2)}) copy-start(bf16[256,256]{1,0:T(8,128)(2,1)} %constant.24.clone.band_ref) | copy-start | bytes 393220
  8.2 0.8 %copy-start.4 = (f32[16,1024]{1,0:T(8,128)S(1)}, f32[16,1024]{1,0:T(8,128)}, u32[]{:S(2)}) copy-start(f32[16,1024]{1,0:T(8,128)} %potential_ref.3) | copy-start | bytes 196612
  9.0 10.7 %copy-start.3 = (bf16[256,256]{1,0:T(8,128)(2,1)S(1)}, bf16[256,256]{1,0:T(8,128)(2,1)}, u32[]{:S(2)}) copy-start(bf16[256,256]{1,0:T(8,128)(2,1)} %constant.24.clone.band_ref) | copy-start | bytes 393220
  9.0 10.7 %copy-start.5 = (f32[16,1024]{1,0:T(8,128)S(1)}, f32[16,1024]{1,0:T(8,128)}, u32[]{:S(2)}) copy-start(f32[16,1024]{1,0:T(8,128)} %potential_ref.3) | copy-start | bytes 196612
  15.9 7.6 %collective-permute-start.2 = (f32[8,16,1024]{2,1,0:T(8,128)S(1)}, f32[8,16,1024]{2,1,0:T(8,128)S(1)}, u32[]{:S(2)}, u32[]{:S(2)}) collective-permute-start(f32[8,16,1024]{2,1,0:T(8,128)S(1)} %collective-permute-done.psi_ref.pair_ref), channel_id=1, source_target_pairs={{4,8},{8,4},{5,9},{9,5},{6,10},{10,6},{7,11},{11,7},{20,24},{24,20... | collective-permute-start | bytes 1572872 | tf_op jit(solution)/shard_map/ppermute | solution.py:432
  16.5 8.9 %collective-permute-start.6 = (f32[8,16,1024]{2,1,0:T(8,128)S(1)}, f32[8,16,1024]{2,1,0:T(8,128)S(1)}, u32[]{:S(2)}, u32[]{:S(2)}) collective-permute-start(f32[8,16,1024]{2,1,0:T(8,128)S(1)} %collective-permute-done.psi_ref.pair_ref), channel_id=1, source_target_pairs={{0,1},{1,0},{2,3},{3,2},{4,5},{5,4},{6,7},{7,6},{8,9},{9,8},{10,11... | collective-permute-start | bytes 1572872 | tf_op jit(solution)/shard_map/ppermute | solution.py:431
  16.6 13.7 %collective-permute-start.5 = (f32[8,16,1024]{2,1,0:T(8,128)S(1)}, f32[8,16,1024]{2,1,0:T(8,128)S(1)}, u32[]{:S(2)}, u32[]{:S(2)}) collective-permute-start(f32[8,16,1024]{2,1,0:T(8,128)S(1)} %collective-permute-done.psi_ref.pair_ref), channel_id=1, source_target_pairs={{0,3},{1,2},{2,1},{3,0},{4,7},{5,6},{6,5},{7,4},{8,11},{9,10},{10,... | collective-permute-start | bytes 1572872 | tf_op jit(solution)/shard_map/ppermute | solution.py:430
  18.4 19.9 %collective-permute-start.10 = (f32[8,16,1024]{2,1,0:T(8,128)S(1)}, f32[8,16,1024]{2,1,0:T(8,128)S(1)}, u32[]{:S(2)}, u32[]{:S(2)}) collective-permute-start(f32[8,16,1024]{2,1,0:T(8,128)S(1)} %collective-permute-done.1.field_ref), channel_id=1, source_target_pairs={{4,0},{8,12},{5,1},{9,13},{6,2},{10,14},{7,3},{11,15},{20,16},{24,... | collective-permute-start | bytes 1572872 | tf_op jit(solution)/shard_map/ppermute | solution.py:433
  20.8 1.0 %copy-start.1 = (f32[8,16,1024]{2,1,0:T(8,128)S(1)}, f32[8,16,1024]{2,1,0:T(8,128)}, u32[]{:S(2)}) copy-start(f32[8,16,1024]{2,1,0:T(8,128)} %own_ref.3) | copy-start | bytes 1572868
  20.8 1.0 %copy-start.6 = (bf16[2,16,144]{2,1,0:T(8,128)(2,1)S(1)}, bf16[2,16,144]{2,1,0:T(8,128)(2,1)}, u32[]{:S(2)}) copy-start(bf16[2,16,144]{2,1,0:T(8,128)(2,1)} %constant.25.clone.band_ref) | copy-start | bytes 27652
  23.5 25.0 %collective-permute-start.11 = (f32[8,16,1024]{2,1,0:T(8,128)S(1)}, f32[8,16,1024]{2,1,0:T(8,128)S(1)}, u32[]{:S(2)}, u32[]{:S(2)}) collective-permute-start(f32[8,16,1024]{2,1,0:T(8,128)S(1)} %collective-permute-done.2.field_ref), channel_id=1, source_target_pairs={{4,0},{8,12},{5,1},{9,13},{6,2},{10,14},{7,3},{11,15},{20,16},{24,... | collective-permute-start | bytes 1572872 | tf_op jit(solution)/shard_map/ppermute | solution.py:452
  32.5 3.4 %collective-permute-start.9 = (f32[32,16]{1,0:T(8,128)S(1)}, f32[32,16]{1,0:T(8,128)S(1)}, u32[]{:S(2)}, u32[]{:S(2)}) collective-permute-start(f32[32,16]{1,0:T(8,128)S(1)} %shard_map.76.refs_0_), channel_id=1, source_target_pairs={{0,3},{1,2},{2,1},{3,0},{4,7},{5,6},{6,5},{7,4},{8,11},{9,10},{10,... | collective-permute-start | bytes 6152 | tf_op jit(solution)/shard_map/ppermute | solution.py:459
  34.5 3.7 %collective-permute-start.8 = (f32[32,16]{1,0:T(8,128)S(1)}, f32[32,16]{1,0:T(8,128)S(1)}, u32[]{:S(2)}, u32[]{:S(2)}) collective-permute-start(f32[32,16]{1,0:T(8,128)S(1)} %shard_map.76.refs_0_), channel_id=1, source_target_pairs={{0,2},{1,3},{2,0},{3,1},{4,6},{5,7},{6,4},{7,5},{8,10},{9,11},{10,... | collective-permute-start | bytes 6152 | tf_op jit(solution)/shard_map/ppermute | solution.py:459
  34.9 3.4 %collective-permute-start.7 = (f32[32,16]{1,0:T(8,128)S(1)}, f32[32,16]{1,0:T(8,128)S(1)}, u32[]{:S(2)}, u32[]{:S(2)}) collective-permute-start(f32[32,16]{1,0:T(8,128)S(1)} %shard_map.76.refs_0_), channel_id=1, source_target_pairs={{0,1},{1,0},{2,3},{3,2},{4,5},{5,4},{6,7},{7,6},{8,9},{9,8},{10,11... | collective-permute-start | bytes 6152 | tf_op jit(solution)/shard_map/ppermute | solution.py:459
  38.8 9.6 %collective-permute-start.12 = (f32[48,256]{1,0:T(8,128)S(1)}, f32[48,256]{1,0:T(8,128)S(1)}, u32[]{:S(2)}, u32[]{:S(2)}) collective-permute-start(f32[48,256]{1,0:T(8,128)S(1)} %get-tuple-element.46), channel_id=1, source_target_pairs={{4,0},{8,12},{5,1},{9,13},{6,2},{10,14},{7,3},{11,15},{20,16},{24,... | collective-permute-start | bytes 147464 | tf_op jit(solution)/shard_map/ppermute | solution.py:481
  40.1 10.9 %collective-permute-start.13 = (f32[16,256]{1,0:T(8,128)S(1)}, f32[16,256]{1,0:T(8,128)S(1)}, u32[]{:S(2)}, u32[]{:S(2)}) collective-permute-start(f32[16,256]{1,0:T(8,128)S(1)} %get-tuple-element.48), channel_id=1, source_target_pairs={{4,12},{8,0},{5,13},{9,1},{6,14},{10,2},{7,15},{11,3},{20,28},{24,... | collective-permute-start | bytes 49160 | tf_op jit(solution)/shard_map/ppermute | solution.py:483
  41.4 9.6 %collective-permute-start.14 = (f32[16,256]{1,0:T(8,128)S(1)}, f32[16,256]{1,0:T(8,128)S(1)}, u32[]{:S(2)}, u32[]{:S(2)}) collective-permute-start(f32[16,256]{1,0:T(8,128)S(1)} %get-tuple-element.49), channel_id=1, source_target_pairs={{4,8},{8,4},{5,9},{9,5},{6,10},{10,6},{7,11},{11,7},{20,24},{24,20... | collective-permute-start | bytes 49160 | tf_op jit(solution)/shard_map/ppermute | solution.py:484

commit v4 on v3

--- a/solution.py
+++ b/solution.py
@@ -128,42 +128,54 @@
     return np.stack(both)
 
 
-def columns_of(shape):
-    return lax.broadcasted_iota(jnp.int32, shape, len(shape) - 1)
-
-
-def owner_of(place_ref, f):
-    z = place_ref[0, 0]
+def columns_kernel(out_ref):
+    out_ref[...] = lax.broadcasted_iota(jnp.int32, out_ref.shape, 1)
+
+
+def owner_of(f):
+    z = lax.axis_index("orb")
     if f < 2:
         return z if f == 0 else jnp.where(z % 2 == 0, z + 1, z - 1)
     left, right = (2, 1) if f == 2 else (3, 0)
     return jnp.where(z < 2, left, right)
 
 
-def masked(field_ref, a, extent_ref, owner):
-    orbs, planes, grid_p = field_ref.shape
-    column = columns_of((planes, grid_p))
-    return jnp.where(column < extent_ref[owner * orbs + a], field_ref[a], 0.0)
-
-
-def split_into(parts_ref, field_ref, extent_ref, owner):
+def on_inner():
+    z = lax.axis_index("orb")
+    return (z == 1) | (z == 2)
+
+
+def live_kernel(columns_ref, extent_ref, out_ref):
+    orbs = out_ref.shape[0] // 4
+    for f in range(4):
+        owner = owner_of(f)
+        for a in range(orbs):
+            row = jnp.where(columns_ref[:1, :] < extent_ref[owner * orbs + a], 1.0, 0.0)
+            out_ref[f * orbs + a : f * orbs + a + 1, :] = row
+
+
+def masked(field_ref, a, live_ref, f):
+    at = f * field_ref.shape[0] + a
+    return field_ref[a] * live_ref[at : at + 1, :]
+
+
+def split_into(parts_ref, field_ref, live_ref, f):
     orbs, planes, _ = field_ref.shape
     for a in range(orbs):
-        high, low = two_parts(masked(field_ref, a, extent_ref, owner))
+        high, low = two_parts(masked(field_ref, a, live_ref, f))
         parts_ref[a * planes : (a + 1) * planes, :] = high
         parts_ref[(orbs + a) * planes : (orbs + a + 1) * planes, :] = low
 
 
-def split_kernel(f, field_ref, extent_ref, place_ref, parts_ref):
-    split_into(parts_ref, field_ref, extent_ref, owner_of(place_ref, f))
-
-
-def local_kernel(f, psi_ref, potential_ref, extent_ref, place_ref, band_ref, out_ref, parts_ref, phi_ref):
+def split_kernel(f, field_ref, live_ref, parts_ref):
+    split_into(parts_ref, field_ref, live_ref, f)
+
+
+def local_kernel(f, psi_ref, potential_ref, live_ref, band_ref, out_ref, parts_ref, phi_ref):
     orbs, planes, grid_p = psi_ref.shape
     tiles = grid_p // lanes
-    owner = owner_of(place_ref, f)
     for a in range(orbs):
-        phi = masked(psi_ref, a, extent_ref, owner)
+        phi = masked(psi_ref, a, live_ref, f)
         phi_ref[a * planes : (a + 1) * planes, :] = phi
         high, low = two_parts(phi)
         parts_ref[a * planes : (a + 1) * planes, :] = high
@@ -184,21 +196,17 @@
 
 
 def plane_kernel(
-    f, far_ref, psi_ref, near_ref, local_ref, extent_ref, place_ref, band_ref, out_ref, parts_ref
+    f, far_ref, psi_ref, near_ref, local_ref, live_ref, band_ref, out_ref, parts_ref
 ):
-    orbs, planes, grid_p = psi_ref.shape
-    column = columns_of((planes, grid_p))
-    owner = owner_of(place_ref, f)
-    band = band_ref[place_ref[0, 1]]
+    orbs, planes, _ = psi_ref.shape
+    band = band_ref[lax.axis_index("cmp") % 2]
     for a in range(orbs):
         slab = jnp.concatenate([far_ref[a], psi_ref[a], near_ref[a]], axis=0)
         high, low = two_parts(slab)
         second = jnp.dot(
             band, jnp.concatenate([high, low, high], axis=0), preferred_element_type=jnp.float32
         )
-        image = jnp.where(
-            column < extent_ref[owner * orbs + a], local_ref[a] - 0.5 * second, 0.0
-        )
+        image = (local_ref[a] - 0.5 * second) * live_ref[f * orbs + a : f * orbs + a + 1, :]
         out_ref[a] = image
         high, low = two_parts(image)
         parts_ref[a * planes : (a + 1) * planes, :] = high
@@ -302,85 +310,87 @@
 
 
 def step_kernel(
-    own_ref, pair_ref, own_parts, pair_parts, third_parts, fourth_parts, image_ref, ward_ref,
-    corr_ref, extent_ref, place_ref, kept_ref, out1_ref, out2_ref, out3_ref, new_ref, all_ref,
-    own_new, sem,
+    own_phi, pair_phi, own_parts, pair_parts, third_parts, fourth_parts, image_ref, ward_ref,
+    corr_ref, kept_ref, out1_ref, out2_ref, out3_ref, new_ref, all_ref,
 ):
-    orbs, planes, grid_p = own_ref.shape
+    orbs, planes, grid_p = image_ref.shape
     width = 2 * lanes
     share = grid_p // 4
-    z = place_ref[0, 0]
-    inner = (z == 1) | (z == 2)
-
-    @pl.when(inner)
+
+    @pl.when(on_inner())
     def _():
         out1_ref[planes:, : corr_ref.shape[1]] = corr_ref[...]
         high, low = spread_out(corr_ref[...], planes)
         fields = (own_parts, pair_parts, third_parts, fourth_parts)
-        limits = [
-            [extent_ref[owner_of(place_ref, f) * orbs + a] for a in range(orbs)] for f in range(2)
-        ]
         for c in range(grid_p // width):
             chunk = slice(c * width, (c + 1) * width)
-            column = columns_of((planes, width)) + c * width
             change = projections(high, low, fields, chunk)
             density = jnp.zeros((planes, width), jnp.float32)
-            for f, (field_ref, half_ref) in enumerate(((own_ref, image_ref), (pair_ref, ward_ref))):
+            for f, (phi_ref, half_ref) in enumerate(((own_phi, image_ref), (pair_phi, ward_ref))):
                 for a in range(orbs):
                     at = (f * orbs + a) * planes
-                    phi = jnp.where(column < limits[f][a], field_ref[a, :, chunk], 0.0)
-                    value = phi - step_length * half_ref[a, :, chunk] + change[at : at + planes]
+                    value = (
+                        phi_ref[a * planes : (a + 1) * planes, chunk]
+                        - step_length * half_ref[a, :, chunk]
+                        + change[at : at + planes]
+                    )
                     density = density + value * value
                     if f == 0:
-                        own_new[a, :, chunk] = value
+                        new_ref[a, :, chunk] = value
             all_ref[:, chunk] = density * (1.0 / (4 * orbs))
-        copy = pltpu.make_async_copy(own_new, new_ref, sem)
-        copy.start()
         for k, part_ref in enumerate((kept_ref, out1_ref, out2_ref, out3_ref)):
-            first = pl.multiple_of(jnp.bitwise_xor(z, k) * share, share)
+            first = pl.multiple_of(jnp.bitwise_xor(lax.axis_index("orb"), k) * share, share)
             part_ref[:planes, :] = all_ref[:, pl.ds(first, share)]
-        copy.wait()
-
-    @pl.when(jnp.logical_not(inner))
+
+
+def outer_split_kernel(third_ref, fourth_ref, live_ref, third_parts, fourth_parts):
+    @pl.when(jnp.logical_not(on_inner()))
     def _():
-        kept_ref[...] = jnp.zeros_like(kept_ref)
-
-
-def outer_kernel(
-    own_ref, own_parts, pair_parts, third_ref, fourth_ref, image_ref, given_ref, extent_ref,
-    place_ref, old_ref, new_ref, third_parts, fourth_parts, own_new, sem,
+        split_into(third_parts, third_ref, live_ref, 2)
+        split_into(fourth_parts, fourth_ref, live_ref, 3)
+
+
+def last_kernel(
+    own_phi, own_parts, pair_parts, third_parts, fourth_parts, image_ref, given_ref, kept_ref,
+    sent2_ref, sent3_ref, inner_new, new_ref, density_ref, own_new, own_density, sems,
 ):
-    orbs, planes, grid_p = own_ref.shape
+    orbs, planes, grid_p = image_ref.shape
     width = 2 * lanes
-    z = place_ref[0, 0]
-    outer = (z == 0) | (z == 3)
-    del old_ref
-
-    @pl.when(outer)
+
+    def write(values_ref):
+        copies = [
+            pltpu.make_async_copy(values_ref, new_ref, sems.at[0]),
+            pltpu.make_async_copy(own_density, density_ref, sems.at[1]),
+        ]
+        for copy in copies:
+            copy.start()
+        for copy in copies:
+            copy.wait()
+
+    @pl.when(on_inner())
     def _():
-        split_into(third_parts, third_ref, extent_ref, owner_of(place_ref, 2))
-        split_into(fourth_parts, fourth_ref, extent_ref, owner_of(place_ref, 3))
+        own_density[...] = kept_ref[...] + sent3_ref[...]
+        write(inner_new)
+
+    @pl.when(jnp.logical_not(on_inner()))
+    def _():
+        own_density[...] = given_ref[:planes] + sent2_ref[...]
         corr = given_ref[planes:, orbs : 2 * orbs]
         corr = jnp.concatenate([corr[orbs : 2 * orbs], corr[:orbs], corr[2 * orbs :]], axis=0)
         high, low = spread_out(corr, planes)
         fields = (own_parts, pair_parts, third_parts, fourth_parts)
         for c in range(grid_p // width):
             chunk = slice(c * width, (c + 1) * width)
-            column = columns_of((planes, width)) + c * width
             change = projections(high, low, fields, chunk)
             for a in range(orbs):
-                phi = jnp.where(column < extent_ref[z * orbs + a], own_ref[a, :, chunk], 0.0)
+                at = slice(a * planes, (a + 1) * planes)
                 own_new[a, :, chunk] = (
-                    phi
-                    - step_length * image_ref[a, :, chunk]
-                    + change[a * planes : (a + 1) * planes]
+                    own_phi[at, chunk] - step_length * image_ref[a, :, chunk] + change[at]
                 )
-        copy = pltpu.make_async_copy(own_new, new_ref, sem)
-        copy.start()
-        copy.wait()
-
-
-def call(kernel, out_shape, specs, scratch=(), out_specs=None, aliases={}):
+        write(own_new)
+
+
+def call(kernel, out_shape, specs, scratch=(), out_specs=None):
     kinds = {"s": pltpu.SMEM, "v": pltpu.VMEM, "a": pl.ANY}
     if out_specs is None:
         out_specs = "v" * len(jax.tree.leaves(out_shape))
@@ -391,7 +401,6 @@
         in_specs=[pl.BlockSpec(memory_space=kinds[kind]) for kind in specs],
         out_specs=places if isinstance(out_shape, (tuple, list)) else places[0],
         scratch_shapes=list(scratch),
-        input_output_aliases=aliases,
         compiler_params=pltpu.CompilerParams(vmem_limit_bytes=10 * 2**20),
         cost_estimate=pl.CostEstimate(flops=1, bytes_accessed=1, transcendentals=0),
     )
@@ -402,43 +411,43 @@
     n_cmp = lax.axis_size("cmp")
     rows = orbs * planes
     cells = planes * n_cmp * grid_p
-    z = lax.axis_index("orb")
-    place = jnp.stack([z, lax.axis_index("cmp") % 2]).reshape(1, 2)
     swap = [(0, 1), (1, 0), (2, 3), (3, 2)]
-    across = [(1, 2), (2, 1)]
-    outward = [(1, 0), (2, 3)]
+    across = [(1, 2), (2, 1), (0, 0), (3, 3)]
     to_near = [(i, i ^ 1) for i in range(n_cmp)]
     to_far = [(i, i ^ 3) for i in range(n_cmp)]
 
     block = jax.ShapeDtypeStruct(psi.shape, jnp.float32)
     parts = jax.ShapeDtypeStruct((2 * rows, grid_p), jnp.bfloat16)
-    field = pltpu.VMEM((rows, grid_p), jnp.float32)
+    flat = jax.ShapeDtypeStruct((rows, grid_p), jnp.float32)
     columns = jnp.asarray(column_band())
     bands = jnp.asarray(plane_bands(planes))
 
     pair = lax.ppermute(psi, "orb", swap)
     third = lax.ppermute(psi, "orb", across)
-    place = call(sum_kernel, jax.ShapeDtypeStruct(place.shape, place.dtype), "v")(place)
-    slab, place = lax.optimization_barrier((psi, place))
+    grid = call(columns_kernel, jax.ShapeDtypeStruct((8, grid_p), jnp.int32), "")()
+    slab, grid = lax.optimization_barrier((psi, grid))
     near = lax.ppermute(slab, "cmp", to_near)
     far = lax.ppermute(slab, "cmp", to_far)
 
-    local, own_parts = call(functools.partial(local_kernel, 0), (block, parts), "vvssv", [field])(
-        psi, potential, extent, place, columns
-    )
+    live = call(live_kernel, jax.ShapeDtypeStruct((4 * orbs, grid_p), jnp.float32), "vs")(
+        grid, extent
+    )
+    local, own_parts, own_phi = call(
+        functools.partial(local_kernel, 0), (block, parts, flat), "vvvv"
+    )(psi, potential, live, columns)
     pair, local, own_parts = lax.optimization_barrier((pair, local, own_parts))
     pair_far = lax.ppermute(pair, "cmp", to_far)
     pair_near = lax.ppermute(pair, "cmp", to_near)
     fourth = lax.ppermute(pair, "orb", across)
-    third_out = lax.ppermute(third, "orb", outward)
-
-    image, image_parts = call(functools.partial(plane_kernel, 0), (block, parts), "vvvvssv")(
-        far, psi, near, local, extent, place, bands
-    )
-    ward_local, pair_parts = call(
-        functools.partial(local_kernel, 1), (block, parts), "vvssv", [field]
-    )(pair, potential, extent, place, columns)
-    third_parts = call(functools.partial(split_kernel, 2), parts, "vss")(third, extent, place)
+    third_out = lax.ppermute(third, "orb", swap)
+
+    image, image_parts = call(functools.partial(plane_kernel, 0), (block, parts), "vvvvvv")(
+        far, psi, near, local, live, bands
+    )
+    ward_local, pair_parts, pair_phi = call(
+        functools.partial(local_kernel, 1), (block, parts, flat), "vvvv"
+    )(pair, potential, live, columns)
+    third_parts = call(functools.partial(split_kernel, 2), parts, "vv")(third, live)
     early = call(
         functools.partial(overlap_kernel, planes, 3),
         jax.ShapeDtypeStruct((3 * orbs, rows), jnp.float32),
@@ -446,11 +455,11 @@
     )(own_parts, pair_parts, third_parts, image_parts)
 
     fourth, ward_local, early = lax.optimization_barrier((fourth, ward_local, early))
-    ward, ward_parts = call(functools.partial(plane_kernel, 1), (block, parts), "vvvvssv")(
-        pair_far, pair, pair_near, ward_local, extent, place, bands
-    )
-    fourth_out = lax.ppermute(fourth, "orb", outward)
-    fourth_parts = call(functools.partial(split_kernel, 3), parts, "vss")(fourth, extent, place)
+    fourth_out = lax.ppermute(fourth, "orb", swap)
+    ward, ward_parts = call(functools.partial(plane_kernel, 1), (block, parts), "vvvvvv")(
+        pair_far, pair, pair_near, ward_local, live, bands
+    )
+    fourth_parts = call(functools.partial(split_kernel, 3), parts, "vv")(fourth, live)
     part = call(
         functools.partial(correlation_kernel, planes, 1.0 / cells),
         jax.ShapeDtypeStruct((4 * orbs, 2 * orbs), jnp.float32),
@@ -464,38 +473,36 @@
 
     share = jax.ShapeDtypeStruct((planes, grid_p // 4), jnp.float32)
     wide = jax.ShapeDtypeStruct((planes + 4 * orbs, grid_p // 4), jnp.float32)
-    *pieces, new = call(
+    kept, first, second, last, inner_new = call(
         step_kernel,
         [share, wide, share, share, block],
-        "vvvvvvvvvss",
+        "vvvvvvvvv",
+        [pltpu.VMEM((planes, grid_p), jnp.float32)],
+    )(
+        own_phi, pair_phi, own_parts, pair_parts, third_parts, fourth_parts, image, ward,
+        correlation,
+    )
+    given = lax.ppermute(first, "orb", swap)
+    sent2 = lax.ppermute(second, "orb", [(i, i ^ 2) for i in range(4)])
+    sent3 = lax.ppermute(last, "orb", across)
+    third_held, fourth_held = call(outer_split_kernel, (parts, parts), "vvv")(
+        third_out, fourth_out, live
+    )
+    given, third_held = lax.optimization_barrier((given, third_held))
+    new, density = call(
+        last_kernel,
+        [block, share],
+        "vvvvvvvvvvv",
         [
-            pltpu.VMEM((planes, grid_p), jnp.float32),
             pltpu.VMEM(block.shape, jnp.float32),
-            pltpu.SemaphoreType.DMA,
+            pltpu.VMEM(share.shape, jnp.float32),
+            pltpu.SemaphoreType.DMA((2,)),
         ],
-        "vvvva",
+        "aa",
     )(
-        psi, pair, own_parts, pair_parts, third_parts, fourth_parts, image, ward, correlation,
-        extent, place,
-    )
-    given = lax.ppermute(pieces[1], "orb", outward)
-    sent = [
-        lax.ppermute(pieces[2], "orb", [(1, 3), (2, 0)]),
-        lax.ppermute(pieces[3], "orb", across),
-    ]
-    new = call(
-        outer_kernel,
-        block,
-        "vvvvvvvssa",
-        [pltpu.VMEM(parts.shape, parts.dtype)] * 2
-        + [pltpu.VMEM(block.shape, jnp.float32), pltpu.SemaphoreType.DMA],
-        "a",
-        {9: 0},
-    )(
-        psi, own_parts, pair_parts, third_out, fourth_out, image, given, extent, place, new
-    )
-    sent, kept = lax.optimization_barrier((sent, pieces[0], new))[:2]
-    density = call(sum_kernel, share, "vvvv")(kept, *sent, given)
+        own_phi, own_parts, pair_parts, third_held, fourth_held, image, given, kept, sent2, sent3,
+        inner_new,
+    )
     return (new, density)
 
 

time: 52 us -> 50.3 us (0.967)
  starting transfers between devices: 16.2 us -> 28.3 us
  waiting for transfers between devices: 20.5 us -> 11.8 us
  Pallas kernels: 10.9 us -> 6.46 us
  local copies, waits for them, and re-layouts: 3.2 us -> 2.62 us
    ppermute x5, starting transfers between devices: 5.82 us -> 17.5 us  [the longest x1 7.39 us: line_device(): fourth_out = lax.ppermute(fourth, 'orb', swap)]
    ppermute x1, waiting for transfers between devices: 4.93 us -> 0.01 us  [line_device(): pair_far = lax.ppermute(pair, 'cmp', to_far)]
    pallas_call x10 -> x11, Pallas kernels: 9.16 us -> 4.69 us  [the longest x1 1.8 us: line_device(): call(last_kernel, [block, share], 'vvvvvvvvvvv', [pltpu.VMEM(block.shape,...]
    ppermute x5, waiting for transfers between devices: 6.39 us -> 3.8 us  [the longest x1 2.67 us: line_device(): fourth_out = lax.ppermute(fourth, 'orb', swap)]
    ppermute x3, waiting for transfers between devices: 3.36 us -> 1.96 us  [line_device(): lax.ppermute(part, 'cmp', [(i, i ^ k) for i in range(n_cmp)])]
    ppermute x1, starting transfers between devices: 0.69 us -> 1.83 us  [line_device(): third = lax.ppermute(psi, 'orb', across)]
    unnamed x16 -> x12, local copies, waits for them, and re-layouts: 3.2 us -> 2.62 us
  transfers between devices with their start and end apart: 15 -> 15, of which waited for: 5 -> 6; matrix products, arithmetic and copies ran while one was open for 0% -> 0% of each run, Pallas kernels for 20% -> 9%
where the time goes in v4:
time: 50.3 us; the launch traced here: 50 us
  starting transfers between devices  28.3 us (56%)
  waiting for transfers between devices  11.8 us (23%)
  Pallas kernels  6.46 us (13%)
  local copies, waits for them, and re-layouts  2.62 us (5%)
  between operations  0.84 us (2%)
    ppermute x1, starting transfers between devices, line_device(): fourth_out = lax.ppermute(fourth, 'orb', swap)  7.39 us
    ppermute x1, waiting for transfers between devices, line_device(): pair = lax.ppermute(psi, 'orb', swap)  5.99 us
    ppermute x1, starting transfers between devices, line_device(): given = lax.ppermute(first, 'orb', swap)  5.08 us
    ppermute x1, starting transfers between devices, line_device(): third_out = lax.ppermute(third, 'orb', swap)  4.37 us
    ppermute x1, starting transfers between devices, line_device(): pair = lax.ppermute(psi, 'orb', swap)  3.09 us
    ppermute x1, waiting for transfers between devices, line_device(): fourth_out = lax.ppermute(fourth, 'orb', swap)  2.67 us
    unnamed x12, local copies, waits for them, and re-layouts  2.62 us
    ppermute x3, waiting for transfers between devices, line_device(): lax.ppermute(part, 'cmp', [(i, i ^ k) for i in range(n_cmp)])  1.96 us
  transfers between devices with their start and end apart: 15, of which 6 were waited for; matrix products, arithmetic and copies ran while one was open for 0% of the time, Pallas kernels for 9%

profile of v4, /device:TPU:0, one launch (start us, length us, event | category | flops | bytes accessed | tf_op | source)
XLA Modules:
  0.0 50.0 jit_solution(481455257210931877)
XLA Ops:
  0.6 0.0 copy-start.2
  0.6 3.1 %collective-permute-start = (f32[8,16,1024]{2,1,0:T(8,128)}, f32[8,16,1024]{2,1,0:T(8,128)S(1)}, u32[]{:S(2)}, u32[]{:S(2)}) collective-permute-start(f32[8,16,1024]{2,1,0:T(8,128)} %psi_ref.3), channel_id=1, source_target_pairs={{0,4},{4,0},{8,12},{12,8},{1,5},{5,1},{9,13},{13,9},{2,6},{6,2},{1... | collective-permute-start | bytes 1572872 | tf_op jit(solution)/shard_map/ppermute | solution.py:425
  3.7 0.0 copy-start.3
  3.7 0.0 collective-permute-start.4
  3.7 1.8 %collective-permute-start.1 = (f32[8,16,1024]{2,1,0:T(8,128)}, f32[8,16,1024]{2,1,0:T(8,128)S(1)}, u32[]{:S(2)}, u32[]{:S(2)}) collective-permute-start(f32[8,16,1024]{2,1,0:T(8,128)} %psi_ref.3), channel_id=1, source_target_pairs={{4,8},{8,4},{0,0},{12,12},{5,9},{9,5},{1,1},{13,13},{6,10},{10,6},... | collective-permute-start | bytes 1572872 | tf_op jit(solution)/shard_map/ppermute | solution.py:426
  5.6 1.5 %collective-permute-start.3 = (f32[8,16,1024]{2,1,0:T(8,128)}, f32[8,16,1024]{2,1,0:T(8,128)S(1)}, u32[]{:S(2)}, u32[]{:S(2)}) collective-permute-start(f32[8,16,1024]{2,1,0:T(8,128)} %psi_ref.3), channel_id=1, source_target_pairs={{0,3},{1,2},{2,1},{3,0},{4,7},{5,6},{6,5},{7,4},{8,11},{9,10},{10,... | collective-permute-start | bytes 1572872 | tf_op jit(solution)/shard_map/ppermute | solution.py:430
  7.0 0.0 copy-start.5
  7.0 0.7 %copy-done.5 = s32[32]{0:T(128)S(1)} copy-done((s32[32]{0:T(128)S(1)}, s32[32]{0:T(128)}, u32[]{:S(2)}) %copy-start.5) | copy-done | bytes 152
  7.7 0.6 %shard_map.69.live_ref = f32[32,1024]{1,0:T(8,128)S(1)} custom-call(s32[8,1024]{1,0:T(8,128)S(1)} %shard_map.68.columns_ref, s32[32]{0:T(128)S(1)} %copy-done.5), custom_call_target="tpu_custom_call" | custom-call | flops 1 | bytes 1 | tf_op jit(solution)/shard_map/pallas_call | solution.py:432
  8.3 0.0 copy-done.2
  8.3 0.0 copy-done.3
  8.3 0.0 copy-start
  8.3 1.0 %copy-done = f32[8,16,1024]{2,1,0:T(8,128)S(1)} copy-done((f32[8,16,1024]{2,1,0:T(8,128)S(1)}, f32[8,16,1024]{2,1,0:T(8,128)}, u32[]{:S(2)}) %copy-start) | copy-done | bytes 524312
  9.3 0.5 %shard_map.70 = (f32[8,16,1024]{2,1,0:T(8,128)S(1)}, bf16[256,1024]{1,0:T(8,128)(2,1)S(1)}, f32[128,1024]{1,0:T(8,128)S(1)}) custom-call(f32[8,16,1024]{2,1,0:T(8,128)S(1)} %copy-done, f32[16,1024]{1,0:T(8,128)S(1)} %copy-done.3, f32[32,1024]{1,0:T(8,128)S(1)} %shard_map.69.live_ref, bf16[256,256]{1,0:T(8,128)(2,1)S(1)} %copy-done.2), custom_call_target="tpu_custom_call" | custom-call | flops 1 | bytes 1 | tf_op jit(solution)/shard_map/pallas_call | solution.py:435
  9.9 6.0 %collective-permute-done.psi_ref = f32[8,16,1024]{2,1,0:T(8,128)S(1)} collective-permute-done((f32[8,16,1024]{2,1,0:T(8,128)}, f32[8,16,1024]{2,1,0:T(8,128)S(1)}, u32[]{:S(2)}, u32[]{:S(2)}) %collective-permute-start) | collective-permute-done | bytes 524320 | tf_op jit(solution)/shard_map/ppermute | solution.py:425
  15.9 0.7 %collective-permute-start.2 = (f32[8,16,1024]{2,1,0:T(8,128)S(1)}, f32[8,16,1024]{2,1,0:T(8,128)S(1)}, u32[]{:S(2)}, u32[]{:S(2)}) collective-permute-start(f32[8,16,1024]{2,1,0:T(8,128)S(1)} %collective-permute-done.psi_ref), channel_id=1, source_target_pairs={{4,8},{8,4},{0,0},{12,12},{5,9},{9,5},{1,1},{13,13},{6,10},{10,6},... | collective-permute-start | bytes 1572872 | tf_op jit(solution)/shard_map/ppermute | solution.py:441
  16.6 0.1 collective-permute-start.6
  16.6 0.0 collective-permute-done.4.near_ref
  16.6 1.8 %collective-permute-start.5 = (f32[8,16,1024]{2,1,0:T(8,128)S(1)}, f32[8,16,1024]{2,1,0:T(8,128)S(1)}, u32[]{:S(2)}, u32[]{:S(2)}) collective-permute-start(f32[8,16,1024]{2,1,0:T(8,128)S(1)} %collective-permute-done.psi_ref), channel_id=1, source_target_pairs={{0,3},{1,2},{2,1},{3,0},{4,7},{5,6},{6,5},{7,4},{8,11},{9,10},{10,... | collective-permute-start | bytes 1572872 | tf_op jit(solution)/shard_map/ppermute | solution.py:439
  18.4 0.0 collective-permute-done.1.field_ref
  18.4 4.4 %collective-permute-start.10 = (f32[8,16,1024]{2,1,0:T(8,128)S(1)}, f32[8,16,1024]{2,1,0:T(8,128)S(1)}, u32[]{:S(2)}, u32[]{:S(2)}) collective-permute-start(f32[8,16,1024]{2,1,0:T(8,128)S(1)} %collective-permute-done.1.field_ref), channel_id=1, source_target_pairs={{0,4},{4,0},{8,12},{12,8},{1,5},{5,1},{9,13},{13,9},{2,6},{6,2},{1... | collective-permute-start | bytes 1572872 | tf_op jit(solution)/shard_map/ppermute | solution.py:442
  22.8 0.5 %shard_map.71 = (f32[8,16,1024]{2,1,0:T(8,128)S(1)}, bf16[256,1024]{1,0:T(8,128)(2,1)S(1)}, f32[128,1024]{1,0:T(8,128)S(1)}) custom-call(f32[8,16,1024]{2,1,0:T(8,128)S(1)} %collective-permute-done.psi_ref, f32[16,1024]{1,0:T(8,128)S(1)} %copy-done.3, f32[32,1024]{1,0:T(8,128)S(1)} %shard_map.69.live_ref, bf16[256,256]{1,0:T(8,128)(2,1)S(1)} %copy-done.2), custom_call_target="tpu_custom_call" | custom-call | flops 1 | bytes 1 | tf_op jit(solution)/shard_map/pallas_call | solution.py:447
  23.3 0.0 copy-start.1
  23.3 0.0 copy-start.4
  23.3 0.1 shard_map.72.refs_2_.third_ref.third_parts
  23.4 0.0 collective-permute-done.3.far_ref
  23.4 0.9 %copy-done.1 = f32[8,16,1024]{2,1,0:T(8,128)S(1)} copy-done((f32[8,16,1024]{2,1,0:T(8,128)S(1)}, f32[8,16,1024]{2,1,0:T(8,128)}, u32[]{:S(2)}) %copy-start.1) | copy-done | bytes 524312
  24.4 0.0 copy-done.4
  24.4 0.4 shard_map.73
  24.8 0.6 %shard_map.74.early_ref = f32[24,128]{1,0:T(8,128)S(1)} custom-call(bf16[256,1024]{1,0:T(8,128)(2,1)S(1)} %get-tuple-element.35.refs_0_.own_ref.own_parts, bf16[256,1024]{1,0:T(8,128)(2,1)S(1)} %get-tuple-element.37.refs_1_.pair_ref.pair_parts, bf16[256,1024]{1,0:T(8,128)(2,1)S(1)} %shard_map.72.refs_2_.third_ref.third_parts, ...), custom_call_target="tpu_custom_call" | custom-call | flops 1 | bytes 1 | tf_op jit(solution)/shard_map/pallas_call | solution.py:451
  25.4 0.0 collective-permute-done.2.field_ref
  25.4 7.4 %collective-permute-start.12 = (f32[8,16,1024]{2,1,0:T(8,128)S(1)}, f32[8,16,1024]{2,1,0:T(8,128)S(1)}, u32[]{:S(2)}, u32[]{:S(2)}) collective-permute-start(f32[8,16,1024]{2,1,0:T(8,128)S(1)} %collective-permute-done.2.field_ref), channel_id=1, source_target_pairs={{0,4},{4,0},{8,12},{12,8},{1,5},{5,1},{9,13},{13,9},{2,6},{6,2},{1... | collective-permute-start | bytes 1572872 | tf_op jit(solution)/shard_map/ppermute | solution.py:458
  32.8 0.1 shard_map.75.fourth_ref.fourth_parts
  32.9 0.0 collective-permute-done.6.near_ref
  32.9 0.0 collective-permute-done.5.far_ref
  32.9 0.4 shard_map.76
  33.4 1.1 %shard_map.77.refs_0_ = f32[32,16]{1,0:T(8,128)S(1)} custom-call(bf16[256,1024]{1,0:T(8,128)(2,1)S(1)} %get-tuple-element.35.refs_0_.own_ref.own_parts, bf16[256,1024]{1,0:T(8,128)(2,1)S(1)} %get-tuple-element.37.refs_1_.pair_ref.pair_parts, bf16[256,1024]{1,0:T(8,128)(2,1)S(1)} %shard_map.72.refs_2_.third_ref.third_parts, ...), custom_call_target="tpu_custom_call" | custom-call | flops 1 | bytes 1 | tf_op jit(solution)/shard_map/pallas_call | solution.py:463
  34.5 0.1 collective-permute-start.9
  34.6 1.5 %collective-permute-start.8 = (f32[32,16]{1,0:T(8,128)S(1)}, f32[32,16]{1,0:T(8,128)S(1)}, u32[]{:S(2)}, u32[]{:S(2)}) collective-permute-start(f32[32,16]{1,0:T(8,128)S(1)} %shard_map.77.refs_0_), channel_id=1, source_target_pairs={{0,2},{1,3},{2,0},{3,1},{4,6},{5,7},{6,4},{7,5},{8,10},{9,11},{10,... | collective-permute-start | bytes 6152 | tf_op jit(solution)/shard_map/ppermute | solution.py:468
  36.2 0.3 collective-permute-start.7
  36.5 1.4 %collective-permute-done.9.refs_3_ = f32[32,16]{1,0:T(8,128)S(1)} collective-permute-done((f32[32,16]{1,0:T(8,128)S(1)}, f32[32,16]{1,0:T(8,128)S(1)}, u32[]{:S(2)}, u32[]{:S(2)}) %collective-permute-start.9) | collective-permute-done | bytes 2080 | tf_op jit(solution)/shard_map/ppermute | solution.py:468
  37.9 0.5 %collective-permute-done.8.refs_2_ = f32[32,16]{1,0:T(8,128)S(1)} collective-permute-done((f32[32,16]{1,0:T(8,128)S(1)}, f32[32,16]{1,0:T(8,128)S(1)}, u32[]{:S(2)}, u32[]{:S(2)}) %collective-permute-start.8) | collective-permute-done | bytes 2080 | tf_op jit(solution)/shard_map/ppermute | solution.py:468
  38.4 0.0 collective-permute-done.7.refs_1_
  38.4 0.0 collective-permute-done.10.third_ref
  38.5 5.1 %collective-permute-start.11 = (f32[48,256]{1,0:T(8,128)S(1)}, f32[48,256]{1,0:T(8,128)S(1)}, u32[]{:S(2)}, u32[]{:S(2)}) collective-permute-start(f32[48,256]{1,0:T(8,128)S(1)} %get-tuple-element.50), channel_id=1, source_target_pairs={{0,4},{4,0},{8,12},{12,8},{1,5},{5,1},{9,13},{13,9},{2,6},{6,2},{1... | collective-permute-start | bytes 147464 | tf_op jit(solution)/shard_map/ppermute | solution.py:485
  43.5 0.0 collective-permute-start.13
  43.6 0.7 %collective-permute-start.14 = (f32[16,256]{1,0:T(8,128)S(1)}, f32[16,256]{1,0:T(8,128)S(1)}, u32[]{:S(2)}, u32[]{:S(2)}) collective-permute-start(f32[16,256]{1,0:T(8,128)S(1)} %get-tuple-element.58), channel_id=1, source_target_pairs={{4,8},{8,4},{0,0},{12,12},{5,9},{9,5},{1,1},{13,13},{6,10},{10,6},... | collective-permute-start | bytes 49160 | tf_op jit(solution)/shard_map/ppermute | solution.py:487
  44.2 2.7 %collective-permute-done.12.fourth_ref = f32[8,16,1024]{2,1,0:T(8,128)S(1)} collective-permute-done((f32[8,16,1024]{2,1,0:T(8,128)S(1)}, f32[8,16,1024]{2,1,0:T(8,128)S(1)}, u32[]{:S(2)}, u32[]{:S(2)}) %collective-permute-start.12) | collective-permute-done | bytes 524320 | tf_op jit(solution)/shard_map/ppermute | solution.py:458
  46.9 0.2 shard_map.80
  47.1 0.3 collective-permute-done.11.given_ref
  47.4 0.8 %collective-permute-done.13.sent2_ref = f32[16,256]{1,0:T(8,128)S(1)} collective-permute-done((f32[16,256]{1,0:T(8,128)S(1)}, f32[16,256]{1,0:T(8,128)S(1)}, u32[]{:S(2)}, u32[]{:S(2)}) %collective-permute-start.13) | collective-permute-done | bytes 16416 | tf_op jit(solution)/shard_map/ppermute | solution.py:486
  48.2 0.0 collective-permute-done.14.sent3_ref
  48.2 1.8 %shard_map.81 = (f32[8,16,1024]{2,1,0:T(8,128)}, f32[16,256]{1,0:T(8,128)}) custom-call(f32[128,1024]{1,0:T(8,128)S(1)} %get-tuple-element.32.own_phi, bf16[256,1024]{1,0:T(8,128)(2,1)S(1)} %get-tuple-element.35.refs_0_.own_ref.own_parts, bf16[256,1024]{1,0:T(8,128)(2,1)S(1)} %get-tuple-element.37.refs_1_.pair_ref.pair_parts, ...), custom_call_target="tpu_custom_call" | custom-call | flops 1 | bytes 1 | tf_op jit(solution)/shard_map/pallas_call | solution.py:492
  (3 shorter events, 0.0 us)
Async XLA Ops:
  0.6 7.7 %copy-start.2 = (bf16[256,256]{1,0:T(8,128)(2,1)S(1)}, bf16[256,256]{1,0:T(8,128)(2,1)}, u32[]{:S(2)}) copy-start(bf16[256,256]{1,0:T(8,128)(2,1)} %constant.4.clone.band_ref) | copy-start | bytes 393220
  0.6 15.2 %collective-permute-start = (f32[8,16,1024]{2,1,0:T(8,128)}, f32[8,16,1024]{2,1,0:T(8,128)S(1)}, u32[]{:S(2)}, u32[]{:S(2)}) collective-permute-start(f32[8,16,1024]{2,1,0:T(8,128)} %psi_ref.3), channel_id=1, source_target_pairs={{0,4},{4,0},{8,12},{12,8},{1,5},{5,1},{9,13},{13,9},{2,6},{6,2},{1... | collective-permute-start | bytes 1572872 | tf_op jit(solution)/shard_map/ppermute | solution.py:425
  3.7 4.6 %copy-start.3 = (f32[16,1024]{1,0:T(8,128)S(1)}, f32[16,1024]{1,0:T(8,128)}, u32[]{:S(2)}) copy-start(f32[16,1024]{1,0:T(8,128)} %potential_ref.3) | copy-start | bytes 196612
  3.7 12.9 %collective-permute-start.4 = (f32[8,16,1024]{2,1,0:T(8,128)}, f32[8,16,1024]{2,1,0:T(8,128)S(1)}, u32[]{:S(2)}, u32[]{:S(2)}) collective-permute-start(f32[8,16,1024]{2,1,0:T(8,128)} %psi_ref.3), channel_id=1, source_target_pairs={{0,1},{1,0},{2,3},{3,2},{4,5},{5,4},{6,7},{7,6},{8,9},{9,8},{10,11... | collective-permute-start | bytes 1572872 | tf_op jit(solution)/shard_map/ppermute | solution.py:429
  3.7 14.7 %collective-permute-start.1 = (f32[8,16,1024]{2,1,0:T(8,128)}, f32[8,16,1024]{2,1,0:T(8,128)S(1)}, u32[]{:S(2)}, u32[]{:S(2)}) collective-permute-start(f32[8,16,1024]{2,1,0:T(8,128)} %psi_ref.3), channel_id=1, source_target_pairs={{4,8},{8,4},{0,0},{12,12},{5,9},{9,5},{1,1},{13,13},{6,10},{10,6},... | collective-permute-start | bytes 1572872 | tf_op jit(solution)/shard_map/ppermute | solution.py:426
  5.6 17.9 %collective-permute-start.3 = (f32[8,16,1024]{2,1,0:T(8,128)}, f32[8,16,1024]{2,1,0:T(8,128)S(1)}, u32[]{:S(2)}, u32[]{:S(2)}) collective-permute-start(f32[8,16,1024]{2,1,0:T(8,128)} %psi_ref.3), channel_id=1, source_target_pairs={{0,3},{1,2},{2,1},{3,0},{4,7},{5,6},{6,5},{7,4},{8,11},{9,10},{10,... | collective-permute-start | bytes 1572872 | tf_op jit(solution)/shard_map/ppermute | solution.py:430
  7.0 0.7 %copy-start.5 = (s32[32]{0:T(128)S(1)}, s32[32]{0:T(128)}, u32[]{:S(2)}) copy-start(s32[32]{0:T(128)} %extent_ref.1) | copy-start | bytes 388
  8.3 1.0 %copy-start = (f32[8,16,1024]{2,1,0:T(8,128)S(1)}, f32[8,16,1024]{2,1,0:T(8,128)}, u32[]{:S(2)}) copy-start(f32[8,16,1024]{2,1,0:T(8,128)} %psi_ref.3) | copy-start | bytes 1572868
  15.9 9.6 %collective-permute-start.2 = (f32[8,16,1024]{2,1,0:T(8,128)S(1)}, f32[8,16,1024]{2,1,0:T(8,128)S(1)}, u32[]{:S(2)}, u32[]{:S(2)}) collective-permute-start(f32[8,16,1024]{2,1,0:T(8,128)S(1)} %collective-permute-done.psi_ref), channel_id=1, source_target_pairs={{4,8},{8,4},{0,0},{12,12},{5,9},{9,5},{1,1},{13,13},{6,10},{10,6},... | collective-permute-start | bytes 1572872 | tf_op jit(solution)/shard_map/ppermute | solution.py:441
  16.6 16.4 %collective-permute-start.6 = (f32[8,16,1024]{2,1,0:T(8,128)S(1)}, f32[8,16,1024]{2,1,0:T(8,128)S(1)}, u32[]{:S(2)}, u32[]{:S(2)}) collective-permute-start(f32[8,16,1024]{2,1,0:T(8,128)S(1)} %collective-permute-done.psi_ref), channel_id=1, source_target_pairs={{0,1},{1,0},{2,3},{3,2},{4,5},{5,4},{6,7},{7,6},{8,9},{9,8},{10,11... | collective-permute-start | bytes 1572872 | tf_op jit(solution)/shard_map/ppermute | solution.py:440
  16.6 16.3 %collective-permute-start.5 = (f32[8,16,1024]{2,1,0:T(8,128)S(1)}, f32[8,16,1024]{2,1,0:T(8,128)S(1)}, u32[]{:S(2)}, u32[]{:S(2)}) collective-permute-start(f32[8,16,1024]{2,1,0:T(8,128)S(1)} %collective-permute-done.psi_ref), channel_id=1, source_target_pairs={{0,3},{1,2},{2,1},{3,0},{4,7},{5,6},{6,5},{7,4},{8,11},{9,10},{10,... | collective-permute-start | bytes 1572872 | tf_op jit(solution)/shard_map/ppermute | solution.py:439
  18.4 20.0 %collective-permute-start.10 = (f32[8,16,1024]{2,1,0:T(8,128)S(1)}, f32[8,16,1024]{2,1,0:T(8,128)S(1)}, u32[]{:S(2)}, u32[]{:S(2)}) collective-permute-start(f32[8,16,1024]{2,1,0:T(8,128)S(1)} %collective-permute-done.1.field_ref), channel_id=1, source_target_pairs={{0,4},{4,0},{8,12},{12,8},{1,5},{5,1},{9,13},{13,9},{2,6},{6,2},{1... | collective-permute-start | bytes 1572872 | tf_op jit(solution)/shard_map/ppermute | solution.py:442
  23.3 1.0 %copy-start.1 = (f32[8,16,1024]{2,1,0:T(8,128)S(1)}, f32[8,16,1024]{2,1,0:T(8,128)}, u32[]{:S(2)}) copy-start(f32[8,16,1024]{2,1,0:T(8,128)} %psi_ref.3) | copy-start | bytes 1572868
  23.3 1.0 %copy-start.4 = (bf16[2,16,144]{2,1,0:T(8,128)(2,1)S(1)}, bf16[2,16,144]{2,1,0:T(8,128)(2,1)}, u32[]{:S(2)}) copy-start(bf16[2,16,144]{2,1,0:T(8,128)(2,1)} %constant.5.clone.band_ref) | copy-start | bytes 27652
  25.4 21.4 %collective-permute-start.12 = (f32[8,16,1024]{2,1,0:T(8,128)S(1)}, f32[8,16,1024]{2,1,0:T(8,128)S(1)}, u32[]{:S(2)}, u32[]{:S(2)}) collective-permute-start(f32[8,16,1024]{2,1,0:T(8,128)S(1)} %collective-permute-done.2.field_ref), channel_id=1, source_target_pairs={{0,4},{4,0},{8,12},{12,8},{1,5},{5,1},{9,13},{13,9},{2,6},{6,2},{1... | collective-permute-start | bytes 1572872 | tf_op jit(solution)/shard_map/ppermute | solution.py:458
  34.5 3.4 %collective-permute-start.9 = (f32[32,16]{1,0:T(8,128)S(1)}, f32[32,16]{1,0:T(8,128)S(1)}, u32[]{:S(2)}, u32[]{:S(2)}) collective-permute-start(f32[32,16]{1,0:T(8,128)S(1)} %shard_map.77.refs_0_), channel_id=1, source_target_pairs={{0,3},{1,2},{2,1},{3,0},{4,7},{5,6},{6,5},{7,4},{8,11},{9,10},{10,... | collective-permute-start | bytes 6152 | tf_op jit(solution)/shard_map/ppermute | solution.py:468
  34.6 3.8 %collective-permute-start.8 = (f32[32,16]{1,0:T(8,128)S(1)}, f32[32,16]{1,0:T(8,128)S(1)}, u32[]{:S(2)}, u32[]{:S(2)}) collective-permute-start(f32[32,16]{1,0:T(8,128)S(1)} %shard_map.77.refs_0_), channel_id=1, source_target_pairs={{0,2},{1,3},{2,0},{3,1},{4,6},{5,7},{6,4},{7,5},{8,10},{9,11},{10,... | collective-permute-start | bytes 6152 | tf_op jit(solution)/shard_map/ppermute | solution.py:468
  36.2 2.3 %collective-permute-start.7 = (f32[32,16]{1,0:T(8,128)S(1)}, f32[32,16]{1,0:T(8,128)S(1)}, u32[]{:S(2)}, u32[]{:S(2)}) collective-permute-start(f32[32,16]{1,0:T(8,128)S(1)} %shard_map.77.refs_0_), channel_id=1, source_target_pairs={{0,1},{1,0},{2,3},{3,2},{4,5},{5,4},{6,7},{7,6},{8,9},{9,8},{10,11... | collective-permute-start | bytes 6152 | tf_op jit(solution)/shard_map/ppermute | solution.py:468
  38.5 8.9 %collective-permute-start.11 = (f32[48,256]{1,0:T(8,128)S(1)}, f32[48,256]{1,0:T(8,128)S(1)}, u32[]{:S(2)}, u32[]{:S(2)}) collective-permute-start(f32[48,256]{1,0:T(8,128)S(1)} %get-tuple-element.50), channel_id=1, source_target_pairs={{0,4},{4,0},{8,12},{12,8},{1,5},{5,1},{9,13},{13,9},{2,6},{6,2},{1... | collective-permute-start | bytes 147464 | tf_op jit(solution)/shard_map/ppermute | solution.py:485
  43.5 4.6 %collective-permute-start.13 = (f32[16,256]{1,0:T(8,128)S(1)}, f32[16,256]{1,0:T(8,128)S(1)}, u32[]{:S(2)}, u32[]{:S(2)}) collective-permute-start(f32[16,256]{1,0:T(8,128)S(1)} %get-tuple-element.57), channel_id=1, source_target_pairs={{0,8},{4,12},{8,0},{12,4},{1,9},{5,13},{9,1},{13,5},{2,10},{6,14},... | collective-permute-start | bytes 49160 | tf_op jit(solution)/shard_map/ppermute | solution.py:486
  43.6 4.6 %collective-permute-start.14 = (f32[16,256]{1,0:T(8,128)S(1)}, f32[16,256]{1,0:T(8,128)S(1)}, u32[]{:S(2)}, u32[]{:S(2)}) collective-permute-start(f32[16,256]{1,0:T(8,128)S(1)} %get-tuple-element.58), channel_id=1, source_target_pairs={{4,8},{8,4},{0,0},{12,12},{5,9},{9,5},{1,1},{13,13},{6,10},{10,6},... | collective-permute-start | bytes 49160 | tf_op jit(solution)/shard_map/ppermute | solution.py:487

commit v5 on v4

--- a/solution.py
+++ b/solution.py
@@ -436,10 +436,12 @@
         functools.partial(local_kernel, 0), (block, parts, flat), "vvvv"
     )(psi, potential, live, columns)
     pair, local, own_parts = lax.optimization_barrier((pair, local, own_parts))
-    pair_far = lax.ppermute(pair, "cmp", to_far)
-    pair_near = lax.ppermute(pair, "cmp", to_near)
     fourth = lax.ppermute(pair, "orb", across)
     third_out = lax.ppermute(third, "orb", swap)
+    third_parts = call(functools.partial(split_kernel, 2), parts, "vv")(third, live)
+    turn, third_parts = lax.optimization_barrier((pair, third_parts))
+    pair_far = lax.ppermute(turn, "cmp", to_far)
+    pair_near = lax.ppermute(pair, "cmp", to_near)
 
     image, image_parts = call(functools.partial(plane_kernel, 0), (block, parts), "vvvvvv")(
         far, psi, near, local, live, bands
@@ -447,7 +449,6 @@
     ward_local, pair_parts, pair_phi = call(
         functools.partial(local_kernel, 1), (block, parts, flat), "vvvv"
     )(pair, potential, live, columns)
-    third_parts = call(functools.partial(split_kernel, 2), parts, "vv")(third, live)
     early = call(
         functools.partial(overlap_kernel, planes, 3),
         jax.ShapeDtypeStruct((3 * orbs, rows), jnp.float32),
@@ -465,10 +466,9 @@
         jax.ShapeDtypeStruct((4 * orbs, 2 * orbs), jnp.float32),
         "vvvvvvv",
     )(own_parts, pair_parts, third_parts, fourth_parts, image_parts, ward_parts, early)
-    shares = [lax.ppermute(part, "cmp", [(i, i ^ k) for i in range(n_cmp)]) for k in (1, 2, 3)]
-    correlation = call(sum_kernel, jax.ShapeDtypeStruct(part.shape, jnp.float32), "vvvv")(
-        part, *shares
-    )
+    small = jax.ShapeDtypeStruct(part.shape, jnp.float32)
+    chip = call(sum_kernel, small, "vv")(part, lax.ppermute(part, "cmp", to_near))
+    correlation = call(sum_kernel, small, "vv")(chip, lax.ppermute(chip, "cmp", to_far))
     correlation, third_out = lax.optimization_barrier((correlation, third_out))
 
     share = jax.ShapeDtypeStruct((planes, grid_p // 4), jnp.float32)

time: 50.3 us -> 49.7 us (0.988)
  local copies, waits for them, and re-layouts: 2.62 us -> 1.72 us
    ppermute x4 -> x3, starting transfers between devices: 3.68 us -> 1.62 us  [the longest x1 1.26 us: line_device(): lax.ppermute(chip, 'cmp', to_far)]
    ppermute x1, starting transfers between devices: 0.07 us -> 1.55 us  [line_device(): pair_near = lax.ppermute(pair, 'cmp', to_near)]
    ppermute x4 -> x3, waiting for transfers between devices: 1.96 us -> 3.08 us  [the longest x1 1.9 us: line_device(): lax.ppermute(chip, 'cmp', to_far)]
    unnamed x12, local copies, waits for them, and re-layouts: 2.62 us -> 1.72 us
    ppermute x1, starting transfers between devices: 0.01 us -> 0.77 us  [line_device(): sent2 = lax.ppermute(second, 'orb', [(i, i ^ 2) for i in range(4)])]
    ppermute x1, waiting for transfers between devices: 0.78 us -> 0.16 us  [line_device(): sent2 = lax.ppermute(second, 'orb', [(i, i ^ 2) for i in range(4)])]
    ppermute x1, starting transfers between devices: 5.08 us -> 4.52 us  [line_device(): given = lax.ppermute(first, 'orb', swap)]
  transfers between devices with their start and end apart: 15 -> 14, of which waited for: 6 -> 6; matrix products, arithmetic and copies ran while one was open for 0% -> 0% of each run, Pallas kernels for 9% -> 9%
where the time goes in v5:
time: 49.7 us; the launch traced here: 49.4 us
  starting transfers between devices  28.3 us (57%)
  waiting for transfers between devices  12.1 us (24%)
  Pallas kernels  6.45 us (13%)
  local copies, waits for them, and re-layouts  1.72 us (3%)
  between operations  0.84 us (2%)
    ppermute x1, starting transfers between devices, line_device(): fourth_out = lax.ppermute(fourth, 'orb', swap)  7.75 us
    ppermute x1, waiting for transfers between devices, line_device(): pair = lax.ppermute(psi, 'orb', swap)  5.99 us
    ppermute x1, starting transfers between devices, line_device(): given = lax.ppermute(first, 'orb', swap)  4.52 us
    ppermute x1, starting transfers between devices, line_device(): third_out = lax.ppermute(third, 'orb', swap)  4.37 us
    ppermute x1, starting transfers between devices, line_device(): pair = lax.ppermute(psi, 'orb', swap)  3.09 us
    ppermute x1, waiting for transfers between devices, line_device(): fourth_out = lax.ppermute(fourth, 'orb', swap)  2.54 us
    ppermute x1, waiting for transfers between devices, line_device(): lax.ppermute(chip, 'cmp', to_far)  1.9 us
    pallas_call x1, Pallas kernels, line_device(): call(last_kernel, [block, share], 'vvvvvvvvvvv', [pltpu.VMEM(block.shape,...  1.8 us
  transfers between devices with their start and end apart: 14, of which 6 were waited for; matrix products, arithmetic and copies ran while one was open for 0% of the time, Pallas kernels for 9%

profile of v5, /device:TPU:0, one launch (start us, length us, event | category | flops | bytes accessed | tf_op | source)
XLA Modules:
  0.0 49.4 jit_solution(9904880513053119346)
XLA Ops:
  0.6 0.0 copy-start.2
  0.6 3.1 %collective-permute-start = (f32[8,16,1024]{2,1,0:T(8,128)}, f32[8,16,1024]{2,1,0:T(8,128)S(1)}, u32[]{:S(2)}, u32[]{:S(2)}) collective-permute-start(f32[8,16,1024]{2,1,0:T(8,128)} %psi_ref.3), channel_id=1, source_target_pairs={{0,4},{4,0},{8,12},{12,8},{1,5},{5,1},{9,13},{13,9},{2,6},{6,2},{1... | collective-permute-start | bytes 1572872 | tf_op jit(solution)/shard_map/ppermute | solution.py:425
  3.7 1.7 %collective-permute-start.1 = (f32[8,16,1024]{2,1,0:T(8,128)}, f32[8,16,1024]{2,1,0:T(8,128)S(1)}, u32[]{:S(2)}, u32[]{:S(2)}) collective-permute-start(f32[8,16,1024]{2,1,0:T(8,128)} %psi_ref.3), channel_id=1, source_target_pairs={{4,8},{8,4},{0,0},{12,12},{5,9},{9,5},{1,1},{13,13},{6,10},{10,6},... | collective-permute-start | bytes 1572872 | tf_op jit(solution)/shard_map/ppermute | solution.py:426
  5.4 0.0 copy-start.3
  5.4 0.0 collective-permute-start.4
  5.4 1.6 %collective-permute-start.3 = (f32[8,16,1024]{2,1,0:T(8,128)}, f32[8,16,1024]{2,1,0:T(8,128)S(1)}, u32[]{:S(2)}, u32[]{:S(2)}) collective-permute-start(f32[8,16,1024]{2,1,0:T(8,128)} %psi_ref.3), channel_id=1, source_target_pairs={{0,3},{1,2},{2,1},{3,0},{4,7},{5,6},{6,5},{7,4},{8,11},{9,10},{10,... | collective-permute-start | bytes 1572872 | tf_op jit(solution)/shard_map/ppermute | solution.py:430
  7.0 0.0 copy-start.5
  7.0 0.7 %copy-done.5 = s32[32]{0:T(128)S(1)} copy-done((s32[32]{0:T(128)S(1)}, s32[32]{0:T(128)}, u32[]{:S(2)}) %copy-start.5) | copy-done | bytes 152
  7.7 0.6 %shard_map.69.live_ref = f32[32,1024]{1,0:T(8,128)S(1)} custom-call(s32[8,1024]{1,0:T(8,128)S(1)} %shard_map.68.columns_ref, s32[32]{0:T(128)S(1)} %copy-done.5), custom_call_target="tpu_custom_call" | custom-call | flops 1 | bytes 1 | tf_op jit(solution)/shard_map/pallas_call | solution.py:432
  8.3 0.0 copy-done.2
  8.3 0.0 copy-done.3
  8.3 0.0 copy-start
  8.3 1.0 %copy-done = f32[8,16,1024]{2,1,0:T(8,128)S(1)} copy-done((f32[8,16,1024]{2,1,0:T(8,128)S(1)}, f32[8,16,1024]{2,1,0:T(8,128)}, u32[]{:S(2)}) %copy-start) | copy-done | bytes 524312
  9.3 0.5 %shard_map.70 = (f32[8,16,1024]{2,1,0:T(8,128)S(1)}, bf16[256,1024]{1,0:T(8,128)(2,1)S(1)}, f32[128,1024]{1,0:T(8,128)S(1)}) custom-call(f32[8,16,1024]{2,1,0:T(8,128)S(1)} %copy-done, f32[16,1024]{1,0:T(8,128)S(1)} %copy-done.3, f32[32,1024]{1,0:T(8,128)S(1)} %shard_map.69.live_ref, bf16[256,256]{1,0:T(8,128)(2,1)S(1)} %copy-done.2), custom_call_target="tpu_custom_call" | custom-call | flops 1 | bytes 1 | tf_op jit(solution)/shard_map/pallas_call | solution.py:435
  9.9 6.0 %collective-permute-done.psi_ref = f32[8,16,1024]{2,1,0:T(8,128)S(1)} collective-permute-done((f32[8,16,1024]{2,1,0:T(8,128)}, f32[8,16,1024]{2,1,0:T(8,128)S(1)}, u32[]{:S(2)}, u32[]{:S(2)}) %collective-permute-start) | collective-permute-done | bytes 524320 | tf_op jit(solution)/shard_map/ppermute | solution.py:425
  15.9 0.7 %collective-permute-start.2 = (f32[8,16,1024]{2,1,0:T(8,128)S(1)}, f32[8,16,1024]{2,1,0:T(8,128)S(1)}, u32[]{:S(2)}, u32[]{:S(2)}) collective-permute-start(f32[8,16,1024]{2,1,0:T(8,128)S(1)} %collective-permute-done.psi_ref), channel_id=1, source_target_pairs={{4,8},{8,4},{0,0},{12,12},{5,9},{9,5},{1,1},{13,13},{6,10},{10,6},... | collective-permute-start | bytes 1572872 | tf_op jit(solution)/shard_map/ppermute | solution.py:439
  16.6 0.0 collective-permute-done.1.field_ref
  16.6 0.1 shard_map.72.refs_2_.third_ref.third_parts
  16.7 0.0 copy-start.1
  16.7 0.0 copy-start.4
  16.7 0.3 collective-permute-start.5
  17.0 1.5 %collective-permute-start.6 = (f32[8,16,1024]{2,1,0:T(8,128)S(1)}, f32[8,16,1024]{2,1,0:T(8,128)S(1)}, u32[]{:S(2)}, u32[]{:S(2)}) collective-permute-start(f32[8,16,1024]{2,1,0:T(8,128)S(1)} %collective-permute-done.psi_ref), channel_id=1, source_target_pairs={{0,1},{1,0},{2,3},{3,2},{4,5},{5,4},{6,7},{7,6},{8,9},{9,8},{10,11... | collective-permute-start | bytes 1572872 | tf_op jit(solution)/shard_map/ppermute | solution.py:444
  18.5 0.0 collective-permute-done.4.near_ref
  18.5 4.4 %collective-permute-start.9 = (f32[8,16,1024]{2,1,0:T(8,128)S(1)}, f32[8,16,1024]{2,1,0:T(8,128)S(1)}, u32[]{:S(2)}, u32[]{:S(2)}) collective-permute-start(f32[8,16,1024]{2,1,0:T(8,128)S(1)} %collective-permute-done.1.field_ref), channel_id=1, source_target_pairs={{0,4},{4,0},{8,12},{12,8},{1,5},{5,1},{9,13},{13,9},{2,6},{6,2},{1... | collective-permute-start | bytes 1572872 | tf_op jit(solution)/shard_map/ppermute | solution.py:440
  22.9 0.5 %shard_map.71 = (f32[8,16,1024]{2,1,0:T(8,128)S(1)}, bf16[256,1024]{1,0:T(8,128)(2,1)S(1)}, f32[128,1024]{1,0:T(8,128)S(1)}) custom-call(f32[8,16,1024]{2,1,0:T(8,128)S(1)} %collective-permute-done.psi_ref, f32[16,1024]{1,0:T(8,128)S(1)} %copy-done.3, f32[32,1024]{1,0:T(8,128)S(1)} %shard_map.69.live_ref, bf16[256,256]{1,0:T(8,128)(2,1)S(1)} %copy-done.2), custom_call_target="tpu_custom_call" | custom-call | flops 1 | bytes 1 | tf_op jit(solution)/shard_map/pallas_call | solution.py:449
  23.4 0.0 collective-permute-done.3.far_ref
  23.4 0.0 copy-done.1
  23.4 0.0 copy-done.4
  23.5 0.4 shard_map.73
  23.9 0.6 %shard_map.74.early_ref = f32[24,128]{1,0:T(8,128)S(1)} custom-call(bf16[256,1024]{1,0:T(8,128)(2,1)S(1)} %get-tuple-element.37.refs_0_.own_ref.own_parts, bf16[256,1024]{1,0:T(8,128)(2,1)S(1)} %get-tuple-element.39.refs_1_.pair_ref.pair_parts, bf16[256,1024]{1,0:T(8,128)(2,1)S(1)} %shard_map.72.refs_2_.third_ref.third_parts, ...), custom_call_target="tpu_custom_call" | custom-call | flops 1 | bytes 1 | tf_op jit(solution)/shard_map/pallas_call | solution.py:452
  24.5 0.0 collective-permute-done.2.field_ref
  24.5 7.8 %collective-permute-start.11 = (f32[8,16,1024]{2,1,0:T(8,128)S(1)}, f32[8,16,1024]{2,1,0:T(8,128)S(1)}, u32[]{:S(2)}, u32[]{:S(2)}) collective-permute-start(f32[8,16,1024]{2,1,0:T(8,128)S(1)} %collective-permute-done.2.field_ref), channel_id=1, source_target_pairs={{0,4},{4,0},{8,12},{12,8},{1,5},{5,1},{9,13},{13,9},{2,6},{6,2},{1... | collective-permute-start | bytes 1572872 | tf_op jit(solution)/shard_map/ppermute | solution.py:459
  32.3 0.1 shard_map.75.fourth_ref.fourth_parts
  32.4 0.0 collective-permute-done.5.far_ref
  32.4 0.0 collective-permute-done.6.near_ref
  32.4 0.4 shard_map.76
  32.8 1.1 %shard_map.77.refs_0_ = f32[32,16]{1,0:T(8,128)S(1)} custom-call(bf16[256,1024]{1,0:T(8,128)(2,1)S(1)} %get-tuple-element.37.refs_0_.own_ref.own_parts, bf16[256,1024]{1,0:T(8,128)(2,1)S(1)} %get-tuple-element.39.refs_1_.pair_ref.pair_parts, bf16[256,1024]{1,0:T(8,128)(2,1)S(1)} %shard_map.72.refs_2_.third_ref.third_parts, ...), custom_call_target="tpu_custom_call" | custom-call | flops 1 | bytes 1 | tf_op jit(solution)/shard_map/pallas_call | solution.py:464
  34.0 0.1 collective-permute-start.7
  34.1 1.2 %collective-permute-done.7.refs_1_ = f32[32,16]{1,0:T(8,128)S(1)} collective-permute-done((f32[32,16]{1,0:T(8,128)S(1)}, f32[32,16]{1,0:T(8,128)S(1)}, u32[]{:S(2)}, u32[]{:S(2)}) %collective-permute-start.7) | collective-permute-done | bytes 2080 | tf_op jit(solution)/shard_map/ppermute | solution.py:470
  35.2 1.3 %collective-permute-start.8 = (f32[32,16]{1,0:T(8,128)S(1)}, f32[32,16]{1,0:T(8,128)S(1)}, u32[]{:S(2)}, u32[]{:S(2)}) collective-permute-start(f32[32,16]{1,0:T(8,128)S(1)} %shard_map.78.refs_0_), channel_id=1, source_target_pairs={{0,3},{1,2},{2,1},{3,0},{4,7},{5,6},{6,5},{7,4},{8,11},{9,10},{10,... | collective-permute-start | bytes 6152 | tf_op jit(solution)/shard_map/ppermute | solution.py:471
  36.5 1.9 %collective-permute-done.8.refs_1_ = f32[32,16]{1,0:T(8,128)S(1)} collective-permute-done((f32[32,16]{1,0:T(8,128)S(1)}, f32[32,16]{1,0:T(8,128)S(1)}, u32[]{:S(2)}, u32[]{:S(2)}) %collective-permute-start.8) | collective-permute-done | bytes 2080 | tf_op jit(solution)/shard_map/ppermute | solution.py:471
  38.4 0.0 collective-permute-done.9.third_ref
  38.4 4.5 %collective-permute-start.10 = (f32[48,256]{1,0:T(8,128)S(1)}, f32[48,256]{1,0:T(8,128)S(1)}, u32[]{:S(2)}, u32[]{:S(2)}) collective-permute-start(f32[48,256]{1,0:T(8,128)S(1)} %get-tuple-element.54), channel_id=1, source_target_pairs={{0,4},{4,0},{8,12},{12,8},{1,5},{5,1},{9,13},{13,9},{2,6},{6,2},{1... | collective-permute-start | bytes 147464 | tf_op jit(solution)/shard_map/ppermute | solution.py:485
  43.0 0.8 %collective-permute-start.12 = (f32[16,256]{1,0:T(8,128)S(1)}, f32[16,256]{1,0:T(8,128)S(1)}, u32[]{:S(2)}, u32[]{:S(2)}) collective-permute-start(f32[16,256]{1,0:T(8,128)S(1)} %get-tuple-element.61), channel_id=1, source_target_pairs={{0,8},{4,12},{8,0},{12,4},{1,9},{5,13},{9,1},{13,5},{2,10},{6,14},... | collective-permute-start | bytes 49160 | tf_op jit(solution)/shard_map/ppermute | solution.py:486
  43.7 0.7 %collective-permute-start.13 = (f32[16,256]{1,0:T(8,128)S(1)}, f32[16,256]{1,0:T(8,128)S(1)}, u32[]{:S(2)}, u32[]{:S(2)}) collective-permute-start(f32[16,256]{1,0:T(8,128)S(1)} %get-tuple-element.62), channel_id=1, source_target_pairs={{4,8},{8,4},{0,0},{12,12},{5,9},{9,5},{1,1},{13,13},{6,10},{10,6},... | collective-permute-start | bytes 49160 | tf_op jit(solution)/shard_map/ppermute | solution.py:487
  44.4 2.5 %collective-permute-done.11.fourth_ref = f32[8,16,1024]{2,1,0:T(8,128)S(1)} collective-permute-done((f32[8,16,1024]{2,1,0:T(8,128)S(1)}, f32[8,16,1024]{2,1,0:T(8,128)S(1)}, u32[]{:S(2)}, u32[]{:S(2)}) %collective-permute-start.11) | collective-permute-done | bytes 524320 | tf_op jit(solution)/shard_map/ppermute | solution.py:459
  46.9 0.2 shard_map.81
  47.1 0.4 collective-permute-done.10.given_ref
  47.5 0.2 collective-permute-done.12.sent2_ref
  47.6 0.0 collective-permute-done.13.sent3_ref
  47.6 1.8 %shard_map.82 = (f32[8,16,1024]{2,1,0:T(8,128)}, f32[16,256]{1,0:T(8,128)}) custom-call(f32[128,1024]{1,0:T(8,128)S(1)} %get-tuple-element.34.own_phi, bf16[256,1024]{1,0:T(8,128)(2,1)S(1)} %get-tuple-element.37.refs_0_.own_ref.own_parts, bf16[256,1024]{1,0:T(8,128)(2,1)S(1)} %get-tuple-element.39.refs_1_.pair_ref.pair_parts, ...), custom_call_target="tpu_custom_call" | custom-call | flops 1 | bytes 1 | tf_op jit(solution)/shard_map/pallas_call | solution.py:492
  (4 shorter events, 0.0 us)
Async XLA Ops:
  0.6 7.7 %copy-start.2 = (bf16[256,256]{1,0:T(8,128)(2,1)S(1)}, bf16[256,256]{1,0:T(8,128)(2,1)}, u32[]{:S(2)}) copy-start(bf16[256,256]{1,0:T(8,128)(2,1)} %constant.4.clone.band_ref) | copy-start | bytes 393220
  0.6 15.2 %collective-permute-start = (f32[8,16,1024]{2,1,0:T(8,128)}, f32[8,16,1024]{2,1,0:T(8,128)S(1)}, u32[]{:S(2)}, u32[]{:S(2)}) collective-permute-start(f32[8,16,1024]{2,1,0:T(8,128)} %psi_ref.3), channel_id=1, source_target_pairs={{0,4},{4,0},{8,12},{12,8},{1,5},{5,1},{9,13},{13,9},{2,6},{6,2},{1... | collective-permute-start | bytes 1572872 | tf_op jit(solution)/shard_map/ppermute | solution.py:425
  3.7 12.8 %collective-permute-start.1 = (f32[8,16,1024]{2,1,0:T(8,128)}, f32[8,16,1024]{2,1,0:T(8,128)S(1)}, u32[]{:S(2)}, u32[]{:S(2)}) collective-permute-start(f32[8,16,1024]{2,1,0:T(8,128)} %psi_ref.3), channel_id=1, source_target_pairs={{4,8},{8,4},{0,0},{12,12},{5,9},{9,5},{1,1},{13,13},{6,10},{10,6},... | collective-permute-start | bytes 1572872 | tf_op jit(solution)/shard_map/ppermute | solution.py:426
  5.4 2.9 %copy-start.3 = (f32[16,1024]{1,0:T(8,128)S(1)}, f32[16,1024]{1,0:T(8,128)}, u32[]{:S(2)}) copy-start(f32[16,1024]{1,0:T(8,128)} %potential_ref.3) | copy-start | bytes 196612
  5.4 13.1 %collective-permute-start.4 = (f32[8,16,1024]{2,1,0:T(8,128)}, f32[8,16,1024]{2,1,0:T(8,128)S(1)}, u32[]{:S(2)}, u32[]{:S(2)}) collective-permute-start(f32[8,16,1024]{2,1,0:T(8,128)} %psi_ref.3), channel_id=1, source_target_pairs={{0,1},{1,0},{2,3},{3,2},{4,5},{5,4},{6,7},{7,6},{8,9},{9,8},{10,11... | collective-permute-start | bytes 1572872 | tf_op jit(solution)/shard_map/ppermute | solution.py:429
  5.4 18.0 %collective-permute-start.3 = (f32[8,16,1024]{2,1,0:T(8,128)}, f32[8,16,1024]{2,1,0:T(8,128)S(1)}, u32[]{:S(2)}, u32[]{:S(2)}) collective-permute-start(f32[8,16,1024]{2,1,0:T(8,128)} %psi_ref.3), channel_id=1, source_target_pairs={{0,3},{1,2},{2,1},{3,0},{4,7},{5,6},{6,5},{7,4},{8,11},{9,10},{10,... | collective-permute-start | bytes 1572872 | tf_op jit(solution)/shard_map/ppermute | solution.py:430
  7.0 0.7 %copy-start.5 = (s32[32]{0:T(128)S(1)}, s32[32]{0:T(128)}, u32[]{:S(2)}) copy-start(s32[32]{0:T(128)} %extent_ref.1) | copy-start | bytes 388
  8.3 1.0 %copy-start = (f32[8,16,1024]{2,1,0:T(8,128)S(1)}, f32[8,16,1024]{2,1,0:T(8,128)}, u32[]{:S(2)}) copy-start(f32[8,16,1024]{2,1,0:T(8,128)} %psi_ref.3) | copy-start | bytes 1572868
  15.9 8.7 %collective-permute-start.2 = (f32[8,16,1024]{2,1,0:T(8,128)S(1)}, f32[8,16,1024]{2,1,0:T(8,128)S(1)}, u32[]{:S(2)}, u32[]{:S(2)}) collective-permute-start(f32[8,16,1024]{2,1,0:T(8,128)S(1)} %collective-permute-done.psi_ref), channel_id=1, source_target_pairs={{4,8},{8,4},{0,0},{12,12},{5,9},{9,5},{1,1},{13,13},{6,10},{10,6},... | collective-permute-start | bytes 1572872 | tf_op jit(solution)/shard_map/ppermute | solution.py:439
  16.7 6.8 %copy-start.1 = (f32[8,16,1024]{2,1,0:T(8,128)S(1)}, f32[8,16,1024]{2,1,0:T(8,128)}, u32[]{:S(2)}) copy-start(f32[8,16,1024]{2,1,0:T(8,128)} %psi_ref.3) | copy-start | bytes 1572868
  16.7 6.8 %copy-start.4 = (bf16[2,16,144]{2,1,0:T(8,128)(2,1)S(1)}, bf16[2,16,144]{2,1,0:T(8,128)(2,1)}, u32[]{:S(2)}) copy-start(bf16[2,16,144]{2,1,0:T(8,128)(2,1)} %constant.5.clone.band_ref) | copy-start | bytes 27652
  16.7 15.7 %collective-permute-start.5 = (f32[8,16,1024]{2,1,0:T(8,128)S(1)}, f32[8,16,1024]{2,1,0:T(8,128)S(1)}, u32[]{:S(2)}, u32[]{:S(2)}) collective-permute-start(f32[8,16,1024]{2,1,0:T(8,128)S(1)} %collective-permute-done.psi_ref), channel_id=1, source_target_pairs={{0,3},{1,2},{2,1},{3,0},{4,7},{5,6},{6,5},{7,4},{8,11},{9,10},{10,... | collective-permute-start | bytes 1572872 | tf_op jit(solution)/shard_map/ppermute | solution.py:443
  17.0 15.4 %collective-permute-start.6 = (f32[8,16,1024]{2,1,0:T(8,128)S(1)}, f32[8,16,1024]{2,1,0:T(8,128)S(1)}, u32[]{:S(2)}, u32[]{:S(2)}) collective-permute-start(f32[8,16,1024]{2,1,0:T(8,128)S(1)} %collective-permute-done.psi_ref), channel_id=1, source_target_pairs={{0,1},{1,0},{2,3},{3,2},{4,5},{5,4},{6,7},{7,6},{8,9},{9,8},{10,11... | collective-permute-start | bytes 1572872 | tf_op jit(solution)/shard_map/ppermute | solution.py:444
  18.5 19.9 %collective-permute-start.9 = (f32[8,16,1024]{2,1,0:T(8,128)S(1)}, f32[8,16,1024]{2,1,0:T(8,128)S(1)}, u32[]{:S(2)}, u32[]{:S(2)}) collective-permute-start(f32[8,16,1024]{2,1,0:T(8,128)S(1)} %collective-permute-done.1.field_ref), channel_id=1, source_target_pairs={{0,4},{4,0},{8,12},{12,8},{1,5},{5,1},{9,13},{13,9},{2,6},{6,2},{1... | collective-permute-start | bytes 1572872 | tf_op jit(solution)/shard_map/ppermute | solution.py:440
  24.5 22.4 %collective-permute-start.11 = (f32[8,16,1024]{2,1,0:T(8,128)S(1)}, f32[8,16,1024]{2,1,0:T(8,128)S(1)}, u32[]{:S(2)}, u32[]{:S(2)}) collective-permute-start(f32[8,16,1024]{2,1,0:T(8,128)S(1)} %collective-permute-done.2.field_ref), channel_id=1, source_target_pairs={{0,4},{4,0},{8,12},{12,8},{1,5},{5,1},{9,13},{13,9},{2,6},{6,2},{1... | collective-permute-start | bytes 1572872 | tf_op jit(solution)/shard_map/ppermute | solution.py:459
  34.0 1.2 %collective-permute-start.7 = (f32[32,16]{1,0:T(8,128)S(1)}, f32[32,16]{1,0:T(8,128)S(1)}, u32[]{:S(2)}, u32[]{:S(2)}) collective-permute-start(f32[32,16]{1,0:T(8,128)S(1)} %shard_map.77.refs_0_), channel_id=1, source_target_pairs={{0,1},{1,0},{2,3},{3,2},{4,5},{5,4},{6,7},{7,6},{8,9},{9,8},{10,11... | collective-permute-start | bytes 6152 | tf_op jit(solution)/shard_map/ppermute | solution.py:470
  35.2 3.2 %collective-permute-start.8 = (f32[32,16]{1,0:T(8,128)S(1)}, f32[32,16]{1,0:T(8,128)S(1)}, u32[]{:S(2)}, u32[]{:S(2)}) collective-permute-start(f32[32,16]{1,0:T(8,128)S(1)} %shard_map.78.refs_0_), channel_id=1, source_target_pairs={{0,3},{1,2},{2,1},{3,0},{4,7},{5,6},{6,5},{7,4},{8,11},{9,10},{10,... | collective-permute-start | bytes 6152 | tf_op jit(solution)/shard_map/ppermute | solution.py:471
  38.4 9.0 %collective-permute-start.10 = (f32[48,256]{1,0:T(8,128)S(1)}, f32[48,256]{1,0:T(8,128)S(1)}, u32[]{:S(2)}, u32[]{:S(2)}) collective-permute-start(f32[48,256]{1,0:T(8,128)S(1)} %get-tuple-element.54), channel_id=1, source_target_pairs={{0,4},{4,0},{8,12},{12,8},{1,5},{5,1},{9,13},{13,9},{2,6},{6,2},{1... | collective-permute-start | bytes 147464 | tf_op jit(solution)/shard_map/ppermute | solution.py:485
  43.0 4.7 %collective-permute-start.12 = (f32[16,256]{1,0:T(8,128)S(1)}, f32[16,256]{1,0:T(8,128)S(1)}, u32[]{:S(2)}, u32[]{:S(2)}) collective-permute-start(f32[16,256]{1,0:T(8,128)S(1)} %get-tuple-element.61), channel_id=1, source_target_pairs={{0,8},{4,12},{8,0},{12,4},{1,9},{5,13},{9,1},{13,5},{2,10},{6,14},... | collective-permute-start | bytes 49160 | tf_op jit(solution)/shard_map/ppermute | solution.py:486
  43.7 3.9 %collective-permute-start.13 = (f32[16,256]{1,0:T(8,128)S(1)}, f32[16,256]{1,0:T(8,128)S(1)}, u32[]{:S(2)}, u32[]{:S(2)}) collective-permute-start(f32[16,256]{1,0:T(8,128)S(1)} %get-tuple-element.62), channel_id=1, source_target_pairs={{4,8},{8,4},{0,0},{12,12},{5,9},{9,5},{1,1},{13,13},{6,10},{10,6},... | collective-permute-start | bytes 49160 | tf_op jit(solution)/shard_map/ppermute | solution.py:487

commit v6 on v5

--- a/solution.py
+++ b/solution.py
@@ -237,14 +237,17 @@
 
 
 def correlation_kernel(
-    planes, scale, own_ref, pair_ref, third_ref, fourth_ref, image_ref, ward_ref, early_ref, out_ref
+    planes, scale, own_ref, pair_ref, third_ref, fourth_ref, ward_ref, early_ref, last_ref, out_ref
 ):
     half = own_ref.shape[0] // 2
     orbs = half // planes
     ward = [overlaps(ref, ward_ref, planes) for ref in (own_ref, pair_ref, third_ref, fourth_ref)]
-    last = overlaps(fourth_ref, image_ref, planes)
     wide = jnp.concatenate(
-        [jnp.concatenate([early_ref[...], last], axis=0), jnp.concatenate(ward, axis=0)], axis=1
+        [
+            jnp.concatenate([early_ref[...], last_ref[...]], axis=0),
+            jnp.concatenate(ward, axis=0),
+        ],
+        axis=1,
     )
     row = lax.broadcasted_iota(jnp.int32, (2 * half, 2 * orbs), 0)
     col = lax.broadcasted_iota(jnp.int32, (2 * half, 2 * orbs), 1)
@@ -319,7 +322,9 @@
 
     @pl.when(on_inner())
     def _():
-        out1_ref[planes:, : corr_ref.shape[1]] = corr_ref[...]
+        held, across = corr_ref.shape[0] // 4, corr_ref.shape[1]
+        for k in range(4):
+            out1_ref[planes:, k * across : (k + 1) * across] = corr_ref[k * held : (k + 1) * held]
         high, low = spread_out(corr_ref[...], planes)
         fields = (own_parts, pair_parts, third_parts, fourth_parts)
         for c in range(grid_p // width):
@@ -351,8 +356,8 @@
 
 
 def last_kernel(
-    own_phi, own_parts, pair_parts, third_parts, fourth_parts, image_ref, given_ref, kept_ref,
-    sent2_ref, sent3_ref, inner_new, new_ref, density_ref, own_new, own_density, sems,
+    own_phi, own_parts, pair_parts, third_parts, fourth_parts, image_ref, sent2_ref, sent3_ref,
+    given_ref, kept_ref, inner_new, new_ref, density_ref, own_new, own_density, sems,
 ):
     orbs, planes, grid_p = image_ref.shape
     width = 2 * lanes
@@ -374,9 +379,14 @@
 
     @pl.when(jnp.logical_not(on_inner()))
     def _():
-        own_density[...] = given_ref[:planes] + sent2_ref[...]
-        corr = given_ref[planes:, orbs : 2 * orbs]
-        corr = jnp.concatenate([corr[orbs : 2 * orbs], corr[:orbs], corr[2 * orbs :]], axis=0)
+        own_density[...] = given_ref[:planes] + sent2_ref[:planes]
+        corr = jnp.concatenate(
+            [
+                given_ref[planes:, (2 * k + 1) * orbs : (2 * k + 2) * orbs]
+                for k in (1, 0, 2, 3)
+            ],
+            axis=0,
+        )
         high, low = spread_out(corr, planes)
         fields = (own_parts, pair_parts, third_parts, fourth_parts)
         for c in range(grid_p // width):
@@ -412,9 +422,16 @@
     rows = orbs * planes
     cells = planes * n_cmp * grid_p
     swap = [(0, 1), (1, 0), (2, 3), (3, 2)]
-    across = [(1, 2), (2, 1), (0, 0), (3, 3)]
+    line = ("orb", "cmp")
     to_near = [(i, i ^ 1) for i in range(n_cmp)]
     to_far = [(i, i ^ 3) for i in range(n_cmp)]
+
+    def with_outer(inner_pairs):
+        outer_pairs = [(z * n_cmp + i, z * n_cmp + k) for z in (0, 3) for i, k in to_near]
+        return inner_pairs + outer_pairs
+
+    across = with_outer([(z * n_cmp + i, (3 - z) * n_cmp + i) for z in (1, 2) for i in range(n_cmp)])
+    inner_far = with_outer([(z * n_cmp + i, z * n_cmp + k) for z in (1, 2) for i, k in to_far])
 
     block = jax.ShapeDtypeStruct(psi.shape, jnp.float32)
     parts = jax.ShapeDtypeStruct((2 * rows, grid_p), jnp.bfloat16)
@@ -423,7 +440,7 @@
     bands = jnp.asarray(plane_bands(planes))
 
     pair = lax.ppermute(psi, "orb", swap)
-    third = lax.ppermute(psi, "orb", across)
+    third = lax.ppermute(psi, line, across)
     grid = call(columns_kernel, jax.ShapeDtypeStruct((8, grid_p), jnp.int32), "")()
     slab, grid = lax.optimization_barrier((psi, grid))
     near = lax.ppermute(slab, "cmp", to_near)
@@ -436,11 +453,11 @@
         functools.partial(local_kernel, 0), (block, parts, flat), "vvvv"
     )(psi, potential, live, columns)
     pair, local, own_parts = lax.optimization_barrier((pair, local, own_parts))
-    fourth = lax.ppermute(pair, "orb", across)
+    fourth = lax.ppermute(pair, line, across)
     third_out = lax.ppermute(third, "orb", swap)
     third_parts = call(functools.partial(split_kernel, 2), parts, "vv")(third, live)
     turn, third_parts = lax.optimization_barrier((pair, third_parts))
-    pair_far = lax.ppermute(turn, "cmp", to_far)
+    pair_far = lax.ppermute(turn, line, inner_far)
     pair_near = lax.ppermute(pair, "cmp", to_near)
 
     image, image_parts = call(functools.partial(plane_kernel, 0), (block, parts), "vvvvvv")(
@@ -461,21 +478,27 @@
         pair_far, pair, pair_near, ward_local, live, bands
     )
     fourth_parts = call(functools.partial(split_kernel, 3), parts, "vv")(fourth, live)
+    fourth_parts, third_out = lax.optimization_barrier((fourth_parts, third_out))
+    last = call(
+        functools.partial(overlap_kernel, planes, 1),
+        jax.ShapeDtypeStruct((orbs, rows), jnp.float32),
+        "vv",
+    )(fourth_parts, image_parts)
     part = call(
         functools.partial(correlation_kernel, planes, 1.0 / cells),
         jax.ShapeDtypeStruct((4 * orbs, 2 * orbs), jnp.float32),
         "vvvvvvv",
-    )(own_parts, pair_parts, third_parts, fourth_parts, image_parts, ward_parts, early)
+    )(own_parts, pair_parts, third_parts, fourth_parts, ward_parts, early, last)
     small = jax.ShapeDtypeStruct(part.shape, jnp.float32)
     chip = call(sum_kernel, small, "vv")(part, lax.ppermute(part, "cmp", to_near))
-    correlation = call(sum_kernel, small, "vv")(chip, lax.ppermute(chip, "cmp", to_far))
-    correlation, third_out = lax.optimization_barrier((correlation, third_out))
+    correlation = call(sum_kernel, small, "vv")(chip, lax.ppermute(chip, line, inner_far))
 
     share = jax.ShapeDtypeStruct((planes, grid_p // 4), jnp.float32)
-    wide = jax.ShapeDtypeStruct((planes + 4 * orbs, grid_p // 4), jnp.float32)
+    wide = jax.ShapeDtypeStruct((planes + orbs, grid_p // 4), jnp.float32)
+    first_sent = jax.ShapeDtypeStruct((2 * planes, grid_p // 4), jnp.float32)
     kept, first, second, last, inner_new = call(
         step_kernel,
-        [share, wide, share, share, block],
+        [share, wide, first_sent, share, block],
         "vvvvvvvvv",
         [pltpu.VMEM((planes, grid_p), jnp.float32)],
     )(
@@ -484,11 +507,11 @@
     )
     given = lax.ppermute(first, "orb", swap)
     sent2 = lax.ppermute(second, "orb", [(i, i ^ 2) for i in range(4)])
-    sent3 = lax.ppermute(last, "orb", across)
+    sent3 = lax.ppermute(last, line, across)
     third_held, fourth_held = call(outer_split_kernel, (parts, parts), "vvv")(
         third_out, fourth_out, live
     )
-    given, third_held = lax.optimization_barrier((given, third_held))
+    sent2, sent3, third_held = lax.optimization_barrier((sent2, sent3, third_held))
     new, density = call(
         last_kernel,
         [block, share],
@@ -500,7 +523,7 @@
         ],
         "aa",
     )(
-        own_phi, own_parts, pair_parts, third_held, fourth_held, image, given, kept, sent2, sent3,
+        own_phi, own_parts, pair_parts, third_held, fourth_held, image, sent2, sent3, given, kept,
         inner_new,
     )
     return (new, density)

time: 49.7 us -> 47.5 us (0.956)
  starting transfers between devices: 28.3 us -> 24.3 us
  waiting for transfers between devices: 12.1 us -> 13.8 us
    ppermute x1, starting transfers between devices: 0.77 us -> 6.32 us  [line_device(): sent2 = lax.ppermute(second, 'orb', [(i, i ^ 2) for i in range(4)])]
    ppermute x1, starting transfers between devices: 4.52 us -> 0.01 us  [line_device(): given = lax.ppermute(first, 'orb', swap)]
    ppermute x5, starting transfers between devices: 4.57 us -> 0.42 us  [the longest x1 0.18 us: line_device(): sent3 = lax.ppermute(last, line, across)]
    ppermute x1, waiting for transfers between devices: 2.54 us -> 0.01 us  [line_device(): fourth_out = lax.ppermute(fourth, 'orb', swap)]
    ppermute x1, waiting for transfers between devices: 5.99 us -> 7.58 us  [line_device(): pair = lax.ppermute(psi, 'orb', swap)]
    ppermute x1, waiting for transfers between devices: 0.36 us -> 1.81 us  [line_device(): given = lax.ppermute(first, 'orb', swap)]
    ppermute x1, starting transfers between devices: 7.75 us -> 8.87 us  [line_device(): fourth_out = lax.ppermute(fourth, 'orb', swap)]
    ppermute x1, starting transfers between devices: 1.55 us -> 0.49 us  [line_device(): pair_near = lax.ppermute(pair, 'cmp', to_near)]
  transfers between devices with their start and end apart: 14 -> 14, of which waited for: 6 -> 7; matrix products, arithmetic and copies ran while one was open for 0% -> 0% of each run, Pallas kernels for 9% -> 10%
where the time goes in v6:
time: 47.5 us; the launch traced here: 47.3 us
  starting transfers between devices  24.3 us (51%)
  waiting for transfers between devices  13.8 us (29%)
  Pallas kernels  6.67 us (14%)
  local copies, waits for them, and re-layouts  1.72 us (4%)
  between operations  0.83 us (2%)
    ppermute x1, starting transfers between devices, line_device(): fourth_out = lax.ppermute(fourth, 'orb', swap)  8.87 us
    ppermute x1, waiting for transfers between devices, line_device(): pair = lax.ppermute(psi, 'orb', swap)  7.58 us
    ppermute x1, starting transfers between devices, line_device(): sent2 = lax.ppermute(second, 'orb', [(i, i ^ 2) for i in range(4)])  6.32 us
    ppermute x1, starting transfers between devices, line_device(): third_out = lax.ppermute(third, 'orb', swap)  3.31 us
    ppermute x1, starting transfers between devices, line_device(): pair = lax.ppermute(psi, 'orb', swap)  3.09 us
    pallas_call x1, Pallas kernels, line_device(): call(last_kernel, [block, share], 'vvvvvvvvvvv', [pltpu.VMEM(block.shape,...  1.89 us
    ppermute x1, waiting for transfers between devices, line_device(): given = lax.ppermute(first, 'orb', swap)  1.81 us
    unnamed x12, local copies, waits for them, and re-layouts  1.72 us
  transfers between devices with their start and end apart: 14, of which 7 were waited for; matrix products, arithmetic and copies ran while one was open for 0% of the time, Pallas kernels for 10%

profile of v6, /device:TPU:0, one launch (start us, length us, event | category | flops | bytes accessed | tf_op | source)
XLA Modules:
  0.0 47.3 jit_solution(5115599924580914006)
XLA Ops:
  0.6 0.0 copy-start.2
  0.6 3.1 %collective-permute-start = (f32[8,16,1024]{2,1,0:T(8,128)}, f32[8,16,1024]{2,1,0:T(8,128)S(1)}, u32[]{:S(2)}, u32[]{:S(2)}) collective-permute-start(f32[8,16,1024]{2,1,0:T(8,128)} %psi_ref.3), channel_id=1, source_target_pairs={{0,4},{4,0},{8,12},{12,8},{1,5},{5,1},{9,13},{13,9},{2,6},{6,2},{1... | collective-permute-start | bytes 1572872 | tf_op jit(solution)/shard_map/ppermute | solution.py:442
  3.7 0.0 collective-permute-start.1
  3.7 0.0 copy-start.3
  3.8 0.5 %collective-permute-start.4 = (f32[8,16,1024]{2,1,0:T(8,128)}, f32[8,16,1024]{2,1,0:T(8,128)S(1)}, u32[]{:S(2)}, u32[]{:S(2)}) collective-permute-start(f32[8,16,1024]{2,1,0:T(8,128)} %psi_ref.3), channel_id=1, source_target_pairs={{0,1},{1,0},{2,3},{3,2},{4,5},{5,4},{6,7},{7,6},{8,9},{9,8},{10,11... | collective-permute-start | bytes 1572872 | tf_op jit(solution)/shard_map/ppermute | solution.py:446
  4.2 1.2 %collective-permute-start.3 = (f32[8,16,1024]{2,1,0:T(8,128)}, f32[8,16,1024]{2,1,0:T(8,128)S(1)}, u32[]{:S(2)}, u32[]{:S(2)}) collective-permute-start(f32[8,16,1024]{2,1,0:T(8,128)} %psi_ref.3), channel_id=1, source_target_pairs={{0,3},{1,2},{2,1},{3,0},{4,7},{5,6},{6,5},{7,4},{8,11},{9,10},{10,... | collective-permute-start | bytes 1572872 | tf_op jit(solution)/shard_map/ppermute | solution.py:447
  5.4 0.0 copy-start.5
  5.4 0.7 %copy-done.5 = s32[32]{0:T(128)S(1)} copy-done((s32[32]{0:T(128)S(1)}, s32[32]{0:T(128)}, u32[]{:S(2)}) %copy-start.5) | copy-done | bytes 152
  6.1 0.6 %shard_map.69.live_ref = f32[32,1024]{1,0:T(8,128)S(1)} custom-call(s32[8,1024]{1,0:T(8,128)S(1)} %shard_map.68.columns_ref, s32[32]{0:T(128)S(1)} %copy-done.5), custom_call_target="tpu_custom_call" | custom-call | flops 1 | bytes 1 | tf_op jit(solution)/shard_map/pallas_call | solution.py:449
  6.7 0.0 copy-done.2
  6.7 0.0 copy-done.3
  6.7 0.0 copy-start
  6.7 1.0 %copy-done = f32[8,16,1024]{2,1,0:T(8,128)S(1)} copy-done((f32[8,16,1024]{2,1,0:T(8,128)S(1)}, f32[8,16,1024]{2,1,0:T(8,128)}, u32[]{:S(2)}) %copy-start) | copy-done | bytes 524312
  7.7 0.5 %shard_map.70 = (f32[8,16,1024]{2,1,0:T(8,128)S(1)}, bf16[256,1024]{1,0:T(8,128)(2,1)S(1)}, f32[128,1024]{1,0:T(8,128)S(1)}) custom-call(f32[8,16,1024]{2,1,0:T(8,128)S(1)} %copy-done, f32[16,1024]{1,0:T(8,128)S(1)} %copy-done.3, f32[32,1024]{1,0:T(8,128)S(1)} %shard_map.69.live_ref, bf16[256,256]{1,0:T(8,128)(2,1)S(1)} %copy-done.2), custom_call_target="tpu_custom_call" | custom-call | flops 1 | bytes 1 | tf_op jit(solution)/shard_map/pallas_call | solution.py:452
  8.3 7.6 %collective-permute-done.psi_ref = f32[8,16,1024]{2,1,0:T(8,128)S(1)} collective-permute-done((f32[8,16,1024]{2,1,0:T(8,128)}, f32[8,16,1024]{2,1,0:T(8,128)S(1)}, u32[]{:S(2)}, u32[]{:S(2)}) %collective-permute-start) | collective-permute-done | bytes 524320 | tf_op jit(solution)/shard_map/ppermute | solution.py:442
  15.9 0.0 collective-permute-start.2
  15.9 0.0 collective-permute-done.1.field_ref
  15.9 3.3 %collective-permute-start.5 = (f32[8,16,1024]{2,1,0:T(8,128)S(1)}, f32[8,16,1024]{2,1,0:T(8,128)S(1)}, u32[]{:S(2)}, u32[]{:S(2)}) collective-permute-start(f32[8,16,1024]{2,1,0:T(8,128)S(1)} %collective-permute-done.1.field_ref), channel_id=1, source_target_pairs={{0,4},{4,0},{8,12},{12,8},{1,5},{5,1},{9,13},{13,9},{2,6},{6,2},{1... | collective-permute-start | bytes 1572872 | tf_op jit(solution)/shard_map/ppermute | solution.py:457
  19.2 0.1 shard_map.72.refs_2_.third_ref.third_parts
  19.3 0.0 copy-start.1
  19.3 0.0 copy-start.4
  19.3 0.1 collective-permute-start.6
  19.4 0.0 collective-permute-done.4.near_ref
  19.4 0.5 %collective-permute-start.7 = (f32[8,16,1024]{2,1,0:T(8,128)S(1)}, f32[8,16,1024]{2,1,0:T(8,128)S(1)}, u32[]{:S(2)}, u32[]{:S(2)}) collective-permute-start(f32[8,16,1024]{2,1,0:T(8,128)S(1)} %collective-permute-done.psi_ref), channel_id=1, source_target_pairs={{0,1},{1,0},{2,3},{3,2},{4,5},{5,4},{6,7},{7,6},{8,9},{9,8},{10,11... | collective-permute-start | bytes 1572872 | tf_op jit(solution)/shard_map/ppermute | solution.py:461
  19.9 0.5 %shard_map.71 = (f32[8,16,1024]{2,1,0:T(8,128)S(1)}, bf16[256,1024]{1,0:T(8,128)(2,1)S(1)}, f32[128,1024]{1,0:T(8,128)S(1)}) custom-call(f32[8,16,1024]{2,1,0:T(8,128)S(1)} %collective-permute-done.psi_ref, f32[16,1024]{1,0:T(8,128)S(1)} %copy-done.3, f32[32,1024]{1,0:T(8,128)S(1)} %shard_map.69.live_ref, bf16[256,256]{1,0:T(8,128)(2,1)S(1)} %copy-done.2), custom_call_target="tpu_custom_call" | custom-call | flops 1 | bytes 1 | tf_op jit(solution)/shard_map/pallas_call | solution.py:466
  20.4 0.0 collective-permute-done.3.far_ref
  20.4 0.0 copy-done.1
  20.4 0.0 copy-done.4
  20.4 0.4 shard_map.73
  20.9 0.6 %shard_map.74.early_ref = f32[24,128]{1,0:T(8,128)S(1)} custom-call(bf16[256,1024]{1,0:T(8,128)(2,1)S(1)} %get-tuple-element.38.refs_0_.own_ref.own_parts, bf16[256,1024]{1,0:T(8,128)(2,1)S(1)} %get-tuple-element.40.refs_1_.pair_ref.pair_parts, bf16[256,1024]{1,0:T(8,128)(2,1)S(1)} %shard_map.72.refs_2_.third_ref.third_parts, ...), custom_call_target="tpu_custom_call" | custom-call | flops 1 | bytes 1 | tf_op jit(solution)/shard_map/pallas_call | solution.py:469
  21.5 0.0 collective-permute-done.2.field_ref
  21.5 8.9 %collective-permute-start.12 = (f32[8,16,1024]{2,1,0:T(8,128)S(1)}, f32[8,16,1024]{2,1,0:T(8,128)S(1)}, u32[]{:S(2)}, u32[]{:S(2)}) collective-permute-start(f32[8,16,1024]{2,1,0:T(8,128)S(1)} %collective-permute-done.2.field_ref), channel_id=1, source_target_pairs={{0,4},{4,0},{8,12},{12,8},{1,5},{5,1},{9,13},{13,9},{2,6},{6,2},{1... | collective-permute-start | bytes 1572872 | tf_op jit(solution)/shard_map/ppermute | solution.py:476
  30.4 0.1 shard_map.75.refs_0_.fourth_ref.fourth_parts
  30.5 0.6 %collective-permute-done.5.third_ref = f32[8,16,1024]{2,1,0:T(8,128)S(1)} collective-permute-done((f32[8,16,1024]{2,1,0:T(8,128)S(1)}, f32[8,16,1024]{2,1,0:T(8,128)S(1)}, u32[]{:S(2)}, u32[]{:S(2)}) %collective-permute-start.5) | collective-permute-done | bytes 524320 | tf_op jit(solution)/shard_map/ppermute | solution.py:457
  31.1 0.3 shard_map.77.last_ref
  31.4 0.0 collective-permute-done.6.far_ref
  31.4 0.0 collective-permute-done.7.near_ref
  31.4 0.4 shard_map.76
  31.9 0.9 %shard_map.78.refs_0_ = f32[32,16]{1,0:T(8,128)S(1)} custom-call(bf16[256,1024]{1,0:T(8,128)(2,1)S(1)} %get-tuple-element.38.refs_0_.own_ref.own_parts, bf16[256,1024]{1,0:T(8,128)(2,1)S(1)} %get-tuple-element.40.refs_1_.pair_ref.pair_parts, bf16[256,1024]{1,0:T(8,128)(2,1)S(1)} %shard_map.72.refs_2_.third_ref.third_parts, ...), custom_call_target="tpu_custom_call" | custom-call | flops 1 | bytes 1 | tf_op jit(solution)/shard_map/pallas_call | solution.py:487
  32.8 0.1 collective-permute-start.8
  32.9 1.2 %collective-permute-done.8.refs_1_ = f32[32,16]{1,0:T(8,128)S(1)} collective-permute-done((f32[32,16]{1,0:T(8,128)S(1)}, f32[32,16]{1,0:T(8,128)S(1)}, u32[]{:S(2)}, u32[]{:S(2)}) %collective-permute-start.8) | collective-permute-done | bytes 2080 | tf_op jit(solution)/shard_map/ppermute | solution.py:493
  34.1 0.2 collective-permute-start.9
  34.2 1.0 %collective-permute-done.9.refs_1_ = f32[32,16]{1,0:T(8,128)S(1)} collective-permute-done((f32[32,16]{1,0:T(8,128)S(1)}, f32[32,16]{1,0:T(8,128)S(1)}, u32[]{:S(2)}, u32[]{:S(2)}) %collective-permute-start.9) | collective-permute-done | bytes 2080 | tf_op jit(solution)/shard_map/ppermute | solution.py:494
  35.3 6.3 %collective-permute-start.10 = (f32[32,256]{1,0:T(8,128)S(1)}, f32[32,256]{1,0:T(8,128)S(1)}, u32[]{:S(2)}, u32[]{:S(2)}) collective-permute-start(f32[32,256]{1,0:T(8,128)S(1)} %get-tuple-element.55), channel_id=1, source_target_pairs={{0,8},{4,12},{8,0},{12,4},{1,9},{5,13},{9,1},{13,5},{2,10},{6,14},... | collective-permute-start | bytes 98312 | tf_op jit(solution)/shard_map/ppermute | solution.py:509
  41.6 0.0 collective-permute-start.13
  41.6 0.2 collective-permute-start.11
  41.8 0.0 collective-permute-done.12.fourth_ref
  41.8 0.2 shard_map.82
  41.9 0.8 %collective-permute-done.11.sent3_ref = f32[16,256]{1,0:T(8,128)S(1)} collective-permute-done((f32[16,256]{1,0:T(8,128)S(1)}, f32[16,256]{1,0:T(8,128)S(1)}, u32[]{:S(2)}, u32[]{:S(2)}) %collective-permute-start.11) | collective-permute-done | bytes 16416 | tf_op jit(solution)/shard_map/ppermute | solution.py:510
  42.8 0.8 %collective-permute-done.10.sent2_ref = f32[32,256]{1,0:T(8,128)S(1)} collective-permute-done((f32[32,256]{1,0:T(8,128)S(1)}, f32[32,256]{1,0:T(8,128)S(1)}, u32[]{:S(2)}, u32[]{:S(2)}) %collective-permute-start.10) | collective-permute-done | bytes 32800 | tf_op jit(solution)/shard_map/ppermute | solution.py:509
  43.6 1.8 %collective-permute-done.13.given_ref = f32[24,256]{1,0:T(8,128)S(1)} collective-permute-done((f32[24,256]{1,0:T(8,128)S(1)}, f32[24,256]{1,0:T(8,128)S(1)}, u32[]{:S(2)}, u32[]{:S(2)}) %collective-permute-start.13) | collective-permute-done | bytes 24608 | tf_op jit(solution)/shard_map/ppermute | solution.py:508
  45.4 1.9 %shard_map.83 = (f32[8,16,1024]{2,1,0:T(8,128)}, f32[16,256]{1,0:T(8,128)}) custom-call(f32[128,1024]{1,0:T(8,128)S(1)} %get-tuple-element.35.own_phi, bf16[256,1024]{1,0:T(8,128)(2,1)S(1)} %get-tuple-element.38.refs_0_.own_ref.own_parts, bf16[256,1024]{1,0:T(8,128)(2,1)S(1)} %get-tuple-element.40.refs_1_.pair_ref.pair_parts, ...), custom_call_target="tpu_custom_call" | custom-call | flops 1 | bytes 1 | tf_op jit(solution)/shard_map/pallas_call | solution.py:515
  (4 shorter events, 0.0 us)
Async XLA Ops:
  0.6 6.0 %copy-start.2 = (bf16[256,256]{1,0:T(8,128)(2,1)S(1)}, bf16[256,256]{1,0:T(8,128)(2,1)}, u32[]{:S(2)}) copy-start(bf16[256,256]{1,0:T(8,128)(2,1)} %constant.4.clone.band_ref) | copy-start | bytes 393220
  0.6 15.2 %collective-permute-start = (f32[8,16,1024]{2,1,0:T(8,128)}, f32[8,16,1024]{2,1,0:T(8,128)S(1)}, u32[]{:S(2)}, u32[]{:S(2)}) collective-permute-start(f32[8,16,1024]{2,1,0:T(8,128)} %psi_ref.3), channel_id=1, source_target_pairs={{0,4},{4,0},{8,12},{12,8},{1,5},{5,1},{9,13},{13,9},{2,6},{6,2},{1... | collective-permute-start | bytes 1572872 | tf_op jit(solution)/shard_map/ppermute | solution.py:442
  3.7 12.1 %collective-permute-start.1 = (f32[8,16,1024]{2,1,0:T(8,128)}, f32[8,16,1024]{2,1,0:T(8,128)S(1)}, u32[]{:S(2)}, u32[]{:S(2)}) collective-permute-start(f32[8,16,1024]{2,1,0:T(8,128)} %psi_ref.3), channel_id=1, source_target_pairs={{4,8},{5,9},{6,10},{7,11},{8,4},{9,5},{10,6},{11,7},{0,1},{1,0},{2... | collective-permute-start | bytes 1572872 | tf_op jit(solution)/shard_map/ppermute | solution.py:443
  3.7 2.9 %copy-start.3 = (f32[16,1024]{1,0:T(8,128)S(1)}, f32[16,1024]{1,0:T(8,128)}, u32[]{:S(2)}) copy-start(f32[16,1024]{1,0:T(8,128)} %potential_ref.3) | copy-start | bytes 196612
  3.8 15.6 %collective-permute-start.4 = (f32[8,16,1024]{2,1,0:T(8,128)}, f32[8,16,1024]{2,1,0:T(8,128)S(1)}, u32[]{:S(2)}, u32[]{:S(2)}) collective-permute-start(f32[8,16,1024]{2,1,0:T(8,128)} %psi_ref.3), channel_id=1, source_target_pairs={{0,1},{1,0},{2,3},{3,2},{4,5},{5,4},{6,7},{7,6},{8,9},{9,8},{10,11... | collective-permute-start | bytes 1572872 | tf_op jit(solution)/shard_map/ppermute | solution.py:446
  4.2 16.2 %collective-permute-start.3 = (f32[8,16,1024]{2,1,0:T(8,128)}, f32[8,16,1024]{2,1,0:T(8,128)S(1)}, u32[]{:S(2)}, u32[]{:S(2)}) collective-permute-start(f32[8,16,1024]{2,1,0:T(8,128)} %psi_ref.3), channel_id=1, source_target_pairs={{0,3},{1,2},{2,1},{3,0},{4,7},{5,6},{6,5},{7,4},{8,11},{9,10},{10,... | collective-permute-start | bytes 1572872 | tf_op jit(solution)/shard_map/ppermute | solution.py:447
  5.4 0.7 %copy-start.5 = (s32[32]{0:T(128)S(1)}, s32[32]{0:T(128)}, u32[]{:S(2)}) copy-start(s32[32]{0:T(128)} %extent_ref.1) | copy-start | bytes 388
  6.7 1.0 %copy-start = (f32[8,16,1024]{2,1,0:T(8,128)S(1)}, f32[8,16,1024]{2,1,0:T(8,128)}, u32[]{:S(2)}) copy-start(f32[8,16,1024]{2,1,0:T(8,128)} %psi_ref.3) | copy-start | bytes 1572868
  15.9 5.6 %collective-permute-start.2 = (f32[8,16,1024]{2,1,0:T(8,128)S(1)}, f32[8,16,1024]{2,1,0:T(8,128)S(1)}, u32[]{:S(2)}, u32[]{:S(2)}) collective-permute-start(f32[8,16,1024]{2,1,0:T(8,128)S(1)} %collective-permute-done.psi_ref), channel_id=1, source_target_pairs={{4,8},{5,9},{6,10},{7,11},{8,4},{9,5},{10,6},{11,7},{0,1},{1,0},{2... | collective-permute-start | bytes 1572872 | tf_op jit(solution)/shard_map/ppermute | solution.py:456
  15.9 15.2 %collective-permute-start.5 = (f32[8,16,1024]{2,1,0:T(8,128)S(1)}, f32[8,16,1024]{2,1,0:T(8,128)S(1)}, u32[]{:S(2)}, u32[]{:S(2)}) collective-permute-start(f32[8,16,1024]{2,1,0:T(8,128)S(1)} %collective-permute-done.1.field_ref), channel_id=1, source_target_pairs={{0,4},{4,0},{8,12},{12,8},{1,5},{5,1},{9,13},{13,9},{2,6},{6,2},{1... | collective-permute-start | bytes 1572872 | tf_op jit(solution)/shard_map/ppermute | solution.py:457
  19.3 1.1 %copy-start.1 = (f32[8,16,1024]{2,1,0:T(8,128)S(1)}, f32[8,16,1024]{2,1,0:T(8,128)}, u32[]{:S(2)}) copy-start(f32[8,16,1024]{2,1,0:T(8,128)} %psi_ref.3) | copy-start | bytes 1572868
  19.3 1.1 %copy-start.4 = (bf16[2,16,144]{2,1,0:T(8,128)(2,1)S(1)}, bf16[2,16,144]{2,1,0:T(8,128)(2,1)}, u32[]{:S(2)}) copy-start(bf16[2,16,144]{2,1,0:T(8,128)(2,1)} %constant.5.clone.band_ref) | copy-start | bytes 27652
  19.3 12.1 %collective-permute-start.6 = (f32[8,16,1024]{2,1,0:T(8,128)S(1)}, f32[8,16,1024]{2,1,0:T(8,128)S(1)}, u32[]{:S(2)}, u32[]{:S(2)}) collective-permute-start(f32[8,16,1024]{2,1,0:T(8,128)S(1)} %collective-permute-done.psi_ref), channel_id=1, source_target_pairs={{4,7},{5,6},{6,5},{7,4},{8,11},{9,10},{10,9},{11,8},{0,1},{1,0},{2... | collective-permute-start | bytes 1572872 | tf_op jit(solution)/shard_map/ppermute | solution.py:460
  19.4 12.0 %collective-permute-start.7 = (f32[8,16,1024]{2,1,0:T(8,128)S(1)}, f32[8,16,1024]{2,1,0:T(8,128)S(1)}, u32[]{:S(2)}, u32[]{:S(2)}) collective-permute-start(f32[8,16,1024]{2,1,0:T(8,128)S(1)} %collective-permute-done.psi_ref), channel_id=1, source_target_pairs={{0,1},{1,0},{2,3},{3,2},{4,5},{5,4},{6,7},{7,6},{8,9},{9,8},{10,11... | collective-permute-start | bytes 1572872 | tf_op jit(solution)/shard_map/ppermute | solution.py:461
  21.5 20.2 %collective-permute-start.12 = (f32[8,16,1024]{2,1,0:T(8,128)S(1)}, f32[8,16,1024]{2,1,0:T(8,128)S(1)}, u32[]{:S(2)}, u32[]{:S(2)}) collective-permute-start(f32[8,16,1024]{2,1,0:T(8,128)S(1)} %collective-permute-done.2.field_ref), channel_id=1, source_target_pairs={{0,4},{4,0},{8,12},{12,8},{1,5},{5,1},{9,13},{13,9},{2,6},{6,2},{1... | collective-permute-start | bytes 1572872 | tf_op jit(solution)/shard_map/ppermute | solution.py:476
  32.8 1.2 %collective-permute-start.8 = (f32[32,16]{1,0:T(8,128)S(1)}, f32[32,16]{1,0:T(8,128)S(1)}, u32[]{:S(2)}, u32[]{:S(2)}) collective-permute-start(f32[32,16]{1,0:T(8,128)S(1)} %shard_map.78.refs_0_), channel_id=1, source_target_pairs={{0,1},{1,0},{2,3},{3,2},{4,5},{5,4},{6,7},{7,6},{8,9},{9,8},{10,11... | collective-permute-start | bytes 6152 | tf_op jit(solution)/shard_map/ppermute | solution.py:493
  34.1 1.2 %collective-permute-start.9 = (f32[32,16]{1,0:T(8,128)S(1)}, f32[32,16]{1,0:T(8,128)S(1)}, u32[]{:S(2)}, u32[]{:S(2)}) collective-permute-start(f32[32,16]{1,0:T(8,128)S(1)} %shard_map.79.refs_0_), channel_id=1, source_target_pairs={{4,7},{5,6},{6,5},{7,4},{8,11},{9,10},{10,9},{11,8},{0,1},{1,0},{2... | collective-permute-start | bytes 6152 | tf_op jit(solution)/shard_map/ppermute | solution.py:494
  35.3 8.3 %collective-permute-start.10 = (f32[32,256]{1,0:T(8,128)S(1)}, f32[32,256]{1,0:T(8,128)S(1)}, u32[]{:S(2)}, u32[]{:S(2)}) collective-permute-start(f32[32,256]{1,0:T(8,128)S(1)} %get-tuple-element.55), channel_id=1, source_target_pairs={{0,8},{4,12},{8,0},{12,4},{1,9},{5,13},{9,1},{13,5},{2,10},{6,14},... | collective-permute-start | bytes 98312 | tf_op jit(solution)/shard_map/ppermute | solution.py:509
  41.6 3.8 %collective-permute-start.13 = (f32[24,256]{1,0:T(8,128)S(1)}, f32[24,256]{1,0:T(8,128)S(1)}, u32[]{:S(2)}, u32[]{:S(2)}) collective-permute-start(f32[24,256]{1,0:T(8,128)S(1)} %get-tuple-element.63), channel_id=1, source_target_pairs={{0,4},{4,0},{8,12},{12,8},{1,5},{5,1},{9,13},{13,9},{2,6},{6,2},{1... | collective-permute-start | bytes 73736 | tf_op jit(solution)/shard_map/ppermute | solution.py:508
  41.6 1.2 %collective-permute-start.11 = (f32[16,256]{1,0:T(8,128)S(1)}, f32[16,256]{1,0:T(8,128)S(1)}, u32[]{:S(2)}, u32[]{:S(2)}) collective-permute-start(f32[16,256]{1,0:T(8,128)S(1)} %get-tuple-element.56), channel_id=1, source_target_pairs={{4,8},{5,9},{6,10},{7,11},{8,4},{9,5},{10,6},{11,7},{0,1},{1,0},{2... | collective-permute-start | bytes 49160 | tf_op jit(solution)/shard_map/ppermute | solution.py:510

commit v7 on v6

--- a/solution.py
+++ b/solution.py
@@ -265,6 +265,12 @@
     refs[-1][...] = total
 
 
+def correlation_sum_kernel(part_ref, other_ref, out_ref, sent_ref):
+    total = part_ref[...] + other_ref[...]
+    out_ref[...] = total
+    sent_ref[: total.shape[0], : total.shape[1]] = total
+
+
 def spread_out(corr, planes):
     n_a, n_b = corr.shape
     shift = planes.bit_length() - 1
@@ -322,9 +328,6 @@
 
     @pl.when(on_inner())
     def _():
-        held, across = corr_ref.shape[0] // 4, corr_ref.shape[1]
-        for k in range(4):
-            out1_ref[planes:, k * across : (k + 1) * across] = corr_ref[k * held : (k + 1) * held]
         high, low = spread_out(corr_ref[...], planes)
         fields = (own_parts, pair_parts, third_parts, fourth_parts)
         for c in range(grid_p // width):
@@ -355,38 +358,26 @@
         split_into(fourth_parts, fourth_ref, live_ref, 3)
 
 
-def last_kernel(
-    own_phi, own_parts, pair_parts, third_parts, fourth_parts, image_ref, sent2_ref, sent3_ref,
-    given_ref, kept_ref, inner_new, new_ref, density_ref, own_new, own_density, sems,
+def finish_kernel(
+    own_phi, own_parts, pair_parts, third_parts, fourth_parts, image_ref, corr_ref, inner_new,
+    new_ref, own_new, sem,
 ):
     orbs, planes, grid_p = image_ref.shape
     width = 2 * lanes
 
     def write(values_ref):
-        copies = [
-            pltpu.make_async_copy(values_ref, new_ref, sems.at[0]),
-            pltpu.make_async_copy(own_density, density_ref, sems.at[1]),
-        ]
-        for copy in copies:
-            copy.start()
-        for copy in copies:
-            copy.wait()
+        copy = pltpu.make_async_copy(values_ref, new_ref, sem)
+        copy.start()
+        copy.wait()
 
     @pl.when(on_inner())
     def _():
-        own_density[...] = kept_ref[...] + sent3_ref[...]
         write(inner_new)
 
     @pl.when(jnp.logical_not(on_inner()))
     def _():
-        own_density[...] = given_ref[:planes] + sent2_ref[:planes]
-        corr = jnp.concatenate(
-            [
-                given_ref[planes:, (2 * k + 1) * orbs : (2 * k + 2) * orbs]
-                for k in (1, 0, 2, 3)
-            ],
-            axis=0,
-        )
+        corr = corr_ref[: 4 * orbs, orbs : 2 * orbs]
+        corr = jnp.concatenate([corr[orbs : 2 * orbs], corr[:orbs], corr[2 * orbs :]], axis=0)
         high, low = spread_out(corr, planes)
         fields = (own_parts, pair_parts, third_parts, fourth_parts)
         for c in range(grid_p // width):
@@ -398,6 +389,18 @@
                     own_phi[at, chunk] - step_length * image_ref[a, :, chunk] + change[at]
                 )
         write(own_new)
+
+
+def last_kernel(sent2_ref, sent3_ref, given_ref, kept_ref, density_ref):
+    planes = density_ref.shape[0]
+
+    @pl.when(on_inner())
+    def _():
+        density_ref[...] = kept_ref[...] + sent3_ref[...]
+
+    @pl.when(jnp.logical_not(on_inner()))
+    def _():
+        density_ref[...] = given_ref[:planes] + sent2_ref[:planes]
 
 
 def call(kernel, out_shape, specs, scratch=(), out_specs=None):
@@ -491,7 +494,13 @@
     )(own_parts, pair_parts, third_parts, fourth_parts, ward_parts, early, last)
     small = jax.ShapeDtypeStruct(part.shape, jnp.float32)
     chip = call(sum_kernel, small, "vv")(part, lax.ppermute(part, "cmp", to_near))
-    correlation = call(sum_kernel, small, "vv")(chip, lax.ppermute(chip, line, inner_far))
+    correlation, sent = call(
+        correlation_sum_kernel,
+        (small, jax.ShapeDtypeStruct((5 * orbs, grid_p // 4), jnp.float32)),
+        "vv",
+    )(chip, lax.ppermute(chip, line, inner_far))
+
+    given_correlation = lax.ppermute(sent, "orb", swap)
 
     share = jax.ShapeDtypeStruct((planes, grid_p // 4), jnp.float32)
     wide = jax.ShapeDtypeStruct((planes + orbs, grid_p // 4), jnp.float32)
@@ -511,21 +520,18 @@
     third_held, fourth_held = call(outer_split_kernel, (parts, parts), "vvv")(
         third_out, fourth_out, live
     )
-    sent2, sent3, third_held = lax.optimization_barrier((sent2, sent3, third_held))
-    new, density = call(
-        last_kernel,
-        [block, share],
-        "vvvvvvvvvvv",
-        [
-            pltpu.VMEM(block.shape, jnp.float32),
-            pltpu.VMEM(share.shape, jnp.float32),
-            pltpu.SemaphoreType.DMA((2,)),
-        ],
-        "aa",
+    new = call(
+        finish_kernel,
+        block,
+        "vvvvvvvv",
+        [pltpu.VMEM(block.shape, jnp.float32), pltpu.SemaphoreType.DMA],
+        "a",
     )(
-        own_phi, own_parts, pair_parts, third_held, fourth_held, image, sent2, sent3, given, kept,
+        own_phi, own_parts, pair_parts, third_held, fourth_held, image, given_correlation,
         inner_new,
     )
+    sent2, sent3, given, new = lax.optimization_barrier((sent2, sent3, given, new))
+    density = call(last_kernel, share, "vvvv")(sent2, sent3, given, kept)
     return (new, density)
 
 

time: 47.5 us -> 46.2 us (0.973)
  waiting for transfers between devices: 13.8 us -> 11.6 us
  Pallas kernels: 6.67 us -> 7.25 us
    ppermute x0 -> x1, starting transfers between devices: none -> 4.1 us  [line_device(): given_correlation = lax.ppermute(sent, 'orb', swap)]
    ppermute x1, starting transfers between devices: 6.32 us -> 2.24 us  [line_device(): sent2 = lax.ppermute(second, 'orb', [(i, i ^ 2) for i in range(4)])]
    ppermute x1, waiting for transfers between devices: 0.83 us -> 0.01 us  [line_device(): sent2 = lax.ppermute(second, 'orb', [(i, i ^ 2) for i in range(4)])]
    ppermute x1, waiting for transfers between devices: 0.82 us -> 0.01 us  [line_device(): sent3 = lax.ppermute(last, line, across)]
    ppermute x1, waiting for transfers between devices: 1.81 us -> 1.25 us  [line_device(): given = lax.ppermute(first, 'orb', swap)]
    pallas_call x2 -> x3, Pallas kernels: 1.89 us -> 2.45 us  [the longest x1 1.83 us: line_device(): call(finish_kernel, block, 'vvvvvvvv', [pltpu.VMEM(block.shape, jnp.float...]
    ppermute x1, starting transfers between devices: 0.01 us -> 0.53 us  [line_device(): given = lax.ppermute(first, 'orb', swap)]
  transfers between devices with their start and end apart: 14 -> 15, of which waited for: 7 -> 5; matrix products, arithmetic and copies ran while one was open for 0% -> 0% of each run, Pallas kernels for 10% -> 14%
where the time goes in v7:
time: 46.2 us; the launch traced here: 46 us
  starting transfers between devices  24.6 us (53%)
  waiting for transfers between devices  11.6 us (25%)
  Pallas kernels  7.25 us (16%)
  local copies, waits for them, and re-layouts  1.72 us (4%)
  between operations  0.85 us (2%)
    ppermute x1, starting transfers between devices, line_device(): fourth_out = lax.ppermute(fourth, 'orb', swap)  8.86 us
    ppermute x1, waiting for transfers between devices, line_device(): pair = lax.ppermute(psi, 'orb', swap)  7.58 us
    ppermute x1, starting transfers between devices, line_device(): given_correlation = lax.ppermute(sent, 'orb', swap)  4.1 us
    ppermute x1, starting transfers between devices, line_device(): third_out = lax.ppermute(third, 'orb', swap)  3.31 us
    ppermute x1, starting transfers between devices, line_device(): pair = lax.ppermute(psi, 'orb', swap)  3.09 us
    ppermute x1, starting transfers between devices, line_device(): sent2 = lax.ppermute(second, 'orb', [(i, i ^ 2) for i in range(4)])  2.24 us
    pallas_call x1, Pallas kernels, line_device(): call(finish_kernel, block, 'vvvvvvvv', [pltpu.VMEM(block.shape, jnp.float...  1.83 us
    unnamed x12, local copies, waits for them, and re-layouts  1.72 us
  transfers between devices with their start and end apart: 15, of which 5 were waited for; matrix products, arithmetic and copies ran while one was open for 0% of the time, Pallas kernels for 14%

profile of v7, /device:TPU:0, one launch (start us, length us, event | category | flops | bytes accessed | tf_op | source)
XLA Modules:
  0.0 46.0 jit_solution(14399708626070681791)
XLA Ops:
  0.6 0.0 copy-start.2
  0.6 3.1 %collective-permute-start = (f32[8,16,1024]{2,1,0:T(8,128)}, f32[8,16,1024]{2,1,0:T(8,128)S(1)}, u32[]{:S(2)}, u32[]{:S(2)}) collective-permute-start(f32[8,16,1024]{2,1,0:T(8,128)} %psi_ref.3), channel_id=1, source_target_pairs={{0,4},{4,0},{8,12},{12,8},{1,5},{5,1},{9,13},{13,9},{2,6},{6,2},{1... | collective-permute-start | bytes 1572872 | tf_op jit(solution)/shard_map/ppermute | solution.py:445
  3.7 0.0 collective-permute-start.1
  3.7 0.0 copy-start.3
  3.8 0.5 %collective-permute-start.4 = (f32[8,16,1024]{2,1,0:T(8,128)}, f32[8,16,1024]{2,1,0:T(8,128)S(1)}, u32[]{:S(2)}, u32[]{:S(2)}) collective-permute-start(f32[8,16,1024]{2,1,0:T(8,128)} %psi_ref.3), channel_id=1, source_target_pairs={{0,1},{1,0},{2,3},{3,2},{4,5},{5,4},{6,7},{7,6},{8,9},{9,8},{10,11... | collective-permute-start | bytes 1572872 | tf_op jit(solution)/shard_map/ppermute | solution.py:449
  4.2 1.2 %collective-permute-start.3 = (f32[8,16,1024]{2,1,0:T(8,128)}, f32[8,16,1024]{2,1,0:T(8,128)S(1)}, u32[]{:S(2)}, u32[]{:S(2)}) collective-permute-start(f32[8,16,1024]{2,1,0:T(8,128)} %psi_ref.3), channel_id=1, source_target_pairs={{0,3},{1,2},{2,1},{3,0},{4,7},{5,6},{6,5},{7,4},{8,11},{9,10},{10,... | collective-permute-start | bytes 1572872 | tf_op jit(solution)/shard_map/ppermute | solution.py:450
  5.4 0.0 copy-start.5
  5.4 0.7 %copy-done.5 = s32[32]{0:T(128)S(1)} copy-done((s32[32]{0:T(128)S(1)}, s32[32]{0:T(128)}, u32[]{:S(2)}) %copy-start.5) | copy-done | bytes 152
  6.1 0.6 %shard_map.69.live_ref = f32[32,1024]{1,0:T(8,128)S(1)} custom-call(s32[8,1024]{1,0:T(8,128)S(1)} %shard_map.68.columns_ref, s32[32]{0:T(128)S(1)} %copy-done.5), custom_call_target="tpu_custom_call" | custom-call | flops 1 | bytes 1 | tf_op jit(solution)/shard_map/pallas_call | solution.py:452
  6.7 0.0 copy-done.2
  6.7 0.0 copy-done.3
  6.7 0.0 copy-start
  6.7 1.0 %copy-done = f32[8,16,1024]{2,1,0:T(8,128)S(1)} copy-done((f32[8,16,1024]{2,1,0:T(8,128)S(1)}, f32[8,16,1024]{2,1,0:T(8,128)}, u32[]{:S(2)}) %copy-start) | copy-done | bytes 524312
  7.7 0.5 %shard_map.70 = (f32[8,16,1024]{2,1,0:T(8,128)S(1)}, bf16[256,1024]{1,0:T(8,128)(2,1)S(1)}, f32[128,1024]{1,0:T(8,128)S(1)}) custom-call(f32[8,16,1024]{2,1,0:T(8,128)S(1)} %copy-done, f32[16,1024]{1,0:T(8,128)S(1)} %copy-done.3, f32[32,1024]{1,0:T(8,128)S(1)} %shard_map.69.live_ref, bf16[256,256]{1,0:T(8,128)(2,1)S(1)} %copy-done.2), custom_call_target="tpu_custom_call" | custom-call | flops 1 | bytes 1 | tf_op jit(solution)/shard_map/pallas_call | solution.py:455
  8.3 7.6 %collective-permute-done.psi_ref = f32[8,16,1024]{2,1,0:T(8,128)S(1)} collective-permute-done((f32[8,16,1024]{2,1,0:T(8,128)}, f32[8,16,1024]{2,1,0:T(8,128)S(1)}, u32[]{:S(2)}, u32[]{:S(2)}) %collective-permute-start) | collective-permute-done | bytes 524320 | tf_op jit(solution)/shard_map/ppermute | solution.py:445
  15.9 0.0 collective-permute-start.2
  15.9 0.0 collective-permute-done.1.field_ref
  15.9 3.3 %collective-permute-start.5 = (f32[8,16,1024]{2,1,0:T(8,128)S(1)}, f32[8,16,1024]{2,1,0:T(8,128)S(1)}, u32[]{:S(2)}, u32[]{:S(2)}) collective-permute-start(f32[8,16,1024]{2,1,0:T(8,128)S(1)} %collective-permute-done.1.field_ref), channel_id=1, source_target_pairs={{0,4},{4,0},{8,12},{12,8},{1,5},{5,1},{9,13},{13,9},{2,6},{6,2},{1... | collective-permute-start | bytes 1572872 | tf_op jit(solution)/shard_map/ppermute | solution.py:460
  19.2 0.1 shard_map.72.refs_2_.third_ref.third_parts
  19.3 0.0 copy-start.1
  19.3 0.0 copy-start.4
  19.3 0.1 collective-permute-start.6
  19.4 0.0 collective-permute-done.4.near_ref
  19.4 0.5 %collective-permute-start.7 = (f32[8,16,1024]{2,1,0:T(8,128)S(1)}, f32[8,16,1024]{2,1,0:T(8,128)S(1)}, u32[]{:S(2)}, u32[]{:S(2)}) collective-permute-start(f32[8,16,1024]{2,1,0:T(8,128)S(1)} %collective-permute-done.psi_ref), channel_id=1, source_target_pairs={{0,1},{1,0},{2,3},{3,2},{4,5},{5,4},{6,7},{7,6},{8,9},{9,8},{10,11... | collective-permute-start | bytes 1572872 | tf_op jit(solution)/shard_map/ppermute | solution.py:464
  19.9 0.5 %shard_map.71 = (f32[8,16,1024]{2,1,0:T(8,128)S(1)}, bf16[256,1024]{1,0:T(8,128)(2,1)S(1)}, f32[128,1024]{1,0:T(8,128)S(1)}) custom-call(f32[8,16,1024]{2,1,0:T(8,128)S(1)} %collective-permute-done.psi_ref, f32[16,1024]{1,0:T(8,128)S(1)} %copy-done.3, f32[32,1024]{1,0:T(8,128)S(1)} %shard_map.69.live_ref, bf16[256,256]{1,0:T(8,128)(2,1)S(1)} %copy-done.2), custom_call_target="tpu_custom_call" | custom-call | flops 1 | bytes 1 | tf_op jit(solution)/shard_map/pallas_call | solution.py:469
  20.4 0.0 collective-permute-done.3.far_ref
  20.4 0.0 copy-done.1
  20.4 0.0 copy-done.4
  20.5 0.4 shard_map.73
  20.9 0.6 %shard_map.74.early_ref = f32[24,128]{1,0:T(8,128)S(1)} custom-call(bf16[256,1024]{1,0:T(8,128)(2,1)S(1)} %get-tuple-element.43.refs_0_.own_ref.own_parts, bf16[256,1024]{1,0:T(8,128)(2,1)S(1)} %get-tuple-element.44.refs_1_.pair_ref.pair_parts, bf16[256,1024]{1,0:T(8,128)(2,1)S(1)} %shard_map.72.refs_2_.third_ref.third_parts, ...), custom_call_target="tpu_custom_call" | custom-call | flops 1 | bytes 1 | tf_op jit(solution)/shard_map/pallas_call | solution.py:472
  21.5 0.0 collective-permute-done.2.field_ref
  21.5 8.9 %collective-permute-start.13 = (f32[8,16,1024]{2,1,0:T(8,128)S(1)}, f32[8,16,1024]{2,1,0:T(8,128)S(1)}, u32[]{:S(2)}, u32[]{:S(2)}) collective-permute-start(f32[8,16,1024]{2,1,0:T(8,128)S(1)} %collective-permute-done.2.field_ref), channel_id=1, source_target_pairs={{0,4},{4,0},{8,12},{12,8},{1,5},{5,1},{9,13},{13,9},{2,6},{6,2},{1... | collective-permute-start | bytes 1572872 | tf_op jit(solution)/shard_map/ppermute | solution.py:479
  30.4 0.1 shard_map.75.refs_0_.fourth_ref.fourth_parts
  30.5 0.6 %collective-permute-done.5.third_ref = f32[8,16,1024]{2,1,0:T(8,128)S(1)} collective-permute-done((f32[8,16,1024]{2,1,0:T(8,128)S(1)}, f32[8,16,1024]{2,1,0:T(8,128)S(1)}, u32[]{:S(2)}, u32[]{:S(2)}) %collective-permute-start.5) | collective-permute-done | bytes 524320 | tf_op jit(solution)/shard_map/ppermute | solution.py:460
  31.1 0.3 shard_map.77.last_ref
  31.4 0.0 collective-permute-done.6.far_ref
  31.4 0.0 collective-permute-done.7.near_ref
  31.4 0.4 shard_map.76
  31.9 0.9 %shard_map.78.refs_0_ = f32[32,16]{1,0:T(8,128)S(1)} custom-call(bf16[256,1024]{1,0:T(8,128)(2,1)S(1)} %get-tuple-element.43.refs_0_.own_ref.own_parts, bf16[256,1024]{1,0:T(8,128)(2,1)S(1)} %get-tuple-element.44.refs_1_.pair_ref.pair_parts, bf16[256,1024]{1,0:T(8,128)(2,1)S(1)} %shard_map.72.refs_2_.third_ref.third_parts, ...), custom_call_target="tpu_custom_call" | custom-call | flops 1 | bytes 1 | tf_op jit(solution)/shard_map/pallas_call | solution.py:490
  32.8 0.1 collective-permute-start.8
  32.9 1.2 %collective-permute-done.8.refs_1_ = f32[32,16]{1,0:T(8,128)S(1)} collective-permute-done((f32[32,16]{1,0:T(8,128)S(1)}, f32[32,16]{1,0:T(8,128)S(1)}, u32[]{:S(2)}, u32[]{:S(2)}) %collective-permute-start.8) | collective-permute-done | bytes 2080 | tf_op jit(solution)/shard_map/ppermute | solution.py:496
  34.1 0.2 collective-permute-start.9
  34.2 1.0 %collective-permute-done.9.other_ref = f32[32,16]{1,0:T(8,128)S(1)} collective-permute-done((f32[32,16]{1,0:T(8,128)S(1)}, f32[32,16]{1,0:T(8,128)S(1)}, u32[]{:S(2)}, u32[]{:S(2)}) %collective-permute-start.9) | collective-permute-done | bytes 2080 | tf_op jit(solution)/shard_map/ppermute | solution.py:501
  35.3 4.1 %collective-permute-start.14 = (f32[40,256]{1,0:T(8,128)S(1)}, f32[40,256]{1,0:T(8,128)S(1)}, u32[]{:S(2)}, u32[]{:S(2)}) collective-permute-start(f32[40,256]{1,0:T(8,128)S(1)} %get-tuple-element.65), channel_id=1, source_target_pairs={{0,4},{4,0},{8,12},{12,8},{1,5},{5,1},{9,13},{13,9},{2,6},{6,2},{1... | collective-permute-start | bytes 122888 | tf_op jit(solution)/shard_map/ppermute | solution.py:503
  39.4 2.2 %collective-permute-start.10 = (f32[32,256]{1,0:T(8,128)S(1)}, f32[32,256]{1,0:T(8,128)S(1)}, u32[]{:S(2)}, u32[]{:S(2)}) collective-permute-start(f32[32,256]{1,0:T(8,128)S(1)} %get-tuple-element.59), channel_id=1, source_target_pairs={{0,8},{4,12},{8,0},{12,4},{1,9},{5,13},{9,1},{13,5},{2,10},{6,14},... | collective-permute-start | bytes 98312 | tf_op jit(solution)/shard_map/ppermute | solution.py:518
  41.6 0.5 %collective-permute-start.12 = (f32[24,256]{1,0:T(8,128)S(1)}, f32[24,256]{1,0:T(8,128)S(1)}, u32[]{:S(2)}, u32[]{:S(2)}) collective-permute-start(f32[24,256]{1,0:T(8,128)S(1)} %get-tuple-element.61), channel_id=1, source_target_pairs={{0,4},{4,0},{8,12},{12,8},{1,5},{5,1},{9,13},{13,9},{2,6},{6,2},{1... | collective-permute-start | bytes 73736 | tf_op jit(solution)/shard_map/ppermute | solution.py:517
  42.1 0.0 collective-permute-start.11
  42.1 0.0 collective-permute-done.13.fourth_ref
  42.1 0.2 shard_map.82
  42.3 0.0 collective-permute-done.14.corr_ref
  42.3 1.8 %shard_map.83 = f32[8,16,1024]{2,1,0:T(8,128)} custom-call(f32[128,1024]{1,0:T(8,128)S(1)} %get-tuple-element.38.own_phi, bf16[256,1024]{1,0:T(8,128)(2,1)S(1)} %get-tuple-element.43.refs_0_.own_ref.own_parts, bf16[256,1024]{1,0:T(8,128)(2,1)S(1)} %get-tuple-element.44.refs_1_.pair_ref.pair_parts, bf16[256,1024]{1,0:T(8,128)(2,1)S(1)} %get-tuple-element.63.third_parts, ...), custom_call_target="tpu_custom_call" | custom-call | flops 1 | bytes 1 | tf_op jit(solution)/shard_map/pallas_call | solution.py:523
  44.2 0.0 collective-permute-done.11.sent3_ref
  44.2 1.2 %collective-permute-done.12.given_ref = f32[24,256]{1,0:T(8,128)S(1)} collective-permute-done((f32[24,256]{1,0:T(8,128)S(1)}, f32[24,256]{1,0:T(8,128)S(1)}, u32[]{:S(2)}, u32[]{:S(2)}) %collective-permute-start.12) | collective-permute-done | bytes 24608 | tf_op jit(solution)/shard_map/ppermute | solution.py:517
  45.4 0.0 collective-permute-done.10.sent2_ref
  45.4 0.6 %shard_map.84 = f32[16,256]{1,0:T(8,128)} custom-call(f32[32,256]{1,0:T(8,128)S(1)} %collective-permute-done.10.sent2_ref, f32[16,256]{1,0:T(8,128)S(1)} %collective-permute-done.11.sent3_ref, f32[24,256]{1,0:T(8,128)S(1)} %collective-permute-done.12.given_ref, f32[16,256]{1,0:T(8,128)S(1)} %get-tuple-element.71.kept_ref), custom_call_target="tpu_custom_call" | custom-call | flops 1 | bytes 1 | tf_op jit(solution)/shard_map/pallas_call | solution.py:534
  (4 shorter events, 0.0 us)
Async XLA Ops:
  0.6 6.0 %copy-start.2 = (bf16[256,256]{1,0:T(8,128)(2,1)S(1)}, bf16[256,256]{1,0:T(8,128)(2,1)}, u32[]{:S(2)}) copy-start(bf16[256,256]{1,0:T(8,128)(2,1)} %constant.4.clone.band_ref) | copy-start | bytes 393220
  0.6 15.2 %collective-permute-start = (f32[8,16,1024]{2,1,0:T(8,128)}, f32[8,16,1024]{2,1,0:T(8,128)S(1)}, u32[]{:S(2)}, u32[]{:S(2)}) collective-permute-start(f32[8,16,1024]{2,1,0:T(8,128)} %psi_ref.3), channel_id=1, source_target_pairs={{0,4},{4,0},{8,12},{12,8},{1,5},{5,1},{9,13},{13,9},{2,6},{6,2},{1... | collective-permute-start | bytes 1572872 | tf_op jit(solution)/shard_map/ppermute | solution.py:445
  3.7 12.1 %collective-permute-start.1 = (f32[8,16,1024]{2,1,0:T(8,128)}, f32[8,16,1024]{2,1,0:T(8,128)S(1)}, u32[]{:S(2)}, u32[]{:S(2)}) collective-permute-start(f32[8,16,1024]{2,1,0:T(8,128)} %psi_ref.3), channel_id=1, source_target_pairs={{4,8},{5,9},{6,10},{7,11},{8,4},{9,5},{10,6},{11,7},{0,1},{1,0},{2... | collective-permute-start | bytes 1572872 | tf_op jit(solution)/shard_map/ppermute | solution.py:446
  3.7 2.9 %copy-start.3 = (f32[16,1024]{1,0:T(8,128)S(1)}, f32[16,1024]{1,0:T(8,128)}, u32[]{:S(2)}) copy-start(f32[16,1024]{1,0:T(8,128)} %potential_ref.3) | copy-start | bytes 196612
  3.8 15.6 %collective-permute-start.4 = (f32[8,16,1024]{2,1,0:T(8,128)}, f32[8,16,1024]{2,1,0:T(8,128)S(1)}, u32[]{:S(2)}, u32[]{:S(2)}) collective-permute-start(f32[8,16,1024]{2,1,0:T(8,128)} %psi_ref.3), channel_id=1, source_target_pairs={{0,1},{1,0},{2,3},{3,2},{4,5},{5,4},{6,7},{7,6},{8,9},{9,8},{10,11... | collective-permute-start | bytes 1572872 | tf_op jit(solution)/shard_map/ppermute | solution.py:449
  4.2 16.2 %collective-permute-start.3 = (f32[8,16,1024]{2,1,0:T(8,128)}, f32[8,16,1024]{2,1,0:T(8,128)S(1)}, u32[]{:S(2)}, u32[]{:S(2)}) collective-permute-start(f32[8,16,1024]{2,1,0:T(8,128)} %psi_ref.3), channel_id=1, source_target_pairs={{0,3},{1,2},{2,1},{3,0},{4,7},{5,6},{6,5},{7,4},{8,11},{9,10},{10,... | collective-permute-start | bytes 1572872 | tf_op jit(solution)/shard_map/ppermute | solution.py:450
  5.4 0.7 %copy-start.5 = (s32[32]{0:T(128)S(1)}, s32[32]{0:T(128)}, u32[]{:S(2)}) copy-start(s32[32]{0:T(128)} %extent_ref.1) | copy-start | bytes 388
  6.7 1.0 %copy-start = (f32[8,16,1024]{2,1,0:T(8,128)S(1)}, f32[8,16,1024]{2,1,0:T(8,128)}, u32[]{:S(2)}) copy-start(f32[8,16,1024]{2,1,0:T(8,128)} %psi_ref.3) | copy-start | bytes 1572868
  15.9 5.7 %collective-permute-start.2 = (f32[8,16,1024]{2,1,0:T(8,128)S(1)}, f32[8,16,1024]{2,1,0:T(8,128)S(1)}, u32[]{:S(2)}, u32[]{:S(2)}) collective-permute-start(f32[8,16,1024]{2,1,0:T(8,128)S(1)} %collective-permute-done.psi_ref), channel_id=1, source_target_pairs={{4,8},{5,9},{6,10},{7,11},{8,4},{9,5},{10,6},{11,7},{0,1},{1,0},{2... | collective-permute-start | bytes 1572872 | tf_op jit(solution)/shard_map/ppermute | solution.py:459
  15.9 15.2 %collective-permute-start.5 = (f32[8,16,1024]{2,1,0:T(8,128)S(1)}, f32[8,16,1024]{2,1,0:T(8,128)S(1)}, u32[]{:S(2)}, u32[]{:S(2)}) collective-permute-start(f32[8,16,1024]{2,1,0:T(8,128)S(1)} %collective-permute-done.1.field_ref), channel_id=1, source_target_pairs={{0,4},{4,0},{8,12},{12,8},{1,5},{5,1},{9,13},{13,9},{2,6},{6,2},{1... | collective-permute-start | bytes 1572872 | tf_op jit(solution)/shard_map/ppermute | solution.py:460
  19.3 1.2 %copy-start.1 = (f32[8,16,1024]{2,1,0:T(8,128)S(1)}, f32[8,16,1024]{2,1,0:T(8,128)}, u32[]{:S(2)}) copy-start(f32[8,16,1024]{2,1,0:T(8,128)} %psi_ref.3) | copy-start | bytes 1572868
  19.3 1.2 %copy-start.4 = (bf16[2,16,144]{2,1,0:T(8,128)(2,1)S(1)}, bf16[2,16,144]{2,1,0:T(8,128)(2,1)}, u32[]{:S(2)}) copy-start(bf16[2,16,144]{2,1,0:T(8,128)(2,1)} %constant.5.clone.band_ref) | copy-start | bytes 27652
  19.3 12.1 %collective-permute-start.6 = (f32[8,16,1024]{2,1,0:T(8,128)S(1)}, f32[8,16,1024]{2,1,0:T(8,128)S(1)}, u32[]{:S(2)}, u32[]{:S(2)}) collective-permute-start(f32[8,16,1024]{2,1,0:T(8,128)S(1)} %collective-permute-done.psi_ref), channel_id=1, source_target_pairs={{4,7},{5,6},{6,5},{7,4},{8,11},{9,10},{10,9},{11,8},{0,1},{1,0},{2... | collective-permute-start | bytes 1572872 | tf_op jit(solution)/shard_map/ppermute | solution.py:463
  19.4 12.0 %collective-permute-start.7 = (f32[8,16,1024]{2,1,0:T(8,128)S(1)}, f32[8,16,1024]{2,1,0:T(8,128)S(1)}, u32[]{:S(2)}, u32[]{:S(2)}) collective-permute-start(f32[8,16,1024]{2,1,0:T(8,128)S(1)} %collective-permute-done.psi_ref), channel_id=1, source_target_pairs={{0,1},{1,0},{2,3},{3,2},{4,5},{5,4},{6,7},{7,6},{8,9},{9,8},{10,11... | collective-permute-start | bytes 1572872 | tf_op jit(solution)/shard_map/ppermute | solution.py:464
  21.5 20.6 %collective-permute-start.13 = (f32[8,16,1024]{2,1,0:T(8,128)S(1)}, f32[8,16,1024]{2,1,0:T(8,128)S(1)}, u32[]{:S(2)}, u32[]{:S(2)}) collective-permute-start(f32[8,16,1024]{2,1,0:T(8,128)S(1)} %collective-permute-done.2.field_ref), channel_id=1, source_target_pairs={{0,4},{4,0},{8,12},{12,8},{1,5},{5,1},{9,13},{13,9},{2,6},{6,2},{1... | collective-permute-start | bytes 1572872 | tf_op jit(solution)/shard_map/ppermute | solution.py:479
  32.8 1.2 %collective-permute-start.8 = (f32[32,16]{1,0:T(8,128)S(1)}, f32[32,16]{1,0:T(8,128)S(1)}, u32[]{:S(2)}, u32[]{:S(2)}) collective-permute-start(f32[32,16]{1,0:T(8,128)S(1)} %shard_map.78.refs_0_), channel_id=1, source_target_pairs={{0,1},{1,0},{2,3},{3,2},{4,5},{5,4},{6,7},{7,6},{8,9},{9,8},{10,11... | collective-permute-start | bytes 6152 | tf_op jit(solution)/shard_map/ppermute | solution.py:496
  34.1 1.2 %collective-permute-start.9 = (f32[32,16]{1,0:T(8,128)S(1)}, f32[32,16]{1,0:T(8,128)S(1)}, u32[]{:S(2)}, u32[]{:S(2)}) collective-permute-start(f32[32,16]{1,0:T(8,128)S(1)} %shard_map.79.part_ref), channel_id=1, source_target_pairs={{4,7},{5,6},{6,5},{7,4},{8,11},{9,10},{10,9},{11,8},{0,1},{1,0},{2... | collective-permute-start | bytes 6152 | tf_op jit(solution)/shard_map/ppermute | solution.py:501
  35.3 7.1 %collective-permute-start.14 = (f32[40,256]{1,0:T(8,128)S(1)}, f32[40,256]{1,0:T(8,128)S(1)}, u32[]{:S(2)}, u32[]{:S(2)}) collective-permute-start(f32[40,256]{1,0:T(8,128)S(1)} %get-tuple-element.65), channel_id=1, source_target_pairs={{0,4},{4,0},{8,12},{12,8},{1,5},{5,1},{9,13},{13,9},{2,6},{6,2},{1... | collective-permute-start | bytes 122888 | tf_op jit(solution)/shard_map/ppermute | solution.py:503
  39.4 6.1 %collective-permute-start.10 = (f32[32,256]{1,0:T(8,128)S(1)}, f32[32,256]{1,0:T(8,128)S(1)}, u32[]{:S(2)}, u32[]{:S(2)}) collective-permute-start(f32[32,256]{1,0:T(8,128)S(1)} %get-tuple-element.59), channel_id=1, source_target_pairs={{0,8},{4,12},{8,0},{12,4},{1,9},{5,13},{9,1},{13,5},{2,10},{6,14},... | collective-permute-start | bytes 98312 | tf_op jit(solution)/shard_map/ppermute | solution.py:518
  41.6 3.8 %collective-permute-start.12 = (f32[24,256]{1,0:T(8,128)S(1)}, f32[24,256]{1,0:T(8,128)S(1)}, u32[]{:S(2)}, u32[]{:S(2)}) collective-permute-start(f32[24,256]{1,0:T(8,128)S(1)} %get-tuple-element.61), channel_id=1, source_target_pairs={{0,4},{4,0},{8,12},{12,8},{1,5},{5,1},{9,13},{13,9},{2,6},{6,2},{1... | collective-permute-start | bytes 73736 | tf_op jit(solution)/shard_map/ppermute | solution.py:517
  42.1 2.0 %collective-permute-start.11 = (f32[16,256]{1,0:T(8,128)S(1)}, f32[16,256]{1,0:T(8,128)S(1)}, u32[]{:S(2)}, u32[]{:S(2)}) collective-permute-start(f32[16,256]{1,0:T(8,128)S(1)} %get-tuple-element.60), channel_id=1, source_target_pairs={{4,8},{5,9},{6,10},{7,11},{8,4},{9,5},{10,6},{11,7},{0,1},{1,0},{2... | collective-permute-start | bytes 49160 | tf_op jit(solution)/shard_map/ppermute | solution.py:519

commit v8 on v7

--- a/solution.py
+++ b/solution.py
@@ -155,20 +155,48 @@
 
 
 def masked(field_ref, a, live_ref, f):
-    at = f * field_ref.shape[0] + a
+    at = f * (live_ref.shape[0] // 4) + a
     return field_ref[a] * live_ref[at : at + 1, :]
 
 
+def split_one(parts_ref, value, a):
+    planes = value.shape[0]
+    half = parts_ref.shape[0] // 2
+    high, low = two_parts(value)
+    parts_ref[a * planes : (a + 1) * planes, :] = high
+    parts_ref[half + a * planes : half + (a + 1) * planes, :] = low
+
+
 def split_into(parts_ref, field_ref, live_ref, f):
-    orbs, planes, _ = field_ref.shape
-    for a in range(orbs):
-        high, low = two_parts(masked(field_ref, a, live_ref, f))
-        parts_ref[a * planes : (a + 1) * planes, :] = high
-        parts_ref[(orbs + a) * planes : (orbs + a + 1) * planes, :] = low
+    for a in range(field_ref.shape[0]):
+        split_one(parts_ref, masked(field_ref, a, live_ref, f), a)
 
 
 def split_kernel(f, field_ref, live_ref, parts_ref):
     split_into(parts_ref, field_ref, live_ref, f)
+
+
+def short_rows(planes):
+    spare = planes - reach
+    for parity, first in ((0, 0), (1, spare)):
+        free = reach if parity == 0 else 0
+        each = reach // spare
+        yield parity, [(free + p // each, p % each, first + p) for p in range(reach)]
+
+
+def shorten_kernel(psi_ref, short_ref):
+    orbs, planes, _ = psi_ref.shape
+    width = short_ref.shape[2]
+    short_ref[...] = psi_ref[:, :, :width]
+    for parity, moves in short_rows(planes):
+
+        @pl.when(lax.axis_index("cmp") % 2 == parity)
+        def _():
+            for a in range(orbs):
+                for row, place, plane in moves:
+                    short_ref[a, row : row + 1, place * lanes : (place + 1) * lanes] = psi_ref[
+                        a, plane : plane + 1, width:
+                    ]
 
 
 def local_kernel(f, psi_ref, potential_ref, live_ref, band_ref, out_ref, parts_ref, phi_ref):
@@ -196,12 +224,25 @@
 
 
 def plane_kernel(
-    f, far_ref, psi_ref, near_ref, local_ref, live_ref, band_ref, out_ref, parts_ref
+    f, far_ref, psi_ref, near_ref, local_ref, live_ref, band_ref, out_ref, parts_ref, *rest_ref
 ):
     orbs, planes, _ = psi_ref.shape
     band = band_ref[lax.axis_index("cmp") % 2]
+    for ref in rest_ref:
+        ref[...] = jnp.zeros_like(ref)
+        for parity, moves in short_rows(planes):
+
+            @pl.when(lax.axis_index("cmp") % 2 != parity)
+            def _():
+                for a in range(orbs):
+                    for row, place, plane in moves:
+                        ref[a, plane : plane + 1, :] = far_ref[
+                            a, row : row + 1, place * lanes : (place + 1) * lanes
+                        ]
+
     for a in range(orbs):
-        slab = jnp.concatenate([far_ref[a], psi_ref[a], near_ref[a]], axis=0)
+        far = jnp.concatenate([far_ref[a]] + [ref[a] for ref in rest_ref], axis=1)
+        slab = jnp.concatenate([far, psi_ref[a], near_ref[a]], axis=0)
         high, low = two_parts(slab)
         second = jnp.dot(
             band, jnp.concatenate([high, low, high], axis=0), preferred_element_type=jnp.float32
@@ -265,10 +306,16 @@
     refs[-1][...] = total
 
 
-def correlation_sum_kernel(part_ref, other_ref, out_ref, sent_ref):
+def correlation_sum_kernel(part_ref, other_ref, fourth_ref, out_ref, sent_ref):
+    orbs, planes, _ = fourth_ref.shape
+    width = sent_ref.shape[1]
     total = part_ref[...] + other_ref[...]
     out_ref[...] = total
-    sent_ref[: total.shape[0], : total.shape[1]] = total
+    across = total.shape[1]
+    for k in range(4):
+        sent_ref[:orbs, k * across : (k + 1) * across] = total[k * orbs : (k + 1) * orbs]
+        first = orbs + k * planes
+        sent_ref[first : first + planes, :] = fourth_ref[orbs - 1, :, k * width : (k + 1) * width]
 
 
 def spread_out(corr, planes):
@@ -351,11 +398,23 @@
             part_ref[:planes, :] = all_ref[:, pl.ds(first, share)]
 
 
-def outer_split_kernel(third_ref, fourth_ref, live_ref, third_parts, fourth_parts):
+def all_but_last_kernel(field_ref, out_ref):
+    out_ref[...] = field_ref[: out_ref.shape[0]]
+
+
+def outer_split_kernel(third_ref, fourth_ref, sent_ref, live_ref, third_parts, fourth_parts):
+    orbs, planes, _ = third_ref.shape
+
     @pl.when(jnp.logical_not(on_inner()))
     def _():
         split_into(third_parts, third_ref, live_ref, 2)
         split_into(fourth_parts, fourth_ref, live_ref, 3)
+        first = orbs
+        value = jnp.concatenate(
+            [sent_ref[first + k * planes : first + (k + 1) * planes, :] for k in range(4)], axis=1
+        )
+        at = 4 * orbs - 1
+        split_one(fourth_parts, value * live_ref[at : at + 1, :], orbs - 1)
 
 
 def finish_kernel(
@@ -376,8 +435,9 @@
 
     @pl.when(jnp.logical_not(on_inner()))
     def _():
-        corr = corr_ref[: 4 * orbs, orbs : 2 * orbs]
-        corr = jnp.concatenate([corr[orbs : 2 * orbs], corr[:orbs], corr[2 * orbs :]], axis=0)
+        corr = jnp.concatenate(
+            [corr_ref[:orbs, (2 * k + 1) * orbs : (2 * k + 2) * orbs] for k in (1, 0, 2, 3)], axis=0
+        )
         high, low = spread_out(corr, planes)
         fields = (own_parts, pair_parts, third_parts, fourth_parts)
         for c in range(grid_p // width):
@@ -459,8 +519,8 @@
     fourth = lax.ppermute(pair, line, across)
     third_out = lax.ppermute(third, "orb", swap)
     third_parts = call(functools.partial(split_kernel, 2), parts, "vv")(third, live)
-    turn, third_parts = lax.optimization_barrier((pair, third_parts))
-    pair_far = lax.ppermute(turn, line, inner_far)
+    short = jax.ShapeDtypeStruct((orbs, planes, grid_p - lanes), jnp.float32)
+    pair_far = lax.ppermute(call(shorten_kernel, short, "v")(pair), line, inner_far)
     pair_near = lax.ppermute(pair, "cmp", to_near)
 
     image, image_parts = call(functools.partial(plane_kernel, 0), (block, parts), "vvvvvv")(
@@ -476,12 +536,18 @@
     )(own_parts, pair_parts, third_parts, image_parts)
 
     fourth, ward_local, early = lax.optimization_barrier((fourth, ward_local, early))
-    fourth_out = lax.ppermute(fourth, "orb", swap)
-    ward, ward_parts = call(functools.partial(plane_kernel, 1), (block, parts), "vvvvvv")(
+    most = jax.ShapeDtypeStruct((orbs - 1, planes, grid_p), jnp.float32)
+    fourth_out = lax.ppermute(call(all_but_last_kernel, most, "v")(fourth), "orb", swap)
+    pair_far, third_out = lax.optimization_barrier((pair_far, third_out))
+    ward, ward_parts = call(
+        functools.partial(plane_kernel, 1),
+        (block, parts),
+        "vvvvvv",
+        [pltpu.VMEM((orbs, planes, lanes), jnp.float32)],
+    )(
         pair_far, pair, pair_near, ward_local, live, bands
     )
     fourth_parts = call(functools.partial(split_kernel, 3), parts, "vv")(fourth, live)
-    fourth_parts, third_out = lax.optimization_barrier((fourth_parts, third_out))
     last = call(
         functools.partial(overlap_kernel, planes, 1),
         jax.ShapeDtypeStruct((orbs, rows), jnp.float32),
@@ -496,9 +562,9 @@
     chip = call(sum_kernel, small, "vv")(part, lax.ppermute(part, "cmp", to_near))
     correlation, sent = call(
         correlation_sum_kernel,
-        (small, jax.ShapeDtypeStruct((5 * orbs, grid_p // 4), jnp.float32)),
-        "vv",
-    )(chip, lax.ppermute(chip, line, inner_far))
+        (small, jax.ShapeDtypeStruct((orbs + 4 * planes, grid_p // 4), jnp.float32)),
+        "vvv",
+    )(chip, lax.ppermute(chip, line, inner_far), fourth)
 
     given_correlation = lax.ppermute(sent, "orb", swap)
 
@@ -517,8 +583,8 @@
     given = lax.ppermute(first, "orb", swap)
     sent2 = lax.ppermute(second, "orb", [(i, i ^ 2) for i in range(4)])
     sent3 = lax.ppermute(last, line, across)
-    third_held, fourth_held = call(outer_split_kernel, (parts, parts), "vvv")(
-        third_out, fourth_out, live
+    third_held, fourth_held = call(outer_split_kernel, (parts, parts), "vvvv")(
+        third_out, fourth_out, given_correlation, live
     )
     new = call(
         finish_kernel,
@@ -542,7 +608,7 @@
         and lax.axis_size("cmp") == 4
         and orbs == 8
         and planes == 16
-        and grid_p % (4 * lanes) == 0
+        and grid_p == lanes * (reach // (planes - reach) + 1)
     )
     return (line_device if fits else general_device)(psi, potential, extent)
 

time: 46.2 us -> 45.4 us (0.983)
  starting transfers between devices: 24.6 us -> 23.2 us
  local copies, waits for them, and re-layouts: 1.72 us -> 2.62 us
  waiting for transfers between devices: 11.6 us -> 11 us
    unnamed x12, local copies, waits for them, and re-layouts: 1.72 us -> 2.62 us
    ppermute x1, starting transfers between devices: 4.1 us -> 3.21 us  [line_device(): given_correlation = lax.ppermute(sent, 'orb', swap)]
    ppermute x1, waiting for transfers between devices: 0.57 us -> 0.01 us  [line_device(): third_out = lax.ppermute(third, 'orb', swap)]
    ppermute x1, starting transfers between devices: 0.49 us -> 0.01 us  [line_device(): pair_near = lax.ppermute(pair, 'cmp', to_near)]
  transfers between devices with their start and end apart: 15 -> 15, of which waited for: 5 -> 5; matrix products, arithmetic and copies ran while one was open for 0% -> 0% of each run, Pallas kernels for 14% -> 15%
where the time goes in v8:
time: 45.4 us; the launch traced here: 45.2 us
  starting transfers between devices  23.2 us (51%)
  waiting for transfers between devices  11 us (24%)
  Pallas kernels  7.54 us (17%)
  local copies, waits for them, and re-layouts  2.62 us (6%)
  between operations  0.85 us (2%)
    ppermute x1, starting transfers between devices, line_device(): lax.ppermute(call(all_but_last_kernel, most, 'v')(fourth), 'orb', swap)  7.94 us
    ppermute x1, waiting for transfers between devices, line_device(): pair = lax.ppermute(psi, 'orb', swap)  7.59 us
    ppermute x1, starting transfers between devices, line_device(): third_out = lax.ppermute(third, 'orb', swap)  3.31 us
    ppermute x1, starting transfers between devices, line_device(): given_correlation = lax.ppermute(sent, 'orb', swap)  3.21 us
    ppermute x1, starting transfers between devices, line_device(): pair = lax.ppermute(psi, 'orb', swap)  3.09 us
    ppermute x1, starting transfers between devices, line_device(): sent2 = lax.ppermute(second, 'orb', [(i, i ^ 2) for i in range(4)])  2.67 us
    unnamed x12, local copies, waits for them, and re-layouts  2.62 us
    pallas_call x1, Pallas kernels, line_device(): call(finish_kernel, block, 'vvvvvvvv', [pltpu.VMEM(block.shape, jnp.float...  1.9 us
  transfers between devices with their start and end apart: 15, of which 5 were waited for; matrix products, arithmetic and copies ran while one was open for 0% of the time, Pallas kernels for 15%

profile of v8, /device:TPU:0, one launch (start us, length us, event | category | flops | bytes accessed | tf_op | source)
XLA Modules:
  0.0 45.2 jit_solution(3005361317632327376)
XLA Ops:
  0.6 0.0 copy-start.2
  0.6 3.1 %collective-permute-start = (f32[8,16,1024]{2,1,0:T(8,128)}, f32[8,16,1024]{2,1,0:T(8,128)S(1)}, u32[]{:S(2)}, u32[]{:S(2)}) collective-permute-start(f32[8,16,1024]{2,1,0:T(8,128)} %psi_ref.3), channel_id=1, source_target_pairs={{0,4},{4,0},{8,12},{12,8},{1,5},{5,1},{9,13},{13,9},{2,6},{6,2},{1... | collective-permute-start | bytes 1572872 | tf_op jit(solution)/shard_map/ppermute | solution.py:505
  3.7 0.0 collective-permute-start.1
  3.7 0.0 copy-start.3
  3.8 0.5 %collective-permute-start.4 = (f32[8,16,1024]{2,1,0:T(8,128)}, f32[8,16,1024]{2,1,0:T(8,128)S(1)}, u32[]{:S(2)}, u32[]{:S(2)}) collective-permute-start(f32[8,16,1024]{2,1,0:T(8,128)} %psi_ref.3), channel_id=1, source_target_pairs={{0,1},{1,0},{2,3},{3,2},{4,5},{5,4},{6,7},{7,6},{8,9},{9,8},{10,11... | collective-permute-start | bytes 1572872 | tf_op jit(solution)/shard_map/ppermute | solution.py:509
  4.2 1.2 %collective-permute-start.3 = (f32[8,16,1024]{2,1,0:T(8,128)}, f32[8,16,1024]{2,1,0:T(8,128)S(1)}, u32[]{:S(2)}, u32[]{:S(2)}) collective-permute-start(f32[8,16,1024]{2,1,0:T(8,128)} %psi_ref.3), channel_id=1, source_target_pairs={{0,3},{1,2},{2,1},{3,0},{4,7},{5,6},{6,5},{7,4},{8,11},{9,10},{10,... | collective-permute-start | bytes 1572872 | tf_op jit(solution)/shard_map/ppermute | solution.py:510
  5.4 0.0 copy-start.5
  5.4 0.7 %copy-done.5 = s32[32]{0:T(128)S(1)} copy-done((s32[32]{0:T(128)S(1)}, s32[32]{0:T(128)}, u32[]{:S(2)}) %copy-start.5) | copy-done | bytes 152
  6.1 0.6 %shard_map.69.live_ref = f32[32,1024]{1,0:T(8,128)S(1)} custom-call(s32[8,1024]{1,0:T(8,128)S(1)} %shard_map.68.columns_ref, s32[32]{0:T(128)S(1)} %copy-done.5), custom_call_target="tpu_custom_call" | custom-call | flops 1 | bytes 1 | tf_op jit(solution)/shard_map/pallas_call | solution.py:512
  6.7 0.0 copy-done.2
  6.7 0.0 copy-done.3
  6.7 0.0 copy-start
  6.7 1.0 %copy-done = f32[8,16,1024]{2,1,0:T(8,128)S(1)} copy-done((f32[8,16,1024]{2,1,0:T(8,128)S(1)}, f32[8,16,1024]{2,1,0:T(8,128)}, u32[]{:S(2)}) %copy-start) | copy-done | bytes 524312
  7.7 0.5 %shard_map.70 = (f32[8,16,1024]{2,1,0:T(8,128)S(1)}, bf16[256,1024]{1,0:T(8,128)(2,1)S(1)}, f32[128,1024]{1,0:T(8,128)S(1)}) custom-call(f32[8,16,1024]{2,1,0:T(8,128)S(1)} %copy-done, f32[16,1024]{1,0:T(8,128)S(1)} %copy-done.3, f32[32,1024]{1,0:T(8,128)S(1)} %shard_map.69.live_ref, bf16[256,256]{1,0:T(8,128)(2,1)S(1)} %copy-done.2), custom_call_target="tpu_custom_call" | custom-call | flops 1 | bytes 1 | tf_op jit(solution)/shard_map/pallas_call | solution.py:515
  8.3 7.6 %collective-permute-done.psi_ref = f32[8,16,1024]{2,1,0:T(8,128)S(1)} collective-permute-done((f32[8,16,1024]{2,1,0:T(8,128)}, f32[8,16,1024]{2,1,0:T(8,128)S(1)}, u32[]{:S(2)}, u32[]{:S(2)}) %collective-permute-start) | collective-permute-done | bytes 524320 | tf_op jit(solution)/shard_map/ppermute | solution.py:505
  15.9 0.0 collective-permute-start.2
  15.9 0.0 collective-permute-done.1.field_ref
  15.9 3.3 %collective-permute-start.6 = (f32[8,16,1024]{2,1,0:T(8,128)S(1)}, f32[8,16,1024]{2,1,0:T(8,128)S(1)}, u32[]{:S(2)}, u32[]{:S(2)}) collective-permute-start(f32[8,16,1024]{2,1,0:T(8,128)S(1)} %collective-permute-done.1.field_ref), channel_id=1, source_target_pairs={{0,4},{4,0},{8,12},{12,8},{1,5},{5,1},{9,13},{13,9},{2,6},{6,2},{1... | collective-permute-start | bytes 1572872 | tf_op jit(solution)/shard_map/ppermute | solution.py:520
  19.2 0.0 collective-permute-start.7
  19.2 0.1 shard_map.76
  19.3 0.0 collective-permute-done.4.near_ref
  19.3 0.6 %collective-permute-start.5 = (f32[8,16,896]{2,1,0:T(8,128)S(1)}, f32[8,16,896]{2,1,0:T(8,128)S(1)}, u32[]{:S(2)}, u32[]{:S(2)}) collective-permute-start(f32[8,16,896]{2,1,0:T(8,128)S(1)} %shard_map.76), channel_id=1, source_target_pairs={{4,7},{5,6},{6,5},{7,4},{8,11},{9,10},{10,9},{11,8},{0,1},{1,0},{2... | collective-permute-start | bytes 1376264 | tf_op jit(solution)/shard_map/ppermute | solution.py:523
  19.8 0.5 %shard_map.71 = (f32[8,16,1024]{2,1,0:T(8,128)S(1)}, bf16[256,1024]{1,0:T(8,128)(2,1)S(1)}, f32[128,1024]{1,0:T(8,128)S(1)}) custom-call(f32[8,16,1024]{2,1,0:T(8,128)S(1)} %collective-permute-done.psi_ref, f32[16,1024]{1,0:T(8,128)S(1)} %copy-done.3, f32[32,1024]{1,0:T(8,128)S(1)} %shard_map.69.live_ref, bf16[256,256]{1,0:T(8,128)(2,1)S(1)} %copy-done.2), custom_call_target="tpu_custom_call" | custom-call | flops 1 | bytes 1 | tf_op jit(solution)/shard_map/pallas_call | solution.py:529
  20.4 0.0 copy-start.1
  20.4 0.0 copy-start.4
  20.4 0.1 shard_map.72.refs_2_.third_ref.third_parts
  20.5 0.0 collective-permute-done.3.far_ref
  20.5 0.9 %copy-done.1 = f32[8,16,1024]{2,1,0:T(8,128)S(1)} copy-done((f32[8,16,1024]{2,1,0:T(8,128)S(1)}, f32[8,16,1024]{2,1,0:T(8,128)}, u32[]{:S(2)}) %copy-start.1) | copy-done | bytes 524312
  21.4 0.0 copy-done.4
  21.4 0.4 shard_map.73
  21.9 0.6 %shard_map.74.early_ref = f32[24,128]{1,0:T(8,128)S(1)} custom-call(bf16[256,1024]{1,0:T(8,128)(2,1)S(1)} %get-tuple-element.41.refs_0_.own_ref.own_parts, bf16[256,1024]{1,0:T(8,128)(2,1)S(1)} %get-tuple-element.42.refs_1_.pair_ref.pair_parts, bf16[256,1024]{1,0:T(8,128)(2,1)S(1)} %shard_map.72.refs_2_.third_ref.third_parts, ...), custom_call_target="tpu_custom_call" | custom-call | flops 1 | bytes 1 | tf_op jit(solution)/shard_map/pallas_call | solution.py:532
  22.5 0.0 collective-permute-done.2.field_ref.fourth_ref
  22.6 7.9 %collective-permute-start.13 = (f32[7,16,1024]{2,1,0:T(8,128)S(1)}, f32[7,16,1024]{2,1,0:T(8,128)S(1)}, u32[]{:S(2)}, u32[]{:S(2)}) collective-permute-start(f32[7,16,1024]{2,1,0:T(8,128)S(1)} %shard_map.83), channel_id=1, source_target_pairs={{0,4},{4,0},{8,12},{12,8},{1,5},{5,1},{9,13},{13,9},{2,6},{6,2},{1... | collective-permute-start | bytes 1376264 | tf_op jit(solution)/shard_map/ppermute | solution.py:540
  30.5 0.1 shard_map.75.refs_0_.fourth_ref.fourth_parts
  30.6 0.3 shard_map.78.last_ref
  30.9 0.0 collective-permute-done.5.far_ref
  31.0 0.0 collective-permute-done.6.third_ref
  31.0 0.0 collective-permute-done.7.near_ref
  31.0 0.5 %shard_map.77 = (f32[8,16,1024]{2,1,0:T(8,128)S(1)}, bf16[256,1024]{1,0:T(8,128)(2,1)S(1)}) custom-call(f32[8,16,896]{2,1,0:T(8,128)S(1)} %collective-permute-done.5.far_ref, f32[8,16,1024]{2,1,0:T(8,128)S(1)} %collective-permute-done.psi_ref, f32[8,16,1024]{2,1,0:T(8,128)S(1)} %collective-permute-done.7.near_ref, ...), custom_call_target="tpu_custom_call" | custom-call | flops 1 | bytes 1 | tf_op jit(solution)/shard_map/pallas_call | solution.py:542
  31.5 0.9 %shard_map.79.refs_0_ = f32[32,16]{1,0:T(8,128)S(1)} custom-call(bf16[256,1024]{1,0:T(8,128)(2,1)S(1)} %get-tuple-element.41.refs_0_.own_ref.own_parts, bf16[256,1024]{1,0:T(8,128)(2,1)S(1)} %get-tuple-element.42.refs_1_.pair_ref.pair_parts, bf16[256,1024]{1,0:T(8,128)(2,1)S(1)} %shard_map.72.refs_2_.third_ref.third_parts, ...), custom_call_target="tpu_custom_call" | custom-call | flops 1 | bytes 1 | tf_op jit(solution)/shard_map/pallas_call | solution.py:556
  32.4 0.1 collective-permute-start.8
  32.5 1.2 %collective-permute-done.8.refs_1_ = f32[32,16]{1,0:T(8,128)S(1)} collective-permute-done((f32[32,16]{1,0:T(8,128)S(1)}, f32[32,16]{1,0:T(8,128)S(1)}, u32[]{:S(2)}, u32[]{:S(2)}) %collective-permute-start.8) | collective-permute-done | bytes 2080 | tf_op jit(solution)/shard_map/ppermute | solution.py:562
  33.7 0.2 collective-permute-start.9
  33.8 1.0 %collective-permute-done.9.other_ref = f32[32,16]{1,0:T(8,128)S(1)} collective-permute-done((f32[32,16]{1,0:T(8,128)S(1)}, f32[32,16]{1,0:T(8,128)S(1)}, u32[]{:S(2)}, u32[]{:S(2)}) %collective-permute-start.9) | collective-permute-done | bytes 2080 | tf_op jit(solution)/shard_map/ppermute | solution.py:567
  34.8 0.1 shard_map.81
  34.9 3.2 %collective-permute-start.14 = (f32[72,256]{1,0:T(8,128)S(1)}, f32[72,256]{1,0:T(8,128)S(1)}, u32[]{:S(2)}, u32[]{:S(2)}) collective-permute-start(f32[72,256]{1,0:T(8,128)S(1)} %get-tuple-element.59), channel_id=1, source_target_pairs={{0,4},{4,0},{8,12},{12,8},{1,5},{5,1},{9,13},{13,9},{2,6},{6,2},{1... | collective-permute-start | bytes 221192 | tf_op jit(solution)/shard_map/ppermute | solution.py:569
  38.1 2.7 %collective-permute-start.10 = (f32[32,256]{1,0:T(8,128)S(1)}, f32[32,256]{1,0:T(8,128)S(1)}, u32[]{:S(2)}, u32[]{:S(2)}) collective-permute-start(f32[32,256]{1,0:T(8,128)S(1)} %get-tuple-element.55), channel_id=1, source_target_pairs={{0,8},{4,12},{8,0},{12,4},{1,9},{5,13},{9,1},{13,5},{2,10},{6,14},... | collective-permute-start | bytes 98312 | tf_op jit(solution)/shard_map/ppermute | solution.py:584
  40.8 0.5 %collective-permute-start.12 = (f32[24,256]{1,0:T(8,128)S(1)}, f32[24,256]{1,0:T(8,128)S(1)}, u32[]{:S(2)}, u32[]{:S(2)}) collective-permute-start(f32[24,256]{1,0:T(8,128)S(1)} %get-tuple-element.57), channel_id=1, source_target_pairs={{0,4},{4,0},{8,12},{12,8},{1,5},{5,1},{9,13},{13,9},{2,6},{6,2},{1... | collective-permute-start | bytes 73736 | tf_op jit(solution)/shard_map/ppermute | solution.py:583
  41.3 0.0 collective-permute-start.11
  41.3 0.3 collective-permute-done.14.sent_ref.corr_ref
  41.6 0.0 collective-permute-done.13.fourth_ref
  41.6 0.2 shard_map.84
  41.8 1.9 %shard_map.85 = f32[8,16,1024]{2,1,0:T(8,128)} custom-call(f32[128,1024]{1,0:T(8,128)S(1)} %get-tuple-element.36.own_phi, bf16[256,1024]{1,0:T(8,128)(2,1)S(1)} %get-tuple-element.41.refs_0_.own_ref.own_parts, bf16[256,1024]{1,0:T(8,128)(2,1)S(1)} %get-tuple-element.42.refs_1_.pair_ref.pair_parts, bf16[256,1024]{1,0:T(8,128)(2,1)S(1)} %get-tuple-element.60.third_parts, ...), custom_call_target="tpu_custom_call" | custom-call | flops 1 | bytes 1 | tf_op jit(solution)/shard_map/pallas_call | solution.py:589
  43.7 0.0 collective-permute-done.11.sent3_ref
  43.7 0.9 %collective-permute-done.12.given_ref = f32[24,256]{1,0:T(8,128)S(1)} collective-permute-done((f32[24,256]{1,0:T(8,128)S(1)}, f32[24,256]{1,0:T(8,128)S(1)}, u32[]{:S(2)}, u32[]{:S(2)}) %collective-permute-start.12) | collective-permute-done | bytes 24608 | tf_op jit(solution)/shard_map/ppermute | solution.py:583
  44.6 0.0 collective-permute-done.10.sent2_ref
  44.6 0.6 %shard_map.86 = f32[16,256]{1,0:T(8,128)} custom-call(f32[32,256]{1,0:T(8,128)S(1)} %collective-permute-done.10.sent2_ref, f32[16,256]{1,0:T(8,128)S(1)} %collective-permute-done.11.sent3_ref, f32[24,256]{1,0:T(8,128)S(1)} %collective-permute-done.12.given_ref, f32[16,256]{1,0:T(8,128)S(1)} %get-tuple-element.67.kept_ref), custom_call_target="tpu_custom_call" | custom-call | flops 1 | bytes 1 | tf_op jit(solution)/shard_map/pallas_call | solution.py:600
  (4 shorter events, 0.0 us)
Async XLA Ops:
  0.6 6.0 %copy-start.2 = (bf16[256,256]{1,0:T(8,128)(2,1)S(1)}, bf16[256,256]{1,0:T(8,128)(2,1)}, u32[]{:S(2)}) copy-start(bf16[256,256]{1,0:T(8,128)(2,1)} %constant.4.clone.band_ref) | copy-start | bytes 393220
  0.6 15.2 %collective-permute-start = (f32[8,16,1024]{2,1,0:T(8,128)}, f32[8,16,1024]{2,1,0:T(8,128)S(1)}, u32[]{:S(2)}, u32[]{:S(2)}) collective-permute-start(f32[8,16,1024]{2,1,0:T(8,128)} %psi_ref.3), channel_id=1, source_target_pairs={{0,4},{4,0},{8,12},{12,8},{1,5},{5,1},{9,13},{13,9},{2,6},{6,2},{1... | collective-permute-start | bytes 1572872 | tf_op jit(solution)/shard_map/ppermute | solution.py:505
  3.7 12.1 %collective-permute-start.1 = (f32[8,16,1024]{2,1,0:T(8,128)}, f32[8,16,1024]{2,1,0:T(8,128)S(1)}, u32[]{:S(2)}, u32[]{:S(2)}) collective-permute-start(f32[8,16,1024]{2,1,0:T(8,128)} %psi_ref.3), channel_id=1, source_target_pairs={{4,8},{5,9},{6,10},{7,11},{8,4},{9,5},{10,6},{11,7},{0,1},{1,0},{2... | collective-permute-start | bytes 1572872 | tf_op jit(solution)/shard_map/ppermute | solution.py:506
  3.7 2.9 %copy-start.3 = (f32[16,1024]{1,0:T(8,128)S(1)}, f32[16,1024]{1,0:T(8,128)}, u32[]{:S(2)}) copy-start(f32[16,1024]{1,0:T(8,128)} %potential_ref.3) | copy-start | bytes 196612
  3.8 15.5 %collective-permute-start.4 = (f32[8,16,1024]{2,1,0:T(8,128)}, f32[8,16,1024]{2,1,0:T(8,128)S(1)}, u32[]{:S(2)}, u32[]{:S(2)}) collective-permute-start(f32[8,16,1024]{2,1,0:T(8,128)} %psi_ref.3), channel_id=1, source_target_pairs={{0,1},{1,0},{2,3},{3,2},{4,5},{5,4},{6,7},{7,6},{8,9},{9,8},{10,11... | collective-permute-start | bytes 1572872 | tf_op jit(solution)/shard_map/ppermute | solution.py:509
  4.2 16.3 %collective-permute-start.3 = (f32[8,16,1024]{2,1,0:T(8,128)}, f32[8,16,1024]{2,1,0:T(8,128)S(1)}, u32[]{:S(2)}, u32[]{:S(2)}) collective-permute-start(f32[8,16,1024]{2,1,0:T(8,128)} %psi_ref.3), channel_id=1, source_target_pairs={{0,3},{1,2},{2,1},{3,0},{4,7},{5,6},{6,5},{7,4},{8,11},{9,10},{10,... | collective-permute-start | bytes 1572872 | tf_op jit(solution)/shard_map/ppermute | solution.py:510
  5.4 0.7 %copy-start.5 = (s32[32]{0:T(128)S(1)}, s32[32]{0:T(128)}, u32[]{:S(2)}) copy-start(s32[32]{0:T(128)} %extent_ref.1) | copy-start | bytes 388
  6.7 1.0 %copy-start = (f32[8,16,1024]{2,1,0:T(8,128)S(1)}, f32[8,16,1024]{2,1,0:T(8,128)}, u32[]{:S(2)}) copy-start(f32[8,16,1024]{2,1,0:T(8,128)} %psi_ref.3) | copy-start | bytes 1572868
  15.9 6.6 %collective-permute-start.2 = (f32[8,16,1024]{2,1,0:T(8,128)S(1)}, f32[8,16,1024]{2,1,0:T(8,128)S(1)}, u32[]{:S(2)}, u32[]{:S(2)}) collective-permute-start(f32[8,16,1024]{2,1,0:T(8,128)S(1)} %collective-permute-done.psi_ref), channel_id=1, source_target_pairs={{4,8},{5,9},{6,10},{7,11},{8,4},{9,5},{10,6},{11,7},{0,1},{1,0},{2... | collective-permute-start | bytes 1572872 | tf_op jit(solution)/shard_map/ppermute | solution.py:519
  15.9 15.1 %collective-permute-start.6 = (f32[8,16,1024]{2,1,0:T(8,128)S(1)}, f32[8,16,1024]{2,1,0:T(8,128)S(1)}, u32[]{:S(2)}, u32[]{:S(2)}) collective-permute-start(f32[8,16,1024]{2,1,0:T(8,128)S(1)} %collective-permute-done.1.field_ref), channel_id=1, source_target_pairs={{0,4},{4,0},{8,12},{12,8},{1,5},{5,1},{9,13},{13,9},{2,6},{6,2},{1... | collective-permute-start | bytes 1572872 | tf_op jit(solution)/shard_map/ppermute | solution.py:520
  19.2 11.8 %collective-permute-start.7 = (f32[8,16,1024]{2,1,0:T(8,128)S(1)}, f32[8,16,1024]{2,1,0:T(8,128)S(1)}, u32[]{:S(2)}, u32[]{:S(2)}) collective-permute-start(f32[8,16,1024]{2,1,0:T(8,128)S(1)} %collective-permute-done.psi_ref), channel_id=1, source_target_pairs={{0,1},{1,0},{2,3},{3,2},{4,5},{5,4},{6,7},{7,6},{8,9},{9,8},{10,11... | collective-permute-start | bytes 1572872 | tf_op jit(solution)/shard_map/ppermute | solution.py:524
  19.3 11.7 %collective-permute-start.5 = (f32[8,16,896]{2,1,0:T(8,128)S(1)}, f32[8,16,896]{2,1,0:T(8,128)S(1)}, u32[]{:S(2)}, u32[]{:S(2)}) collective-permute-start(f32[8,16,896]{2,1,0:T(8,128)S(1)} %shard_map.76), channel_id=1, source_target_pairs={{4,7},{5,6},{6,5},{7,4},{8,11},{9,10},{10,9},{11,8},{0,1},{1,0},{2... | collective-permute-start | bytes 1376264 | tf_op jit(solution)/shard_map/ppermute | solution.py:523
  20.4 1.0 %copy-start.1 = (f32[8,16,1024]{2,1,0:T(8,128)S(1)}, f32[8,16,1024]{2,1,0:T(8,128)}, u32[]{:S(2)}) copy-start(f32[8,16,1024]{2,1,0:T(8,128)} %psi_ref.3) | copy-start | bytes 1572868
  20.4 1.0 %copy-start.4 = (bf16[2,16,144]{2,1,0:T(8,128)(2,1)S(1)}, bf16[2,16,144]{2,1,0:T(8,128)(2,1)}, u32[]{:S(2)}) copy-start(bf16[2,16,144]{2,1,0:T(8,128)(2,1)} %constant.5.clone.band_ref) | copy-start | bytes 27652
  22.6 19.1 %collective-permute-start.13 = (f32[7,16,1024]{2,1,0:T(8,128)S(1)}, f32[7,16,1024]{2,1,0:T(8,128)S(1)}, u32[]{:S(2)}, u32[]{:S(2)}) collective-permute-start(f32[7,16,1024]{2,1,0:T(8,128)S(1)} %shard_map.83), channel_id=1, source_target_pairs={{0,4},{4,0},{8,12},{12,8},{1,5},{5,1},{9,13},{13,9},{2,6},{6,2},{1... | collective-permute-start | bytes 1376264 | tf_op jit(solution)/shard_map/ppermute | solution.py:540
  32.4 1.2 %collective-permute-start.8 = (f32[32,16]{1,0:T(8,128)S(1)}, f32[32,16]{1,0:T(8,128)S(1)}, u32[]{:S(2)}, u32[]{:S(2)}) collective-permute-start(f32[32,16]{1,0:T(8,128)S(1)} %shard_map.79.refs_0_), channel_id=1, source_target_pairs={{0,1},{1,0},{2,3},{3,2},{4,5},{5,4},{6,7},{7,6},{8,9},{9,8},{10,11... | collective-permute-start | bytes 6152 | tf_op jit(solution)/shard_map/ppermute | solution.py:562
  33.7 1.2 %collective-permute-start.9 = (f32[32,16]{1,0:T(8,128)S(1)}, f32[32,16]{1,0:T(8,128)S(1)}, u32[]{:S(2)}, u32[]{:S(2)}) collective-permute-start(f32[32,16]{1,0:T(8,128)S(1)} %shard_map.80.part_ref), channel_id=1, source_target_pairs={{4,7},{5,6},{6,5},{7,4},{8,11},{9,10},{10,9},{11,8},{0,1},{1,0},{2... | collective-permute-start | bytes 6152 | tf_op jit(solution)/shard_map/ppermute | solution.py:567
  34.9 6.7 %collective-permute-start.14 = (f32[72,256]{1,0:T(8,128)S(1)}, f32[72,256]{1,0:T(8,128)S(1)}, u32[]{:S(2)}, u32[]{:S(2)}) collective-permute-start(f32[72,256]{1,0:T(8,128)S(1)} %get-tuple-element.59), channel_id=1, source_target_pairs={{0,4},{4,0},{8,12},{12,8},{1,5},{5,1},{9,13},{13,9},{2,6},{6,2},{1... | collective-permute-start | bytes 221192 | tf_op jit(solution)/shard_map/ppermute | solution.py:569
  38.1 6.5 %collective-permute-start.10 = (f32[32,256]{1,0:T(8,128)S(1)}, f32[32,256]{1,0:T(8,128)S(1)}, u32[]{:S(2)}, u32[]{:S(2)}) collective-permute-start(f32[32,256]{1,0:T(8,128)S(1)} %get-tuple-element.55), channel_id=1, source_target_pairs={{0,8},{4,12},{8,0},{12,4},{1,9},{5,13},{9,1},{13,5},{2,10},{6,14},... | collective-permute-start | bytes 98312 | tf_op jit(solution)/shard_map/ppermute | solution.py:584
  40.8 3.8 %collective-permute-start.12 = (f32[24,256]{1,0:T(8,128)S(1)}, f32[24,256]{1,0:T(8,128)S(1)}, u32[]{:S(2)}, u32[]{:S(2)}) collective-permute-start(f32[24,256]{1,0:T(8,128)S(1)} %get-tuple-element.57), channel_id=1, source_target_pairs={{0,4},{4,0},{8,12},{12,8},{1,5},{5,1},{9,13},{13,9},{2,6},{6,2},{1... | collective-permute-start | bytes 73736 | tf_op jit(solution)/shard_map/ppermute | solution.py:583
  41.3 2.4 %collective-permute-start.11 = (f32[16,256]{1,0:T(8,128)S(1)}, f32[16,256]{1,0:T(8,128)S(1)}, u32[]{:S(2)}, u32[]{:S(2)}) collective-permute-start(f32[16,256]{1,0:T(8,128)S(1)} %get-tuple-element.56), channel_id=1, source_target_pairs={{4,8},{5,9},{6,10},{7,11},{8,4},{9,5},{10,6},{11,7},{0,1},{1,0},{2... | collective-permute-start | bytes 49160 | tf_op jit(solution)/shard_map/ppermute | solution.py:585

commit v9 on v8

--- a/solution.py
+++ b/solution.py
@@ -108,24 +108,32 @@
     return high, (value - high.astype(np.float32)).astype(jnp.bfloat16)
 
 
+def three_parts(value):
+    high, rest = two_parts(value)
+    middle, low = two_parts(value - high.astype(np.float32))
+    del rest
+    return high, middle, low
+
+
 def column_band():
     rows = np.arange(2 * lanes)[:, None]
     cols = np.arange(lanes)[None, :]
-    high, low = two_parts(weight(rows - cols - reach))
-    return np.concatenate([high, low], axis=1)
+    return np.concatenate(three_parts(weight(rows - cols - reach)), axis=1)
+
+
+def six_products(band):
+    high, middle, low = three_parts(band)
+    return np.concatenate([high, high, high, middle, middle, low], axis=1)
 
 
 def plane_bands(planes):
     rows = np.arange(planes)[:, None]
     cols = np.arange(planes)[None, :]
-    both = []
-    for side in (-planes, planes):
-        band = np.concatenate(
-            [weight(cols + side - rows), weight(cols - rows), weight(cols - side - rows)], axis=1
-        )
-        high, low = two_parts(band)
-        both.append(np.concatenate([high, high, low], axis=1))
-    return np.stack(both)
+    sides = [
+        np.concatenate([weight(cols + side - rows), weight(cols - side - rows)], axis=1)
+        for side in (-planes, planes)
+    ]
+    return six_products(weight(cols - rows)), np.stack([six_products(band) for band in sides])
 
 
 def columns_kernel(out_ref):
@@ -199,7 +207,18 @@
                     ]
 
 
-def local_kernel(f, psi_ref, potential_ref, live_ref, band_ref, out_ref, parts_ref, phi_ref):
+def band_product(band, slabs):
+    high, middle, low = three_parts(slabs)
+    return jnp.dot(
+        band,
+        jnp.concatenate([high, middle, low, high, middle, high], axis=0),
+        preferred_element_type=jnp.float32,
+    )
+
+
+def local_kernel(
+    f, psi_ref, potential_ref, live_ref, band_ref, own_band_ref, out_ref, parts_ref, phi_ref
+):
     orbs, planes, grid_p = psi_ref.shape
     tiles = grid_p // lanes
     for a in range(orbs):
@@ -208,25 +227,34 @@
         high, low = two_parts(phi)
         parts_ref[a * planes : (a + 1) * planes, :] = high
         parts_ref[(orbs + a) * planes : (orbs + a + 1) * planes, :] = low
-    high, low = two_parts(pltpu.roll(phi_ref[...], reach, 1))
+    fields = three_parts(pltpu.roll(phi_ref[...], reach, 1))
     for t in range(tiles):
         here, after = t * lanes, (t + 1) % tiles * lanes
-        high_t = jnp.concatenate([high[:, here : here + lanes], high[:, after : after + lanes]], 1)
-        low_t = jnp.concatenate([low[:, here : here + lanes], low[:, after : after + lanes]], 1)
-        both = jnp.dot(high_t, band_ref[...], preferred_element_type=jnp.float32)
-        rest = jnp.dot(low_t, band_ref[:, :lanes], preferred_element_type=jnp.float32)
-        second = both[:, :lanes] + both[:, lanes:] + rest
+        second = None
+        for n in (1, 2, 3):
+            field = fields[3 - n]
+            wide = jnp.concatenate(
+                [field[:, here : here + lanes], field[:, after : after + lanes]], axis=1
+            )
+            product = jnp.dot(
+                wide, band_ref[:, : n * lanes], preferred_element_type=jnp.float32
+            )
+            for k in reversed(range(n)):
+                term = product[:, k * lanes : (k + 1) * lanes]
+                second = term if second is None else second + term
         field = phi_ref[:, here : here + lanes].reshape(orbs, planes, lanes)
         out_ref[:, :, here : here + lanes] = (
             potential_ref[:, here : here + lanes][None] * field
             - 0.5 * second.reshape(orbs, planes, lanes)
         )
+    for a in range(orbs):
+        out_ref[a] = out_ref[a] - 0.5 * band_product(own_band_ref[...], psi_ref[a])
 
 
 def plane_kernel(
-    f, far_ref, psi_ref, near_ref, local_ref, live_ref, band_ref, out_ref, parts_ref, *rest_ref
+    f, far_ref, near_ref, local_ref, live_ref, band_ref, out_ref, parts_ref, *rest_ref
 ):
-    orbs, planes, _ = psi_ref.shape
+    orbs, planes, _ = near_ref.shape
     band = band_ref[lax.axis_index("cmp") % 2]
     for ref in rest_ref:
         ref[...] = jnp.zeros_like(ref)
@@ -242,11 +270,7 @@
 
     for a in range(orbs):
         far = jnp.concatenate([far_ref[a]] + [ref[a] for ref in rest_ref], axis=1)
-        slab = jnp.concatenate([far, psi_ref[a], near_ref[a]], axis=0)
-        high, low = two_parts(slab)
-        second = jnp.dot(
-            band, jnp.concatenate([high, low, high], axis=0), preferred_element_type=jnp.float32
-        )
+        second = band_product(band, jnp.concatenate([far, near_ref[a]], axis=0))
         image = (local_ref[a] - 0.5 * second) * live_ref[f * orbs + a : f * orbs + a + 1, :]
         out_ref[a] = image
         high, low = two_parts(image)
@@ -500,7 +524,7 @@
     parts = jax.ShapeDtypeStruct((2 * rows, grid_p), jnp.bfloat16)
     flat = jax.ShapeDtypeStruct((rows, grid_p), jnp.float32)
     columns = jnp.asarray(column_band())
-    bands = jnp.asarray(plane_bands(planes))
+    own_band, bands = (jnp.asarray(band) for band in plane_bands(planes))
 
     pair = lax.ppermute(psi, "orb", swap)
     third = lax.ppermute(psi, line, across)
@@ -513,8 +537,8 @@
         grid, extent
     )
     local, own_parts, own_phi = call(
-        functools.partial(local_kernel, 0), (block, parts, flat), "vvvv"
-    )(psi, potential, live, columns)
+        functools.partial(local_kernel, 0), (block, parts, flat), "vvvvv"
+    )(psi, potential, live, columns, own_band)
     pair, local, own_parts = lax.optimization_barrier((pair, local, own_parts))
     fourth = lax.ppermute(pair, line, across)
     third_out = lax.ppermute(third, "orb", swap)
@@ -523,12 +547,12 @@
     pair_far = lax.ppermute(call(shorten_kernel, short, "v")(pair), line, inner_far)
     pair_near = lax.ppermute(pair, "cmp", to_near)
 
-    image, image_parts = call(functools.partial(plane_kernel, 0), (block, parts), "vvvvvv")(
-        far, psi, near, local, live, bands
+    image, image_parts = call(functools.partial(plane_kernel, 0), (block, parts), "vvvvv")(
+        far, near, local, live, bands
     )
     ward_local, pair_parts, pair_phi = call(
-        functools.partial(local_kernel, 1), (block, parts, flat), "vvvv"
-    )(pair, potential, live, columns)
+        functools.partial(local_kernel, 1), (block, parts, flat), "vvvvv"
+    )(pair, potential, live, columns, own_band)
     early = call(
         functools.partial(overlap_kernel, planes, 3),
         jax.ShapeDtypeStruct((3 * orbs, rows), jnp.float32),
@@ -542,10 +566,10 @@
     ward, ward_parts = call(
         functools.partial(plane_kernel, 1),
         (block, parts),
-        "vvvvvv",
+        "vvvvv",
         [pltpu.VMEM((orbs, planes, lanes), jnp.float32)],
     )(
-        pair_far, pair, pair_near, ward_local, live, bands
+        pair_far, pair_near, ward_local, live, bands
     )
     fourth_parts = call(functools.partial(split_kernel, 3), parts, "vv")(fourth, live)
     last = call(

time: 45.4 us -> 45.6 us (level)
  waiting for transfers between devices: 11 us -> 9.68 us
  Pallas kernels: 7.54 us -> 8.72 us
  local copies, waits for them, and re-layouts: 2.62 us -> 3.15 us
    ppermute x1, waiting for transfers between devices: 7.59 us -> 6.26 us  [line_device(): pair = lax.ppermute(psi, 'orb', swap)]
    pallas_call x4, Pallas kernels: 2.02 us -> 3.21 us  [the longest x1 1.04 us: line_device(): call(functools.partial(local_kernel, 1), (block, parts, flat), 'vvvvv')]
    unnamed x12, local copies, waits for them, and re-layouts: 2.62 us -> 3.15 us
  transfers between devices with their start and end apart: 15 -> 15, of which waited for: 5 -> 5; matrix products, arithmetic and copies ran while one was open for 0% -> 0% of each run, Pallas kernels for 15% -> 18%
where the time goes in v9:
time: 45.6 us; the launch traced here: 45.4 us
  starting transfers between devices  23 us (50%)
  waiting for transfers between devices  9.68 us (21%)
  Pallas kernels  8.72 us (19%)
  local copies, waits for them, and re-layouts  3.15 us (7%)
  between operations  0.82 us (2%)
    ppermute x1, starting transfers between devices, line_device(): lax.ppermute(call(all_but_last_kernel, most, 'v')(fourth), 'orb', swap)  7.68 us
    ppermute x1, waiting for transfers between devices, line_device(): pair = lax.ppermute(psi, 'orb', swap)  6.26 us
    ppermute x1, starting transfers between devices, line_device(): third_out = lax.ppermute(third, 'orb', swap)  3.31 us
    ppermute x1, starting transfers between devices, line_device(): given_correlation = lax.ppermute(sent, 'orb', swap)  3.21 us
    unnamed x12, local copies, waits for them, and re-layouts  3.15 us
    ppermute x1, starting transfers between devices, line_device(): pair = lax.ppermute(psi, 'orb', swap)  3.09 us
    ppermute x1, starting transfers between devices, line_device(): sent2 = lax.ppermute(second, 'orb', [(i, i ^ 2) for i in range(4)])  2.68 us
    pallas_call x1, Pallas kernels, line_device(): call(finish_kernel, block, 'vvvvvvvv', [pltpu.VMEM(block.shape, jnp.float...  1.9 us
  transfers between devices with their start and end apart: 15, of which 5 were waited for; matrix products, arithmetic and copies ran while one was open for 0% of the time, Pallas kernels for 18%

profile of v9, /device:TPU:0, one launch (start us, length us, event | category | flops | bytes accessed | tf_op | source)
XLA Modules:
  0.0 45.4 jit_solution(6019823377104460933)
XLA Ops:
  0.6 0.0 copy-start.4
  0.6 0.0 copy-start
  0.7 3.1 %collective-permute-start = (f32[8,16,1024]{2,1,0:T(8,128)}, f32[8,16,1024]{2,1,0:T(8,128)S(1)}, u32[]{:S(2)}, u32[]{:S(2)}) collective-permute-start(f32[8,16,1024]{2,1,0:T(8,128)} %psi_ref.1), channel_id=1, source_target_pairs={{0,4},{4,0},{8,12},{12,8},{1,5},{5,1},{9,13},{13,9},{2,6},{6,2},{1... | collective-permute-start | bytes 1572872 | tf_op jit(solution)/shard_map/ppermute | solution.py:529
  3.7 0.0 collective-permute-start.1
  3.8 0.5 %collective-permute-start.4 = (f32[8,16,1024]{2,1,0:T(8,128)}, f32[8,16,1024]{2,1,0:T(8,128)S(1)}, u32[]{:S(2)}, u32[]{:S(2)}) collective-permute-start(f32[8,16,1024]{2,1,0:T(8,128)} %psi_ref.1), channel_id=1, source_target_pairs={{0,1},{1,0},{2,3},{3,2},{4,5},{5,4},{6,7},{7,6},{8,9},{9,8},{10,11... | collective-permute-start | bytes 1572872 | tf_op jit(solution)/shard_map/ppermute | solution.py:533
  4.3 1.2 %collective-permute-start.3 = (f32[8,16,1024]{2,1,0:T(8,128)}, f32[8,16,1024]{2,1,0:T(8,128)S(1)}, u32[]{:S(2)}, u32[]{:S(2)}) collective-permute-start(f32[8,16,1024]{2,1,0:T(8,128)} %psi_ref.1), channel_id=1, source_target_pairs={{0,3},{1,2},{2,1},{3,0},{4,7},{5,6},{6,5},{7,4},{8,11},{9,10},{10,... | collective-permute-start | bytes 1572872 | tf_op jit(solution)/shard_map/ppermute | solution.py:534
  5.4 0.0 copy-start.5
  5.4 0.7 %copy-done.5 = s32[32]{0:T(128)S(1)} copy-done((s32[32]{0:T(128)S(1)}, s32[32]{0:T(128)}, u32[]{:S(2)}) %copy-start.5) | copy-done | bytes 152
  6.1 0.6 %shard_map.78.live_ref = f32[32,1024]{1,0:T(8,128)S(1)} custom-call(s32[8,1024]{1,0:T(8,128)S(1)} %shard_map.77.columns_ref, s32[32]{0:T(128)S(1)} %copy-done.5), custom_call_target="tpu_custom_call" | custom-call | flops 1 | bytes 1 | tf_op jit(solution)/shard_map/pallas_call | solution.py:536
  6.7 0.0 copy-done.4
  6.7 0.0 copy-done
  6.7 0.0 copy-start.1
  6.7 1.0 %copy-done.1 = f32[8,16,1024]{2,1,0:T(8,128)S(1)} copy-done((f32[8,16,1024]{2,1,0:T(8,128)S(1)}, f32[8,16,1024]{2,1,0:T(8,128)}, u32[]{:S(2)}) %copy-start.1) | copy-done | bytes 524312
  7.7 0.0 copy-start.2
  7.7 0.8 %copy-done.2 = f32[16,1024]{1,0:T(8,128)S(1)} copy-done((f32[16,1024]{1,0:T(8,128)S(1)}, f32[16,1024]{1,0:T(8,128)}, u32[]{:S(2)}) %copy-start.2) | copy-done | bytes 65560
  8.6 1.0 %shard_map.79 = (f32[8,16,1024]{2,1,0:T(8,128)S(1)}, bf16[256,1024]{1,0:T(8,128)(2,1)S(1)}, f32[128,1024]{1,0:T(8,128)S(1)}) custom-call(f32[8,16,1024]{2,1,0:T(8,128)S(1)} %copy-done.1, f32[16,1024]{1,0:T(8,128)S(1)} %copy-done.2, f32[32,1024]{1,0:T(8,128)S(1)} %shard_map.78.live_ref, bf16[256,384]{1,0:T(8,128)(2,1)S(1)} %copy-done, ...), custom_call_target="tpu_custom_call" | custom-call | flops 1 | bytes 1 | tf_op jit(solution)/shard_map/pallas_call | solution.py:539
  9.6 6.3 %collective-permute-done.psi_ref = f32[8,16,1024]{2,1,0:T(8,128)S(1)} collective-permute-done((f32[8,16,1024]{2,1,0:T(8,128)}, f32[8,16,1024]{2,1,0:T(8,128)S(1)}, u32[]{:S(2)}, u32[]{:S(2)}) %collective-permute-start) | collective-permute-done | bytes 524320 | tf_op jit(solution)/shard_map/ppermute | solution.py:529
  15.9 0.0 collective-permute-start.2
  15.9 0.0 collective-permute-done.1.field_ref
  15.9 3.3 %collective-permute-start.6 = (f32[8,16,1024]{2,1,0:T(8,128)S(1)}, f32[8,16,1024]{2,1,0:T(8,128)S(1)}, u32[]{:S(2)}, u32[]{:S(2)}) collective-permute-start(f32[8,16,1024]{2,1,0:T(8,128)S(1)} %collective-permute-done.1.field_ref), channel_id=1, source_target_pairs={{0,4},{4,0},{8,12},{12,8},{1,5},{5,1},{9,13},{13,9},{2,6},{6,2},{1... | collective-permute-start | bytes 1572872 | tf_op jit(solution)/shard_map/ppermute | solution.py:544
  19.2 0.0 collective-permute-start.7
  19.2 0.1 shard_map.85
  19.3 0.0 collective-permute-done.4.near_ref
  19.3 0.6 %collective-permute-start.5 = (f32[8,16,896]{2,1,0:T(8,128)S(1)}, f32[8,16,896]{2,1,0:T(8,128)S(1)}, u32[]{:S(2)}, u32[]{:S(2)}) collective-permute-start(f32[8,16,896]{2,1,0:T(8,128)S(1)} %shard_map.85), channel_id=1, source_target_pairs={{4,7},{5,6},{6,5},{7,4},{8,11},{9,10},{10,9},{11,8},{0,1},{1,0},{2... | collective-permute-start | bytes 1376264 | tf_op jit(solution)/shard_map/ppermute | solution.py:547
  19.9 1.0 %shard_map.80 = (f32[8,16,1024]{2,1,0:T(8,128)S(1)}, bf16[256,1024]{1,0:T(8,128)(2,1)S(1)}, f32[128,1024]{1,0:T(8,128)S(1)}) custom-call(f32[8,16,1024]{2,1,0:T(8,128)S(1)} %collective-permute-done.psi_ref, f32[16,1024]{1,0:T(8,128)S(1)} %copy-done.2, f32[32,1024]{1,0:T(8,128)S(1)} %shard_map.78.live_ref, bf16[256,384]{1,0:T(8,128)(2,1)S(1)} %copy-done, ...), custom_call_target="tpu_custom_call" | custom-call | flops 1 | bytes 1 | tf_op jit(solution)/shard_map/pallas_call | solution.py:553
  20.9 0.0 copy-start.3
  20.9 0.1 shard_map.81.refs_2_.third_ref.third_parts
  21.0 0.0 collective-permute-done.3.far_ref
  21.0 0.6 %copy-done.3 = bf16[2,16,192]{2,1,0:T(8,128)(2,1)S(1)} copy-done((bf16[2,16,192]{2,1,0:T(8,128)(2,1)S(1)}, bf16[2,16,192]{2,1,0:T(8,128)(2,1)}, u32[]{:S(2)}) %copy-start.3) | copy-done | bytes 12312
  21.6 0.5 %shard_map.82 = (f32[8,16,1024]{2,1,0:T(8,128)S(1)}, bf16[256,1024]{1,0:T(8,128)(2,1)S(1)}) custom-call(f32[8,16,1024]{2,1,0:T(8,128)S(1)} %collective-permute-done.3.far_ref, f32[8,16,1024]{2,1,0:T(8,128)S(1)} %collective-permute-done.4.near_ref, f32[8,16,1024]{2,1,0:T(8,128)S(1)} %get-tuple-element.45.local_ref, f32[32,1024]{1,0:T(8,128)S(1)} %shard_map.78.live_ref, ...), custom_call_target="tpu_custom_call" | custom-call | flops 1 | bytes 1 | tf_op jit(solution)/shard_map/pallas_call | solution.py:550
  22.2 0.6 %shard_map.83.early_ref = f32[24,128]{1,0:T(8,128)S(1)} custom-call(bf16[256,1024]{1,0:T(8,128)(2,1)S(1)} %get-tuple-element.41.refs_0_.own_ref.own_parts, bf16[256,1024]{1,0:T(8,128)(2,1)S(1)} %get-tuple-element.42.refs_1_.pair_ref.pair_parts, bf16[256,1024]{1,0:T(8,128)(2,1)S(1)} %shard_map.81.refs_2_.third_ref.third_parts, ...), custom_call_target="tpu_custom_call" | custom-call | flops 1 | bytes 1 | tf_op jit(solution)/shard_map/pallas_call | solution.py:556
  22.8 0.0 collective-permute-done.2.field_ref.fourth_ref
  22.8 7.7 %collective-permute-start.13 = (f32[7,16,1024]{2,1,0:T(8,128)S(1)}, f32[7,16,1024]{2,1,0:T(8,128)S(1)}, u32[]{:S(2)}, u32[]{:S(2)}) collective-permute-start(f32[7,16,1024]{2,1,0:T(8,128)S(1)} %shard_map.92), channel_id=1, source_target_pairs={{0,4},{4,0},{8,12},{12,8},{1,5},{5,1},{9,13},{13,9},{2,6},{6,2},{1... | collective-permute-start | bytes 1376264 | tf_op jit(solution)/shard_map/ppermute | solution.py:564
  30.5 0.1 shard_map.84.refs_0_.fourth_ref.fourth_parts
  30.6 0.3 shard_map.87.last_ref
  30.9 0.0 collective-permute-done.5.far_ref
  31.0 0.0 collective-permute-done.6.third_ref
  31.0 0.0 collective-permute-done.7.near_ref
  31.0 0.6 %shard_map.86 = (f32[8,16,1024]{2,1,0:T(8,128)S(1)}, bf16[256,1024]{1,0:T(8,128)(2,1)S(1)}) custom-call(f32[8,16,896]{2,1,0:T(8,128)S(1)} %collective-permute-done.5.far_ref, f32[8,16,1024]{2,1,0:T(8,128)S(1)} %collective-permute-done.7.near_ref, f32[8,16,1024]{2,1,0:T(8,128)S(1)} %get-tuple-element.50.local_ref, f32[32,1024]{1,0:T(8,128)S(1)} %shard_map.78.live_ref, ...), custom_call_target="tpu_custom_call" | custom-call | flops 1 | bytes 1 | tf_op jit(solution)/shard_map/pallas_call | solution.py:566
  31.6 0.9 %shard_map.88.refs_0_ = f32[32,16]{1,0:T(8,128)S(1)} custom-call(bf16[256,1024]{1,0:T(8,128)(2,1)S(1)} %get-tuple-element.41.refs_0_.own_ref.own_parts, bf16[256,1024]{1,0:T(8,128)(2,1)S(1)} %get-tuple-element.42.refs_1_.pair_ref.pair_parts, bf16[256,1024]{1,0:T(8,128)(2,1)S(1)} %shard_map.81.refs_2_.third_ref.third_parts, ...), custom_call_target="tpu_custom_call" | custom-call | flops 1 | bytes 1 | tf_op jit(solution)/shard_map/pallas_call | solution.py:580
  32.5 0.1 collective-permute-start.8
  32.6 1.2 %collective-permute-done.8.refs_1_ = f32[32,16]{1,0:T(8,128)S(1)} collective-permute-done((f32[32,16]{1,0:T(8,128)S(1)}, f32[32,16]{1,0:T(8,128)S(1)}, u32[]{:S(2)}, u32[]{:S(2)}) %collective-permute-start.8) | collective-permute-done | bytes 2080 | tf_op jit(solution)/shard_map/ppermute | solution.py:586
  33.8 0.2 collective-permute-start.9
  33.9 1.0 %collective-permute-done.9.other_ref = f32[32,16]{1,0:T(8,128)S(1)} collective-permute-done((f32[32,16]{1,0:T(8,128)S(1)}, f32[32,16]{1,0:T(8,128)S(1)}, u32[]{:S(2)}, u32[]{:S(2)}) %collective-permute-start.9) | collective-permute-done | bytes 2080 | tf_op jit(solution)/shard_map/ppermute | solution.py:591
  34.9 0.1 shard_map.90
  35.0 3.2 %collective-permute-start.14 = (f32[72,256]{1,0:T(8,128)S(1)}, f32[72,256]{1,0:T(8,128)S(1)}, u32[]{:S(2)}, u32[]{:S(2)}) collective-permute-start(f32[72,256]{1,0:T(8,128)S(1)} %get-tuple-element.59), channel_id=1, source_target_pairs={{0,4},{4,0},{8,12},{12,8},{1,5},{5,1},{9,13},{13,9},{2,6},{6,2},{1... | collective-permute-start | bytes 221192 | tf_op jit(solution)/shard_map/ppermute | solution.py:593
  38.2 2.7 %collective-permute-start.10 = (f32[32,256]{1,0:T(8,128)S(1)}, f32[32,256]{1,0:T(8,128)S(1)}, u32[]{:S(2)}, u32[]{:S(2)}) collective-permute-start(f32[32,256]{1,0:T(8,128)S(1)} %get-tuple-element.55), channel_id=1, source_target_pairs={{0,8},{4,12},{8,0},{12,4},{1,9},{5,13},{9,1},{13,5},{2,10},{6,14},... | collective-permute-start | bytes 98312 | tf_op jit(solution)/shard_map/ppermute | solution.py:608
  40.9 0.5 %collective-permute-start.12 = (f32[24,256]{1,0:T(8,128)S(1)}, f32[24,256]{1,0:T(8,128)S(1)}, u32[]{:S(2)}, u32[]{:S(2)}) collective-permute-start(f32[24,256]{1,0:T(8,128)S(1)} %get-tuple-element.57), channel_id=1, source_target_pairs={{0,4},{4,0},{8,12},{12,8},{1,5},{5,1},{9,13},{13,9},{2,6},{6,2},{1... | collective-permute-start | bytes 73736 | tf_op jit(solution)/shard_map/ppermute | solution.py:607
  41.4 0.0 collective-permute-start.11
  41.4 0.2 collective-permute-done.14.sent_ref.corr_ref
  41.6 0.0 collective-permute-done.13.fourth_ref
  41.6 0.2 shard_map.93
  41.8 1.9 %shard_map.94 = f32[8,16,1024]{2,1,0:T(8,128)} custom-call(f32[128,1024]{1,0:T(8,128)S(1)} %get-tuple-element.36.own_phi, bf16[256,1024]{1,0:T(8,128)(2,1)S(1)} %get-tuple-element.41.refs_0_.own_ref.own_parts, bf16[256,1024]{1,0:T(8,128)(2,1)S(1)} %get-tuple-element.42.refs_1_.pair_ref.pair_parts, bf16[256,1024]{1,0:T(8,128)(2,1)S(1)} %get-tuple-element.60.third_parts, ...), custom_call_target="tpu_custom_call" | custom-call | flops 1 | bytes 1 | tf_op jit(solution)/shard_map/pallas_call | solution.py:613
  43.7 0.0 collective-permute-done.11.sent3_ref
  43.7 1.0 %collective-permute-done.12.given_ref = f32[24,256]{1,0:T(8,128)S(1)} collective-permute-done((f32[24,256]{1,0:T(8,128)S(1)}, f32[24,256]{1,0:T(8,128)S(1)}, u32[]{:S(2)}, u32[]{:S(2)}) %collective-permute-start.12) | collective-permute-done | bytes 24608 | tf_op jit(solution)/shard_map/ppermute | solution.py:607
  44.7 0.0 collective-permute-done.10.sent2_ref
  44.7 0.6 %shard_map.95 = f32[16,256]{1,0:T(8,128)} custom-call(f32[32,256]{1,0:T(8,128)S(1)} %collective-permute-done.10.sent2_ref, f32[16,256]{1,0:T(8,128)S(1)} %collective-permute-done.11.sent3_ref, f32[24,256]{1,0:T(8,128)S(1)} %collective-permute-done.12.given_ref, f32[16,256]{1,0:T(8,128)S(1)} %get-tuple-element.67.kept_ref), custom_call_target="tpu_custom_call" | custom-call | flops 1 | bytes 1 | tf_op jit(solution)/shard_map/pallas_call | solution.py:624
  (4 shorter events, 0.0 us)
Async XLA Ops:
  0.6 6.0 %copy-start.4 = (bf16[16,96]{1,0:T(8,128)(2,1)S(1)}, bf16[16,96]{1,0:T(8,128)(2,1)}, u32[]{:S(2)}) copy-start(bf16[16,96]{1,0:T(8,128)(2,1)} %constant.7.clone.own_band_ref) | copy-start | bytes 9220
  0.6 6.0 %copy-start = (bf16[256,384]{1,0:T(8,128)(2,1)S(1)}, bf16[256,384]{1,0:T(8,128)(2,1)}, u32[]{:S(2)}) copy-start(bf16[256,384]{1,0:T(8,128)(2,1)} %constant.6.clone.band_ref) | copy-start | bytes 589828
  0.7 15.2 %collective-permute-start = (f32[8,16,1024]{2,1,0:T(8,128)}, f32[8,16,1024]{2,1,0:T(8,128)S(1)}, u32[]{:S(2)}, u32[]{:S(2)}) collective-permute-start(f32[8,16,1024]{2,1,0:T(8,128)} %psi_ref.1), channel_id=1, source_target_pairs={{0,4},{4,0},{8,12},{12,8},{1,5},{5,1},{9,13},{13,9},{2,6},{6,2},{1... | collective-permute-start | bytes 1572872 | tf_op jit(solution)/shard_map/ppermute | solution.py:529
  3.7 12.1 %collective-permute-start.1 = (f32[8,16,1024]{2,1,0:T(8,128)}, f32[8,16,1024]{2,1,0:T(8,128)S(1)}, u32[]{:S(2)}, u32[]{:S(2)}) collective-permute-start(f32[8,16,1024]{2,1,0:T(8,128)} %psi_ref.1), channel_id=1, source_target_pairs={{4,8},{5,9},{6,10},{7,11},{8,4},{9,5},{10,6},{11,7},{0,1},{1,0},{2... | collective-permute-start | bytes 1572872 | tf_op jit(solution)/shard_map/ppermute | solution.py:530
  3.8 15.5 %collective-permute-start.4 = (f32[8,16,1024]{2,1,0:T(8,128)}, f32[8,16,1024]{2,1,0:T(8,128)S(1)}, u32[]{:S(2)}, u32[]{:S(2)}) collective-permute-start(f32[8,16,1024]{2,1,0:T(8,128)} %psi_ref.1), channel_id=1, source_target_pairs={{0,1},{1,0},{2,3},{3,2},{4,5},{5,4},{6,7},{7,6},{8,9},{9,8},{10,11... | collective-permute-start | bytes 1572872 | tf_op jit(solution)/shard_map/ppermute | solution.py:533
  4.3 16.8 %collective-permute-start.3 = (f32[8,16,1024]{2,1,0:T(8,128)}, f32[8,16,1024]{2,1,0:T(8,128)S(1)}, u32[]{:S(2)}, u32[]{:S(2)}) collective-permute-start(f32[8,16,1024]{2,1,0:T(8,128)} %psi_ref.1), channel_id=1, source_target_pairs={{0,3},{1,2},{2,1},{3,0},{4,7},{5,6},{6,5},{7,4},{8,11},{9,10},{10,... | collective-permute-start | bytes 1572872 | tf_op jit(solution)/shard_map/ppermute | solution.py:534
  5.4 0.7 %copy-start.5 = (s32[32]{0:T(128)S(1)}, s32[32]{0:T(128)}, u32[]{:S(2)}) copy-start(s32[32]{0:T(128)} %extent_ref.1) | copy-start | bytes 388
  6.7 1.0 %copy-start.1 = (f32[8,16,1024]{2,1,0:T(8,128)S(1)}, f32[8,16,1024]{2,1,0:T(8,128)}, u32[]{:S(2)}) copy-start(f32[8,16,1024]{2,1,0:T(8,128)} %psi_ref.1) | copy-start | bytes 1572868
  7.7 0.8 %copy-start.2 = (f32[16,1024]{1,0:T(8,128)S(1)}, f32[16,1024]{1,0:T(8,128)}, u32[]{:S(2)}) copy-start(f32[16,1024]{1,0:T(8,128)} %potential_ref.3) | copy-start | bytes 196612
  15.9 6.9 %collective-permute-start.2 = (f32[8,16,1024]{2,1,0:T(8,128)S(1)}, f32[8,16,1024]{2,1,0:T(8,128)S(1)}, u32[]{:S(2)}, u32[]{:S(2)}) collective-permute-start(f32[8,16,1024]{2,1,0:T(8,128)S(1)} %collective-permute-done.psi_ref), channel_id=1, source_target_pairs={{4,8},{5,9},{6,10},{7,11},{8,4},{9,5},{10,6},{11,7},{0,1},{1,0},{2... | collective-permute-start | bytes 1572872 | tf_op jit(solution)/shard_map/ppermute | solution.py:543
  15.9 15.1 %collective-permute-start.6 = (f32[8,16,1024]{2,1,0:T(8,128)S(1)}, f32[8,16,1024]{2,1,0:T(8,128)S(1)}, u32[]{:S(2)}, u32[]{:S(2)}) collective-permute-start(f32[8,16,1024]{2,1,0:T(8,128)S(1)} %collective-permute-done.1.field_ref), channel_id=1, source_target_pairs={{0,4},{4,0},{8,12},{12,8},{1,5},{5,1},{9,13},{13,9},{2,6},{6,2},{1... | collective-permute-start | bytes 1572872 | tf_op jit(solution)/shard_map/ppermute | solution.py:544
  19.2 11.8 %collective-permute-start.7 = (f32[8,16,1024]{2,1,0:T(8,128)S(1)}, f32[8,16,1024]{2,1,0:T(8,128)S(1)}, u32[]{:S(2)}, u32[]{:S(2)}) collective-permute-start(f32[8,16,1024]{2,1,0:T(8,128)S(1)} %collective-permute-done.psi_ref), channel_id=1, source_target_pairs={{0,1},{1,0},{2,3},{3,2},{4,5},{5,4},{6,7},{7,6},{8,9},{9,8},{10,11... | collective-permute-start | bytes 1572872 | tf_op jit(solution)/shard_map/ppermute | solution.py:548
  19.3 11.7 %collective-permute-start.5 = (f32[8,16,896]{2,1,0:T(8,128)S(1)}, f32[8,16,896]{2,1,0:T(8,128)S(1)}, u32[]{:S(2)}, u32[]{:S(2)}) collective-permute-start(f32[8,16,896]{2,1,0:T(8,128)S(1)} %shard_map.85), channel_id=1, source_target_pairs={{4,7},{5,6},{6,5},{7,4},{8,11},{9,10},{10,9},{11,8},{0,1},{1,0},{2... | collective-permute-start | bytes 1376264 | tf_op jit(solution)/shard_map/ppermute | solution.py:547
  20.9 0.7 %copy-start.3 = (bf16[2,16,192]{2,1,0:T(8,128)(2,1)S(1)}, bf16[2,16,192]{2,1,0:T(8,128)(2,1)}, u32[]{:S(2)}) copy-start(bf16[2,16,192]{2,1,0:T(8,128)(2,1)} %constant.8.clone.band_ref) | copy-start | bytes 36868
  22.8 18.8 %collective-permute-start.13 = (f32[7,16,1024]{2,1,0:T(8,128)S(1)}, f32[7,16,1024]{2,1,0:T(8,128)S(1)}, u32[]{:S(2)}, u32[]{:S(2)}) collective-permute-start(f32[7,16,1024]{2,1,0:T(8,128)S(1)} %shard_map.92), channel_id=1, source_target_pairs={{0,4},{4,0},{8,12},{12,8},{1,5},{5,1},{9,13},{13,9},{2,6},{6,2},{1... | collective-permute-start | bytes 1376264 | tf_op jit(solution)/shard_map/ppermute | solution.py:564
  32.5 1.2 %collective-permute-start.8 = (f32[32,16]{1,0:T(8,128)S(1)}, f32[32,16]{1,0:T(8,128)S(1)}, u32[]{:S(2)}, u32[]{:S(2)}) collective-permute-start(f32[32,16]{1,0:T(8,128)S(1)} %shard_map.88.refs_0_), channel_id=1, source_target_pairs={{0,1},{1,0},{2,3},{3,2},{4,5},{5,4},{6,7},{7,6},{8,9},{9,8},{10,11... | collective-permute-start | bytes 6152 | tf_op jit(solution)/shard_map/ppermute | solution.py:586
  33.8 1.2 %collective-permute-start.9 = (f32[32,16]{1,0:T(8,128)S(1)}, f32[32,16]{1,0:T(8,128)S(1)}, u32[]{:S(2)}, u32[]{:S(2)}) collective-permute-start(f32[32,16]{1,0:T(8,128)S(1)} %shard_map.89.part_ref), channel_id=1, source_target_pairs={{4,7},{5,6},{6,5},{7,4},{8,11},{9,10},{10,9},{11,8},{0,1},{1,0},{2... | collective-permute-start | bytes 6152 | tf_op jit(solution)/shard_map/ppermute | solution.py:591
  35.0 6.6 %collective-permute-start.14 = (f32[72,256]{1,0:T(8,128)S(1)}, f32[72,256]{1,0:T(8,128)S(1)}, u32[]{:S(2)}, u32[]{:S(2)}) collective-permute-start(f32[72,256]{1,0:T(8,128)S(1)} %get-tuple-element.59), channel_id=1, source_target_pairs={{0,4},{4,0},{8,12},{12,8},{1,5},{5,1},{9,13},{13,9},{2,6},{6,2},{1... | collective-permute-start | bytes 221192 | tf_op jit(solution)/shard_map/ppermute | solution.py:593
  38.2 6.5 %collective-permute-start.10 = (f32[32,256]{1,0:T(8,128)S(1)}, f32[32,256]{1,0:T(8,128)S(1)}, u32[]{:S(2)}, u32[]{:S(2)}) collective-permute-start(f32[32,256]{1,0:T(8,128)S(1)} %get-tuple-element.55), channel_id=1, source_target_pairs={{0,8},{4,12},{8,0},{12,4},{1,9},{5,13},{9,1},{13,5},{2,10},{6,14},... | collective-permute-start | bytes 98312 | tf_op jit(solution)/shard_map/ppermute | solution.py:608
  40.9 3.8 %collective-permute-start.12 = (f32[24,256]{1,0:T(8,128)S(1)}, f32[24,256]{1,0:T(8,128)S(1)}, u32[]{:S(2)}, u32[]{:S(2)}) collective-permute-start(f32[24,256]{1,0:T(8,128)S(1)} %get-tuple-element.57), channel_id=1, source_target_pairs={{0,4},{4,0},{8,12},{12,8},{1,5},{5,1},{9,13},{13,9},{2,6},{6,2},{1... | collective-permute-start | bytes 73736 | tf_op jit(solution)/shard_map/ppermute | solution.py:607
  41.4 2.3 %collective-permute-start.11 = (f32[16,256]{1,0:T(8,128)S(1)}, f32[16,256]{1,0:T(8,128)S(1)}, u32[]{:S(2)}, u32[]{:S(2)}) collective-permute-start(f32[16,256]{1,0:T(8,128)S(1)} %get-tuple-element.56), channel_id=1, source_target_pairs={{4,8},{5,9},{6,10},{7,11},{8,4},{9,5},{10,6},{11,7},{0,1},{1,0},{2... | collective-permute-start | bytes 49160 | tf_op jit(solution)/shard_map/ppermute | solution.py:609
